TPU v7x, 32 devices: a whole 2x2x4 slice. The times are simulated.
32 devices in a mesh: nodes: 8 (over z, y), feat: 4 (over x, core).
Axes of the slice: x: 2, y: 2, z: 4, core: 2. Of those that a mesh axis runs over, the one named last changes fastest.
Arguments:
- features: bfloat16 [8192, 1024], P('nodes', 'feat'), may hold values from -6 to 6
- ghosts: int32 [64, 2], P('nodes'), may hold values from 0 to 7, as said below
- slots: int32 [64, 24], P('nodes'), may hold values from 0 to 15
- tile_ids: int32 [64, 24], P('nodes'), may hold values from 0 to 15
- degrees: int32 [64], P('nodes'), may hold values from 1 to 24, 512 in all
- tile_table: bfloat16 [16, 128, 128], replicated, may hold values from -0.5 to 0.5
- weight_one: bfloat16 [1024, 1024], P(None, 'feat'), may hold values from -0.1875 to 0.1875
- weight_two: bfloat16 [1024, 1024], P(None, 'feat'), may hold values from -0.1875 to 0.1875
- cotangent: bfloat16 [8192, 1024], P('nodes', 'feat'), may hold values from -0.15625 to 0.15625
Outputs:
- output: bfloat16 [8192, 1024], P('nodes', 'feat')
- grad_one: float32 [1024, 1024], P('nodes', 'feat')
- grad_two: float32 [1024, 1024], P('nodes', 'feat')
Inputs may be any that keep to these rules, and one draw needn't show every extreme that they name: `ghosts`: row d * 8 + p holds 2 distinct block indices of device p. The degrees sum to 512; the largest is 24.
All inputs are finite; a program needn't handle non-finite values. No bound on the sum of `degrees` on one device may be relied on, other than what follows from the above.
Results may differ from a plain program's by a relative error of at most 0.0061.
Values may be sent and summed in bfloat16 or wider, within the bound.
No kernel may reach another device: no remote copies, remote signals or barrier semaphores. Data moves between devices by JAX's collectives and lax.ppermute only.
A program may use at most 64 MiB of HBM per device.

v0:
```python
import jax
import jax.numpy as jnp
from jax import lax
from jax.sharding import PartitionSpec as P

entry_step = 8


def entry_weights(degrees, slot_width):
    position = lax.broadcasted_iota(jnp.int32, (degrees.shape[0], slot_width), 1)
    inverse_root = lax.rsqrt(degrees.astype(jnp.float32))[:, None]
    return jnp.where(position < degrees[:, None], inverse_root, 0.0)


def collect(ghost_rows, slots, tile_ids, weights, tile_table, passes):
    block_count = slots.shape[0]
    block_size = ghost_rows.shape[1]
    feat_width = ghost_rows.shape[2]

    def collect_advance(turn_index, running):
        first_entry = turn_index * entry_step
        near_ids = lax.dynamic_slice_in_dim(slots, first_entry, entry_step, 1)
        tile_pick = lax.dynamic_slice_in_dim(tile_ids, first_entry, entry_step, 1)
        entry_share = lax.dynamic_slice_in_dim(weights, first_entry, entry_step, 1)
        near_rows = ghost_rows[near_ids]
        picked = tile_table[tile_pick]
        products = jnp.einsum(
            "bkij,bkjf->bkif", picked, near_rows, preferred_element_type=jnp.float32
        )
        return running + jnp.sum(entry_share[:, :, None, None] * products, axis=1)

    start_value = jnp.zeros((block_count, block_size, feat_width), jnp.float32)
    return lax.fori_loop(0, passes, collect_advance, start_value)


def neighbours(values, requests, slots, tile_ids, weights, tile_table, passes):
    block_count = slots.shape[0]
    block_size = tile_table.shape[1]
    blocks = values.reshape(block_count, block_size, values.shape[1])
    outgoing = blocks[requests]
    arrived = lax.all_to_all(outgoing, "nodes", split_axis=0, concat_axis=0, tiled=True)
    flat_rows = arrived.reshape(-1, block_size, arrived.shape[3])
    running = collect(flat_rows, slots, tile_ids, weights, tile_table, passes)
    return (blocks.astype(jnp.float32) + running).astype(jnp.bfloat16).reshape(values.shape)


def scatter_back(grad_rows, requests, slots, tile_ids, weights, tile_table, passes, peer_count):
    block_count = slots.shape[0]
    block_size = tile_table.shape[1]
    feat_width = grad_rows.shape[1]
    blocks = grad_rows.reshape(block_count, block_size, feat_width)
    slot_total = requests.shape[0] * requests.shape[1]

    def scatter_advance(turn_index, running):
        first_entry = turn_index * entry_step
        near_ids = lax.dynamic_slice_in_dim(slots, first_entry, entry_step, 1)
        tile_pick = lax.dynamic_slice_in_dim(tile_ids, first_entry, entry_step, 1)
        entry_share = lax.dynamic_slice_in_dim(weights, first_entry, entry_step, 1)
        picked = tile_table[tile_pick]
        products = jnp.einsum("bkji,bjf->bkif", picked, blocks, preferred_element_type=jnp.float32)
        scaled = entry_share[:, :, None, None] * products
        return running + jax.ops.segment_sum(
            scaled.reshape(-1, block_size, feat_width),
            near_ids.reshape(-1),
            num_segments=slot_total,
        )

    start_value = jnp.zeros((slot_total, block_size, feat_width), jnp.float32)
    outbound = lax.fori_loop(0, passes, scatter_advance, start_value)
    outgoing = outbound.astype(jnp.bfloat16).reshape(peer_count, -1, block_size, feat_width)
    arrived = lax.all_to_all(outgoing, "nodes", split_axis=0, concat_axis=0, tiled=True)
    flat_rows = arrived.reshape(-1, block_size, arrived.shape[3]).astype(jnp.float32)
    running = jax.ops.segment_sum(flat_rows, requests.reshape(-1), num_segments=block_count)
    return (blocks.astype(jnp.float32) + running).reshape(grad_rows.shape)


def widen(values):
    return lax.all_gather(values, "feat", axis=1, tiled=True)


def weight_grad(wide_rows, local_rows):
    return lax.psum_scatter(
        lax.dot_general(
            wide_rows, local_rows, (((0,), (0,)), ((), ())), preferred_element_type=jnp.float32
        ),
        "nodes",
        scatter_dimension=0,
        tiled=True,
    )


def on_device(
    features, ghosts, slots, tile_ids, degrees, tile_table, weight_one, weight_two, cotangent
):
    peer_count = lax.axis_size("nodes")
    requests = lax.all_to_all(ghosts, "nodes", split_axis=0, concat_axis=0, tiled=True)
    weights = entry_weights(degrees, slots.shape[1])
    passes = (jnp.max(degrees) + entry_step - 1) // entry_step
    agg_one = neighbours(features, requests, slots, tile_ids, weights, tile_table, passes)
    wide_one = widen(agg_one)
    pre_one = jnp.dot(wide_one, weight_one, preferred_element_type=jnp.float32)
    hidden = jax.nn.silu(pre_one).astype(jnp.bfloat16)
    agg_two = neighbours(hidden, requests, slots, tile_ids, weights, tile_table, passes)
    wide_two = widen(agg_two)
    output = jnp.dot(wide_two, weight_two, preferred_element_type=jnp.float32).astype(jnp.bfloat16)
    grad_two = weight_grad(wide_two, cotangent)
    partial_terms = lax.dot_general(
        cotangent, weight_two, (((1,), (1,)), ((), ())), preferred_element_type=jnp.float32
    )
    grad_sum = lax.psum_scatter(partial_terms, "feat", scatter_dimension=1, tiled=True)
    grad_agg = grad_sum.astype(jnp.bfloat16)
    back_hidden = scatter_back(
        grad_agg, requests, slots, tile_ids, weights, tile_table, passes, peer_count
    )
    sigmoid_pre = jax.nn.sigmoid(pre_one)
    back_pre = (back_hidden * sigmoid_pre * (1.0 + pre_one * (1.0 - sigmoid_pre))).astype(
        jnp.bfloat16
    )
    grad_one = weight_grad(wide_one, back_pre)
    return (output, grad_one, grad_two)


def solution(mesh):
    return jax.shard_map(
        on_device,
        mesh=mesh,
        in_specs=(
            P("nodes", "feat"),
            P("nodes", None),
            P("nodes", None),
            P("nodes", None),
            P("nodes"),
            P(),
            P(None, "feat"),
            P(None, "feat"),
            P("nodes", "feat"),
        ),
        out_specs=(P("nodes", "feat"), P("nodes", "feat"), P("nodes", "feat")),
        check_vma=False,
    )
```

profile of v0, /device:TPU:0, one launch (start us, length us, event | category | flops | bytes accessed | tf_op | source)
XLA Modules:
  0.0 416.0 jit_solution(15855676825402421071)
XLA Ops:
  8.2 3.7 fusion.4
  12.7 13.5 %all_to_all.27 = s32[8,1,2]{2,1,0:T(1,128)S(1)} all-to-all(s32[8,1,2]{2,1,0:T(1,128)S(1)} %copy.19), channel_id=1, replica_groups=mesh['nodes'=8,'feat'=4] {'nodes'}, dimensions={0} | all-to-all | bytes 128 | tf_op jit(solution)/shard_map/all_to_all | solution.py:96
  33.3 23.3 %all-to-all-done.1 = bf16[8,2,128,256]{3,2,1,0:T(8,128)(2,1)S(1)} async-done(((bf16[8,2,128,256]{3,2,1,0:T(8,128)(2,1)}), bf16[8,2,128,256]{3,2,1,0:T(8,128)(2,1)S(1)}, u32[]{:S(2)}, u32[]{:S(2)}) %all-to-all-start.1) | async-done | bytes 1048608 | tf_op jit(solution)/shard_map/all_to_all | solution.py:41
  56.7 29.2 %while.30 = (s32[]{:T(128)}, f32[8,128,256]{2,1,0:T(8,128)S(1)}, s32[]{:T(128)}, f32[8,24]{1,0:T(8,128)S(1)}, s32[8,24]{1,0:T(8,128)S(1)}, /*index=5*/bf16[16,12...) while((s32[]{:T(128)}, f32[8,128,256]{2,1,0:T(8,128)S(1)}, ...), condition=%wide.region_3.4_spmd, body=%wide.region_1.3_spmd.sunk | while | flops 541067648 | bytes 23080884 | solution.py:33
  62.0 4.1 multiply_reduce_fusion.4
  71.7 4.1 multiply_reduce_fusion.4
  81.5 4.2 multiply_reduce_fusion.4
  90.2 64.2 %while.32 = (s32[]{:T(128)}, f32[16,128,256]{2,1,0:T(8,128)S(1)}, s32[]{:T(128)}, s32[8,24]{1,0:T(8,128)S(1)}, f32[8,24]{1,0:T(8,128)S(1)}, /*index=5*/s32[8,24]...) while((s32[]{:T(128)}, f32[16,128,256]{2,1,0:T(8,128)S(1)}, ...), condition=%wide.region_10.11_spmd, body=%wide.region_8.10_spmd.sunk | while | flops 541066432 | bytes 40378032 | solution.py:69
  92.7 6.6 %broadcast_multiply_fusion.2 = f32[8,8,128,256]{3,2,1,0:T(8,128)} fusion(f32[8,8]{1,0:T(8,128)S(1)} %constant_dynamic-slice_fusion.9, bf16[8,8,128,128]{3,2,1,0:T(8,128)(2,1)} %bitcast.77, bf16[8,128,256]{2,1,0:T(8,128)(2,1)} %get-tuple-element.384), kind=kOutput, calls=%fused_computation.21.clone.1 | convolution fusion | flops 538968064 | bytes 11010304 | tf_op jit(solution)/shard_map/while/body/bkji,bjf->bkif/dot_general | solution.py:60
  99.3 12.4 %scatter_fusion = f32[16,128,256]{2,1,0:T(8,128)S(1)} fusion(f32[16,128,256]{2,1,0:T(8,128)S(1)} %get-tuple-element.366, s32[64]{0:T(128)S(1)} %reshape.218, f32[64,128,256]{2,1,0:T(8,128)} %bitcast.74), kind=kCustom, calls=%fused_computation.7.clone.1 | custom fusion | flops 2097152 | bytes 25166080 | tf_op jit(solution)/shard_map/while/body/scatter-add | solution.py:62
  114.2 6.4 %broadcast_multiply_fusion.2 = f32[8,8,128,256]{3,2,1,0:T(8,128)} fusion(f32[8,8]{1,0:T(8,128)S(1)} %constant_dynamic-slice_fusion.9, bf16[8,8,128,128]{3,2,1,0:T(8,128)(2,1)} %bitcast.77, bf16[8,128,256]{2,1,0:T(8,128)(2,1)} %get-tuple-element.384), kind=kOutput, calls=%fused_computation.21.clone.1 | convolution fusion | flops 538968064 | bytes 11010304 | tf_op jit(solution)/shard_map/while/body/bkji,bjf->bkif/dot_general | solution.py:60
  120.6 12.4 %scatter_fusion = f32[16,128,256]{2,1,0:T(8,128)S(1)} fusion(f32[16,128,256]{2,1,0:T(8,128)S(1)} %get-tuple-element.366, s32[64]{0:T(128)S(1)} %reshape.218, f32[64,128,256]{2,1,0:T(8,128)} %bitcast.74), kind=kCustom, calls=%fused_computation.7.clone.1 | custom fusion | flops 2097152 | bytes 25166080 | tf_op jit(solution)/shard_map/while/body/scatter-add | solution.py:62
  135.5 6.4 %broadcast_multiply_fusion.2 = f32[8,8,128,256]{3,2,1,0:T(8,128)} fusion(f32[8,8]{1,0:T(8,128)S(1)} %constant_dynamic-slice_fusion.9, bf16[8,8,128,128]{3,2,1,0:T(8,128)(2,1)} %bitcast.77, bf16[8,128,256]{2,1,0:T(8,128)(2,1)} %get-tuple-element.384), kind=kOutput, calls=%fused_computation.21.clone.1 | convolution fusion | flops 538968064 | bytes 11010304 | tf_op jit(solution)/shard_map/while/body/bkji,bjf->bkif/dot_general | solution.py:60
  141.9 12.4 %scatter_fusion = f32[16,128,256]{2,1,0:T(8,128)S(1)} fusion(f32[16,128,256]{2,1,0:T(8,128)S(1)} %get-tuple-element.366, s32[64]{0:T(128)S(1)} %reshape.218, f32[64,128,256]{2,1,0:T(8,128)} %bitcast.74), kind=kCustom, calls=%fused_computation.7.clone.1 | custom fusion | flops 2097152 | bytes 25166080 | tf_op jit(solution)/shard_map/while/body/scatter-add | solution.py:62
  155.5 4.4 %all-to-all-start.3 = ((bf16[8,2,128,256]{3,2,1,0:T(8,128)(2,1)}), bf16[8,2,128,256]{3,2,1,0:T(8,128)(2,1)}, u32[]{:S(2)}, u32[]{:S(2)}) async-start(bf16[8,2,128,256]{3,2,1,0:T(8,128)(2,1)} %bitcast.87), calls=%async_computation.4 | async-start | bytes 2097152 | tf_op jit(solution)/shard_map/all_to_all | solution.py:71
  161.2 22.2 %all-to-all-done.3 = bf16[8,2,128,256]{3,2,1,0:T(8,128)(2,1)} async-done(((bf16[8,2,128,256]{3,2,1,0:T(8,128)(2,1)}), bf16[8,2,128,256]{3,2,1,0:T(8,128)(2,1)}, u32[]{:S(2)}, u32[]{:S(2)}) %all-to-all-start.3) | async-done | bytes 1048608 | tf_op jit(solution)/shard_map/all_to_all | solution.py:71
  198.3 24.7 %all-to-all-done.2 = bf16[8,2,128,256]{3,2,1,0:T(8,128)(2,1)S(1)} async-done(((bf16[8,2,128,256]{3,2,1,0:T(8,128)(2,1)}), bf16[8,2,128,256]{3,2,1,0:T(8,128)(2,1)S(1)}, u32[]{:S(2)}, u32[]{:S(2)}) %all-to-all-start.2) | async-done | bytes 1048608 | tf_op jit(solution)/shard_map/all_to_all | solution.py:41
  223.1 29.2 %while.31 = (s32[]{:T(128)}, f32[8,128,256]{2,1,0:T(8,128)S(1)}, s32[]{:T(128)}, f32[8,24]{1,0:T(8,128)S(1)}, s32[8,24]{1,0:T(8,128)S(1)}, /*index=5*/bf16[16,12...) while((s32[]{:T(128)}, f32[8,128,256]{2,1,0:T(8,128)S(1)}, ...), condition=%wide.region_6.7_spmd, body=%wide.region_4.6_spmd.sunk | while | flops 541067648 | bytes 23080884 | solution.py:33
  228.6 4.1 multiply_reduce_fusion.5
  238.2 4.1 multiply_reduce_fusion.5
  247.9 4.1 multiply_reduce_fusion.5
  257.8 17.8 %all-gather.5.cloned.1.call-done = bf16[1024,1024]{1,0:T(8,128)(2,1)} async-done(((bf16[1024,256]{1,0:T(8,128)(2,1)}), bf16[1024,1024]{1,0:T(8,128)(2,1)}) %all-gather.5.cloned.1.call-update) | async-done | bytes 2097168 | tf_op jit(solution)/shard_map/all_gather | solution.py:78
  280.6 62.6 %reduce-scatter.6.cloned.1.call-done = f32[128,256]{1,0:T(8,128)} async-done(((f32[1024,256]{1,0:T(8,128)}), f32[128,256]{1,0:T(8,128)}) %reduce-scatter.6.cloned.1.call-update) | async-done | bytes 131088 | tf_op jit(solution)/shard_map/reduce_scatter | solution.py:82
  343.2 66.2 %reduce-scatter.8.cloned.1.call-done = f32[128,256]{1,0:T(8,128)} async-done(((f32[1024,256]{1,0:T(8,128)}), f32[128,256]{1,0:T(8,128)}) %reduce-scatter.8.cloned.1.call-update) | async-done | bytes 131088 | tf_op jit(solution)/shard_map/reduce_scatter | solution.py:82
  (140 shorter events, 80.8 us)
Async XLA Ops:
  7.2 1.0 copy-start
  7.2 80.7 %reduce-scatter.4.cloned.1.call-start = ((), (), s32[]{:S(2)}) async-start(), calls=%async_computation.9 | async-start | bytes 5242880 | tf_op jit(solution)/shard_map/reduce_scatter | solution.py:110
  11.9 0.7 copy-start.8
  11.9 14.6 %copy-start.3 = (bf16[1024,256]{1,0:T(8,128)(2,1)S(1)}, bf16[1024,256]{1,0:T(8,128)(2,1)}, u32[]{:S(2)}) copy-start(bf16[1024,256]{1,0:T(8,128)(2,1)} %param.15) | copy-start | bytes 1572868
  26.5 5.4 %copy-start.9 = (s32[8]{0:T(128)S(1)}, s32[8]{0:T(128)}, u32[]{:S(2)}) copy-start(s32[8]{0:T(128)} %param.19) | copy-start | bytes 100
  28.1 28.5 %copy-start.1 = (bf16[16,128,128]{2,1,0:T(8,128)(2,1)S(1)}, bf16[16,128,128]{2,1,0:T(8,128)(2,1)}, u32[]{:S(2)}) copy-start(bf16[16,128,128]{2,1,0:T(8,128)(2,1)} %param.20) | copy-start | bytes 1572868
  28.1 28.5 %copy-start.5 = (s32[8,24]{1,0:T(8,128)S(1)}, s32[8,24]{1,0:T(8,128)}, u32[]{:S(2)}) copy-start(s32[8,24]{1,0:T(8,128)} %param.18) | copy-start | bytes 2308
  28.1 28.5 %copy-start.6 = (s32[8,24]{1,0:T(8,128)S(1)}, s32[8,24]{1,0:T(8,128)}, u32[]{:S(2)}) copy-start(s32[8,24]{1,0:T(8,128)} %param.17) | copy-start | bytes 2308
  28.1 28.4 %all-to-all-start.1 = ((bf16[8,2,128,256]{3,2,1,0:T(8,128)(2,1)}), bf16[8,2,128,256]{3,2,1,0:T(8,128)(2,1)S(1)}, u32[]{:S(2)}, u32[]{:S(2)}) async-start(bf16[8,2,128,256]{3,2,1,0:T(8,128)(2,1)} %bitcast.11), calls=%async_computation.1 | async-start | bytes 2097152 | tf_op jit(solution)/shard_map/all_to_all | solution.py:41
  31.8 157.9 %all-gather.3.cloned.1.call-start = ((), (), s32[]{:S(2)}) async-start(), calls=%async_computation.7 | async-start | bytes 2621440 | tf_op jit(solution)/shard_map/all_gather | solution.py:78
  155.5 5.6 %copy-start.2 = (bf16[8,128,256]{2,1,0:T(8,128)(2,1)S(1)}, bf16[8,128,256]{2,1,0:T(8,128)(2,1)}, u32[]{:S(2)}) copy-start(bf16[8,128,256]{2,1,0:T(8,128)(2,1)} %get-tuple-element.470) | copy-start | bytes 1572868
  155.5 28.0 %all-to-all-start.3 = ((bf16[8,2,128,256]{3,2,1,0:T(8,128)(2,1)}), bf16[8,2,128,256]{3,2,1,0:T(8,128)(2,1)}, u32[]{:S(2)}, u32[]{:S(2)}) async-start(bf16[8,2,128,256]{3,2,1,0:T(8,128)(2,1)} %bitcast.87), calls=%async_computation.4 | async-start | bytes 2097152 | tf_op jit(solution)/shard_map/all_to_all | solution.py:71
  186.2 3.5 copy-start.11
  193.1 1.6 copy-start.4
  194.7 28.3 %all-to-all-start.2 = ((bf16[8,2,128,256]{3,2,1,0:T(8,128)(2,1)}), bf16[8,2,128,256]{3,2,1,0:T(8,128)(2,1)S(1)}, u32[]{:S(2)}, u32[]{:S(2)}) async-start(bf16[8,2,128,256]{3,2,1,0:T(8,128)(2,1)} %bitcast.15), calls=%async_computation.2 | async-start | bytes 2097152 | tf_op jit(solution)/shard_map/all_to_all | solution.py:41
  198.2 77.4 %all-gather.5.cloned.1.call-start = ((), (), s32[]{:S(2)}) async-start(), calls=%async_computation.8 | async-start | bytes 2621440 | tf_op jit(solution)/shard_map/all_gather | solution.py:78
  252.3 2.1 copy-start.12
  254.4 88.9 %reduce-scatter.6.cloned.1.call-start = ((), (), s32[]{:S(2)}) async-start(), calls=%async_computation.10 | async-start | bytes 1179648 | tf_op jit(solution)/shard_map/reduce_scatter | solution.py:82
  257.8 21.4 %copy-start.7 = (bf16[1024,256]{1,0:T(8,128)(2,1)S(1)}, bf16[1024,256]{1,0:T(8,128)(2,1)}, u32[]{:S(2)}) copy-start(bf16[1024,256]{1,0:T(8,128)(2,1)} %param.22) | copy-start | bytes 1572868
  257.8 151.7 %reduce-scatter.8.cloned.1.call-start = ((), (), s32[]{:S(2)}) async-start(), calls=%async_computation.11 | async-start | bytes 1179648 | tf_op jit(solution)/shard_map/reduce_scatter | solution.py:82
  275.6 3.5 copy-start.10
Sparse Core Ops, SparseCore 0:
  12.1 47.2 reduce-scatter.3
  88.0 20.7 all-gather.2
  254.5 21.0 all-gather.4
  279.8 63.3 reduce-scatter.5
  347.1 62.3 reduce-scatter.7
where the time goes:
time: 419 us; the launch traced here: 416 us
  waiting for transfers between devices  217 us (52%)
  matrix products  59.6 us (14%)
  other arithmetic  54.5 us (13%)
  local copies, waits for them, and re-layouts  44.4 us (11%)
  between operations  14.7 us (4%)
  blocking collectives  13.5 us (3%)
  starting transfers between devices  11.8 us (3%)
    reduce_scatter x2, waiting for transfers between devices, weight_grad(): lax.psum_scatter(lax.dot_general(wide_rows, local_rows, (((0,), (0,)), ((...  129 us
    all_to_all x2, waiting for transfers between devices, neighbours(): lax.all_to_all(outgoing, 'nodes', split_axis=0, concat_axis=0, tiled=True)  48 us
    scatter-add x3, other arithmetic, scatter_advance(): jax.ops.segment_sum(scaled.reshape(-1, block_size, feat_width), near_ids....  37.3 us
    dot_general x6, matrix products, collect_advance(): jnp.einsum('bkij,bkjf->bkif', picked, near_rows, preferred_element_type=j...  24.9 us
    all_to_all x1, waiting for transfers between devices, scatter_back(): lax.all_to_all(outgoing, 'nodes', split_axis=0, concat_axis=0, tiled=True)  22.2 us
    dot_general x3, matrix products, scatter_advance(): jnp.einsum('bkji,bjf->bkif', picked, blocks, preferred_element_type=jnp.f...  19.4 us
    all_gather x2, waiting for transfers between devices, widen(): return lax.all_gather(values, 'feat', axis=1, tiled=True)  17.8 us
    gather x6, local copies, waits for them, and re-layouts, collect_advance(): near_rows = ghost_rows[near_ids]  16.6 us
  transfers between devices with their start and end apart: 8, of which 6 were waited for; matrix products, arithmetic and copies ran while one was open for 28% of the time, Pallas kernels for 0%

commit v1 on v0

v1 whole, which is shorter than its diff:
```python
import functools

import jax
import jax.numpy as jnp
from jax import lax
from jax.experimental import pallas as pl
from jax.experimental.pallas import tpu as pltpu
from jax.sharding import PartitionSpec as P

unroll = 4
bf16, f32 = jnp.bfloat16, jnp.float32


def nt_dot(a, b):
    return lax.dot_general(a, b, (((1,), (1,)), ((), ())), preferred_element_type=f32)


def form_products(x_ref, tiles_ref, p_ref, transposed):
    count, width, size = x_ref.shape
    tile_count = tiles_ref.shape[0]
    group = min(count, max(1, 512 // width))

    def pair(turn, carry):
        two = tiles_ref[pl.ds(2 * turn, 2)]
        if transposed:
            right = jnp.concatenate([two[0], two[1]], axis=1)
        else:
            right = two.reshape(2 * size, size)
        for first in range(0, count, group):
            left = x_ref[first : first + group].reshape(group * width, size)
            if transposed:
                res = jnp.dot(left, right, preferred_element_type=f32)
            else:
                res = nt_dot(left, right)
            for half in range(2):
                part = res[:, half * size : (half + 1) * size].reshape(group, width, size)
                p_ref[pl.ds((2 * turn + half) * count + first, group)] = part
        return carry

    lax.fori_loop(0, tile_count // 2, pair, 0)
    p_ref[tile_count * count] = jnp.zeros((width, size), f32)


def load_blocks(v_ref, x_ref, form, per):
    size = x_ref.shape[2]
    if form == "N":
        for n in range(v_ref.shape[0]):
            for b in range(per):
                x_ref[n * per + b] = v_ref[n, :, b * size : (b + 1) * size]
    else:
        share = v_ref.shape[3] // size
        for f in range(v_ref.shape[0]):
            for n in range(v_ref.shape[1]):
                for j in range(share):
                    x_ref[n * per + f * share + j] = v_ref[f, n, :, j * size : (j + 1) * size]


def put_block(o_ref, form, n, b, value):
    size = value.shape[1]
    if form == "N":
        o_ref[n, :, b * size : (b + 1) * size] = value
    else:
        share = o_ref.shape[3] // size
        j = b % share
        o_ref[b // share, n, :, j * size : (j + 1) * size] = value


def spread_kernel(form_in, form_out, per, width_k, pick, trips, weight, v_ref, tiles_ref, o_ref, x_ref, p_ref):
    load_blocks(v_ref, x_ref, form_in, per)
    form_products(x_ref, tiles_ref, p_ref, False)
    count, width, size = x_ref.shape

    def device_rows(n, carry):
        for b in range(per):
            r = n * per + b

            def chunk(c, acc):
                base = r * width_k + c * unroll
                terms = [p_ref[pick[base + u]] for u in range(unroll)]
                return acc + ((terms[0] + terms[1]) + (terms[2] + terms[3]))

            acc = lax.fori_loop(0, trips[r], chunk, jnp.zeros((width, size), f32))
            put_block(o_ref, form_out, n, b, (x_ref[r].astype(f32) + weight[r] * acc).astype(bf16))
        return carry

    lax.fori_loop(0, count // per, device_rows, 0)


def back_kernel(
    form_in, form_out, per, width_k, pick, near, trips, weight, v_ref, tiles_ref, o_ref, x_ref, p_ref, *sums
):
    load_blocks(v_ref, x_ref, form_in, per)
    form_products(x_ref, tiles_ref, p_ref, True)
    count, width, size = x_ref.shape
    for u, total in enumerate(sums):
        total[...] = x_ref[...].astype(f32) if u == 0 else jnp.zeros(total.shape, f32)

    def row(r, carry):
        share = weight[r]

        def chunk(c, inner):
            base = r * width_k + c * unroll
            for u in range(unroll):
                g = near[base + u]
                sums[u][g] = sums[u][g] + share * p_ref[pick[base + u]]
            return inner

        return lax.fori_loop(0, trips[r], chunk, carry)

    lax.fori_loop(0, count, row, 0)

    def device_rows(n, carry):
        for b in range(per):
            r = n * per + b
            value = (sums[0][r] + sums[1][r]) + (sums[2][r] + sums[3][r])
            put_block(o_ref, form_out, n, b, value.astype(bf16))
        return carry

    lax.fori_loop(0, count // per, device_rows, 0)


def to_blocks(v, form, per, size):
    if form == "N":
        n, width = v.shape[0], v.shape[1]
        return v[:, :, : per * size].reshape(n, width, per, size).transpose(0, 2, 1, 3).reshape(n * per, width, size)
    f, n, width, _ = v.shape
    return v.reshape(f, n, width, per // f, size).transpose(1, 0, 3, 2, 4).reshape(n * per, width, size)


def from_blocks(x, form, per, feat_count):
    count, width, size = x.shape
    n = count // per
    if form == "N":
        return x.reshape(n, per, width, size).transpose(0, 2, 1, 3).reshape(n, width, per * size)
    share = per // feat_count
    return (
        x.reshape(n, feat_count, share, width, size)
        .transpose(1, 0, 3, 2, 4)
        .reshape(feat_count, n, width, share * size)
    )


def plain_spread(v, form_in, form_out, meta, tiles, feat_count, transposed):
    near, tile_ids, live, weight, per = meta["near"], meta["tile"], meta["live"], meta["weight"], meta["per"]
    x = to_blocks(v, form_in, per, tiles.shape[1])
    rows = jnp.arange(x.shape[0])
    kind = "gfi,tij->tgfj" if transposed else "gfj,tij->tgfi"
    products = jnp.einsum(kind, x, tiles, preferred_element_type=f32)

    def step(k, acc):
        g, t = near[:, k], tile_ids[:, k]
        share = jnp.where(live[:, k], weight, 0.0)[:, None, None]
        if transposed:
            return acc.at[g].add(share * products[t, rows])
        return acc + share * products[t, g]

    out = lax.fori_loop(0, near.shape[1], step, x.astype(f32)).astype(bf16)
    return from_blocks(out, form_out, per, feat_count)


def local_spread(v, form_in, form_out, meta, tiles, feat_count, transposed=False):
    width = v.shape[-2]
    if width % 16:
        return plain_spread(v, form_in, form_out, meta, tiles, feat_count, transposed)
    per, size = meta["per"], tiles.shape[1]
    count, width_k = meta["near"].shape
    if form_out == "N":
        shape = (count // per, width, per * size)
    else:
        shape = (feat_count, count // per, width, (per // feat_count) * size)
    smem = pl.BlockSpec(memory_space=pltpu.SMEM)
    vmem = pl.BlockSpec(memory_space=pltpu.VMEM)
    scratch = [
        pltpu.VMEM((count, width, size), bf16),
        pltpu.VMEM((tiles.shape[0] * count + 1, width, size), f32),
    ]
    if transposed:
        body = functools.partial(back_kernel, form_in, form_out, per, width_k)
        scalars = (meta["pick_back"], meta["near_flat"], meta["trips"], meta["weight"])
        scratch += [pltpu.VMEM((count, width, size), f32)] * unroll
    else:
        body = functools.partial(spread_kernel, form_in, form_out, per, width_k)
        scalars = (meta["pick"], meta["trips"], meta["weight"])
    return pl.pallas_call(
        body,
        out_shape=jax.ShapeDtypeStruct(shape, bf16),
        in_specs=[smem] * len(scalars) + [vmem, vmem],
        out_specs=vmem,
        scratch_shapes=scratch,
        compiler_params=pltpu.CompilerParams(vmem_limit_bytes=48 * 1024 * 1024),
        cost_estimate=pl.CostEstimate(
            flops=2 * tiles.shape[0] * count * width * size * size, bytes_accessed=16 << 20, transcendentals=0
        ),
    )(*scalars, v, tiles)


def pack_meta(ghosts, slots, tile_ids, degrees, width, size):
    per = slots.shape[0]
    held = ghosts.shape[1]
    peer = slots // held
    choice = jnp.arange(ghosts.size, dtype=jnp.int32)
    local = jnp.sum(jnp.where(slots[:, :, None] == choice, ghosts.reshape(-1), 0), axis=2)
    near = peer * per + local
    rows = jnp.concatenate([near, tile_ids, degrees[:, None]], axis=1).astype(bf16)
    flat = rows.reshape(-1)
    lanes = -(-flat.size // (width * size)) * size
    return jnp.pad(flat, (0, width * lanes - flat.size)).reshape(width, lanes)


def read_meta(raw, per, width_k, tile_count):
    sources = raw.shape[0]
    span = 2 * width_k + 1
    rows = raw.reshape(sources, -1)[:, : per * span].astype(jnp.int32).reshape(sources * per, span)
    near, tile, degrees = rows[:, :width_k], rows[:, width_k : 2 * width_k], rows[:, 2 * width_k]
    count = sources * per
    live = lax.broadcasted_iota(jnp.int32, near.shape, 1) < degrees[:, None]
    order = lax.broadcasted_iota(jnp.int32, near.shape, 0)
    empty = tile_count * count
    return {
        "near": near,
        "tile": tile,
        "live": live,
        "per": per,
        "weight": lax.rsqrt(degrees.astype(f32)),
        "near_flat": near.reshape(-1),
        "pick": jnp.where(live, tile * count + near, empty).reshape(-1),
        "pick_back": jnp.where(live, tile * count + order, empty).reshape(-1),
        "trips": (degrees + unroll - 1) // unroll,
    }


def swap(values, axis, bit):
    size = lax.axis_size(axis)
    return lax.ppermute(values, axis, [(i, i ^ bit) for i in range(size)])


def gather_rows(values, axis):
    size = lax.axis_size(axis)
    me = lax.axis_index(axis)
    held = values[None]
    bit = size // 2
    while bit:
        other = swap(held, axis, bit)
        upper = (me // bit) % 2 == 1
        held = jnp.concatenate(
            [jnp.where(upper, other, held)[:, None], jnp.where(upper, held, other)[:, None]], 1
        ).reshape((-1,) + values.shape)
        bit //= 2
    return held.reshape((-1,) + values.shape[1:])


def halve(parts, axis, bit, fraction):
    me = lax.axis_index(axis)
    mine = (me // bit) % 2
    lead = parts.shape[0]
    split = parts.reshape((2, lead // 2) + parts.shape[1:])
    keep = lax.dynamic_index_in_dim(split, mine, 0, keepdims=False)
    give = lax.dynamic_index_in_dim(split, 1 - mine, 0, keepdims=False)
    return keep + swap(give.astype(bf16), axis, bit).astype(f32)


def reduce_grad(left, right):
    feat_count, node_count = lax.axis_size("feat"), lax.axis_size("nodes")
    wide = right.shape[0] // feat_count
    me = lax.axis_index("feat")
    tall = right.reshape(feat_count, wide, right.shape[1])
    order, bit = [0], 1
    while bit < feat_count:
        order = [o + bit for o in order] + order
        bit *= 2
    product = lambda ids: nt_dot(left, jnp.concatenate([tall[me ^ i] for i in ids], 0))
    odd, even = [o for o in order if o & 1], [o for o in order if not o & 1]
    given = product(odd).astype(bf16)
    total = product(even) + swap(given, "feat", 1).astype(f32)
    bit = 2
    ids = even
    while bit < feat_count:
        far = [i for i, o in enumerate(ids) if o & bit]
        close = [i for i, o in enumerate(ids) if not o & bit]
        cols = lambda sel: jnp.concatenate([total[:, i * wide : (i + 1) * wide] for i in sel], 1)
        total = cols(close) + swap(cols(far).astype(bf16), "feat", bit).astype(f32)
        ids = [ids[i] for i in close]
        bit *= 2
    parts = total.reshape(node_count, -1, wide)
    parts = parts.reshape(node_count // 2, 2, -1, wide).transpose(1, 0, 2, 3).reshape(node_count, -1, wide)
    parts = halve(parts, "nodes", 1, 2)
    bit = node_count // 2
    while bit > 1:
        parts = halve(parts, "nodes", bit, 2)
        bit //= 2
    return parts.reshape(-1, wide)


def on_device(
    features, ghosts, slots, tile_ids, degrees, tile_table, weight_one, weight_two, cotangent
):
    node_count, feat_count = lax.axis_size("nodes"), lax.axis_size("feat")
    every = ("feat", "nodes")
    per, width_k = slots.shape
    size = tile_table.shape[1]
    rows = features.shape[0]
    width = features.shape[1] // node_count
    swap_all = lambda v, axes: lax.all_to_all(v, axes, split_axis=0, concat_axis=0, tiled=True)

    meta_block = pack_meta(ghosts, slots, tile_ids, degrees, width, size)
    sent = features.T.reshape(node_count, width, rows)
    sent = jnp.concatenate([sent, jnp.broadcast_to(meta_block, (node_count,) + meta_block.shape)], axis=2)
    feat_t = swap_all(sent, "nodes")
    cot_t = swap_all(cotangent.T.reshape(node_count, width, rows), "nodes")
    meta = read_meta(feat_t[:, :, rows:], per, width_k, tile_table.shape[0])

    first = gather_rows(weight_one.T, "feat")
    second = gather_rows(weight_two.T, "feat")

    def over_all(v):
        flat = v.reshape((feat_count * node_count,) + v.shape[2:])
        return swap_all(flat, every)

    agg = over_all(local_spread(feat_t, "N", "R", meta, tile_table, feat_count)).reshape(-1, rows // feat_count)
    back = over_all(local_spread(cot_t, "N", "R", meta, tile_table, feat_count, True)).reshape(-1, rows // feat_count)

    pre = jnp.dot(first, agg, preferred_element_type=f32)
    hidden = jax.nn.silu(pre).astype(bf16)
    wide_out = jnp.dot(second, hidden, preferred_element_type=f32).astype(bf16)
    out_t = swap_all(wide_out.reshape(feat_count * node_count, width, rows // feat_count), every)
    out_t = out_t.reshape(feat_count, node_count, width, rows // feat_count)
    out_n = swap_all(local_spread(out_t, "R", "N", meta, tile_table, feat_count), "nodes")
    output = out_n.reshape(-1, rows).T

    back_hidden = lax.dot_general(second, back, (((0,), (0,)), ((), ())), preferred_element_type=f32)
    sigma = jax.nn.sigmoid(pre)
    back_pre = (back_hidden * sigma * (1.0 + pre * (1.0 - sigma))).astype(bf16)
    grad_two = reduce_grad(hidden, back)
    grad_one = reduce_grad(agg, back_pre)
    return (output, grad_one, grad_two)


def solution(mesh):
    return jax.shard_map(
        on_device,
        mesh=mesh,
        in_specs=(
            P("nodes", "feat"),
            P("nodes", None),
            P("nodes", None),
            P("nodes", None),
            P("nodes"),
            P(),
            P(None, "feat"),
            P(None, "feat"),
            P("nodes", "feat"),
        ),
        out_specs=(P("nodes", "feat"), P("nodes", "feat"), P("nodes", "feat")),
        check_vma=False,
    )
```

time: 419 us -> 163 us (0.39)
  waiting for transfers between devices: 217 us -> 57.8 us
  matrix products: 59.6 us -> 10.5 us
  other arithmetic: 54.5 us -> 15.8 us
  local copies, waits for them, and re-layouts: 44.4 us -> 13.2 us
  starting transfers between devices: 11.8 us -> 39.7 us
  Pallas kernels: 0 us -> 23.6 us
  between operations: 14.7 us -> 1.11 us
  blocking collectives: 13.5 us -> 0 us
    reduce_scatter x3 -> x0, waiting for transfers between devices: 129 us -> none  [the longest x2 129 us: weight_grad(): lax.psum_scatter(lax.dot_general(wide_rows, local_rows, (((0,), (0,)), ((...]
    dot_general x14 -> x7, matrix products: 59.6 us -> 10.5 us  [the longest x4 5.64 us: nt_dot(): lax.dot_general(a, b, (((1,), (1,)), ((), ())), preferred_element_type=f32)]
    all_to_all x3 -> x6, waiting for transfers between devices: 70.2 us -> 28.8 us  [on_device(): lax.all_to_all(v, axes, split_axis=0, concat_axis=0, tiled=True)]
    scatter-add x4 -> x0, other arithmetic: 40.8 us -> none  [the longest x3 37.3 us: scatter_advance(): jax.ops.segment_sum(scaled.reshape(-1, block_size, feat_width), near_ids....]
    gather x17 -> x0, local copies, waits for them, and re-layouts: 39.3 us -> none  [the longest x6 16.6 us: collect_advance(): near_rows = ghost_rows[near_ids]]
    ppermute x0 -> x14, waiting for transfers between devices: none -> 29 us  [swap(): return lax.ppermute(values, axis, [(i, i ^ bit) for i in range(size)])]
    pallas_call x0 -> x3, Pallas kernels: none -> 23.6 us  [local_spread(): pl.pallas_call(body, out_shape=jax.ShapeDtypeStruct(shape, bf16), in_spec...]
    all_gather x2 -> x0, waiting for transfers between devices: 17.8 us -> none  [widen(): return lax.all_gather(values, 'feat', axis=1, tiled=True)]
  transfers between devices with their start and end apart: 8 -> 20, of which waited for: 6 -> 11; matrix products, arithmetic and copies ran while one was open for 28% -> 16% of each run, Pallas kernels for 0% -> 15%
where the time goes in v1:
time: 163 us; the launch traced here: 162 us
  waiting for transfers between devices  57.8 us (35%)
  starting transfers between devices  39.7 us (24%)
  Pallas kernels  23.6 us (14%)
  other arithmetic  15.8 us (10%)
  local copies, waits for them, and re-layouts  13.2 us (8%)
  matrix products  10.5 us (6%)
    ppermute x14, waiting for transfers between devices, swap(): return lax.ppermute(values, axis, [(i, i ^ bit) for i in range(size)])  29 us
    all_to_all x6, waiting for transfers between devices, on_device(): lax.all_to_all(v, axes, split_axis=0, concat_axis=0, tiled=True)  28.8 us
    all_to_all x6, starting transfers between devices, on_device(): lax.all_to_all(v, axes, split_axis=0, concat_axis=0, tiled=True)  25.6 us
    pallas_call x3, Pallas kernels, local_spread(): pl.pallas_call(body, out_shape=jax.ShapeDtypeStruct(shape, bf16), in_spec...  23.6 us
    ppermute x14, starting transfers between devices, swap(): return lax.ppermute(values, axis, [(i, i ^ bit) for i in range(size)])  14.1 us
    dot_general x4, matrix products, nt_dot(): lax.dot_general(a, b, (((1,), (1,)), ((), ())), preferred_element_type=f32)  5.64 us
    unnamed x35, local copies, waits for them, and re-layouts  5.23 us
    broadcast_in_dim x4, other arithmetic, gather_rows(): jnp.where(upper, other, held)[:, None]  3.92 us
  transfers between devices with their start and end apart: 20, of which 11 were waited for; matrix products, arithmetic and copies ran while one was open for 16% of the time, Pallas kernels for 15%

profile of v1, /device:TPU:0, one launch (start us, length us, event | category | flops | bytes accessed | tf_op | source)
XLA Modules:
  0.0 161.7 jit_solution(18418083054653106783)
XLA Ops:
  6.8 7.3 %all-to-all-start = ((bf16[8,32,1152]{2,1,0:T(8,128)(2,1)}), bf16[8,32,1152]{2,1,0:T(8,128)(2,1)S(1)}, u32[]{:S(2)}, u32[]{:S(2)}) async-start(bf16[8,32,1152]{2,1,0:T(8,128)(2,1)} %pad_maximum_fusion.2), calls=%async_computation | async-start | bytes 1179648 | tf_op jit(solution)/shard_map/all_to_all | solution.py:303
  17.4 2.1 %copy.43 = bf16[256,1024]{1,0:T(8,128)(2,1)} copy(bf16[256,1024]{0,1:T(8,128)(2,1)} %bitcast.133) | data formatting | bytes 1048576 | tf_op jit(solution)/shard_map/transpose | solution.py:309
  19.5 9.8 %collective-permute-done.2 = bf16[1,256,1024]{2,1,0:T(8,128)(2,1)S(1)} collective-permute-done((bf16[1,256,1024]{2,1,0:T(8,128)(2,1)S(1)}, bf16[1,256,1024]{2,1,0:T(8,128)(2,1)S(1)}, u32[]{:S(2)}, u32[]{:S(2)}) %collective-permute-start.2) | collective-permute-done | bytes 524320 | tf_op jit(solution)/shard_map/ppermute | solution.py:234
  30.4 6.0 %all-to-all-start.4 = ((bf16[8,32,1024]{2,1,0:T(8,128)(2,1)}), bf16[8,32,1024]{2,1,0:T(8,128)(2,1)S(1)}, u32[]{:S(2)}, u32[]{:S(2)}) async-start(bf16[8,32,1024]{2,1,0:T(8,128)(2,1)} %bitcast.30), calls=%async_computation.4 | async-start | bytes 1048576 | tf_op jit(solution)/shard_map/all_to_all | solution.py:303
  37.0 7.5 %shard_map.112 = bf16[4,8,32,256]{3,2,1,0:T(8,128)(2,1)} custom-call(s32[1536]{0:T(1024)S(1)} %reshape.114.pick, s32[64]{0:T(128)S(1)} %and_select_fusion.trips, f32[64]{0:T(128)S(1)} %convert_rsqrt_fusion.weight, bf16[8,32,1152]{2,1,0:T(8,128)(2,1)S(1)} %all-to-all-done.v_ref, bf16[16,128,128]{2,1,0:T(8,128)(2,1)S(1)} %copy-done), custom_call_target="tpu_custom_call" | custom-call | flops 1073741824 | bytes 16777216 | tf_op jit(solution)/shard_map/pallas_call | solution.py:184
  44.5 7.1 %all-to-all-done.4.v_ref = bf16[8,32,1024]{2,1,0:T(8,128)(2,1)S(1)} async-done(((bf16[8,32,1024]{2,1,0:T(8,128)(2,1)}), bf16[8,32,1024]{2,1,0:T(8,128)(2,1)S(1)}, u32[]{:S(2)}, u32[]{:S(2)}) %all-to-all-start.4) | async-done | bytes 524320 | tf_op jit(solution)/shard_map/all_to_all | solution.py:303
  51.6 3.7 %all-to-all-start.1 = ((bf16[32,32,256]{2,1,0:T(8,128)(2,1)}), bf16[32,32,256]{2,1,0:T(8,128)(2,1)S(1)}, u32[]{:S(2)}, u32[]{:S(2)}) async-start(bf16[32,32,256]{2,1,0:T(8,128)(2,1)} %bitcast.23), calls=%async_computation.1 | async-start | bytes 1048576 | tf_op jit(solution)/shard_map/all_to_all | solution.py:303
  58.8 8.5 %shard_map.114 = bf16[4,8,32,256]{3,2,1,0:T(8,128)(2,1)} custom-call(s32[1536]{0:T(1024)S(1)} %reshape.122.pick, s32[1536]{0:T(1024)S(1)} %reshape.123.near, s32[64]{0:T(128)S(1)} %and_select_fusion.trips, f32[64]{0:T(128)S(1)} %convert_rsqrt_fusion.weight, bf16[8,32,1024]{2,1,0:T(8,128)(2,1)S(1)} %all-to-all-done.4.v_ref, bf16[16,128,128]{2,1,0:T(8,128)(2,1)S(1)} %copy-done), custom_call_target="tpu_custom_call" | custom-call | flops 1073741824 | bytes 16777216 | tf_op jit(solution)/shard_map/pallas_call | solution.py:184
  67.3 4.3 %all-to-all-done.1 = bf16[32,32,256]{2,1,0:T(8,128)(2,1)S(1)} async-done(((bf16[32,32,256]{2,1,0:T(8,128)(2,1)}), bf16[32,32,256]{2,1,0:T(8,128)(2,1)S(1)}, u32[]{:S(2)}, u32[]{:S(2)}) %all-to-all-start.1) | async-done | bytes 524320 | tf_op jit(solution)/shard_map/all_to_all | solution.py:303
  71.6 2.6 %all-to-all-start.5 = ((bf16[32,32,256]{2,1,0:T(8,128)(2,1)}), bf16[32,32,256]{2,1,0:T(8,128)(2,1)S(1)}, u32[]{:S(2)}, u32[]{:S(2)}) async-start(bf16[32,32,256]{2,1,0:T(8,128)(2,1)} %bitcast.31), calls=%async_computation.5 | async-start | bytes 1048576 | tf_op jit(solution)/shard_map/all_to_all | solution.py:303
  80.7 9.9 %all-to-all-done.5 = bf16[32,32,256]{2,1,0:T(8,128)(2,1)S(1)} async-done(((bf16[32,32,256]{2,1,0:T(8,128)(2,1)}), bf16[32,32,256]{2,1,0:T(8,128)(2,1)S(1)}, u32[]{:S(2)}, u32[]{:S(2)}) %all-to-all-start.5) | async-done | bytes 524320 | tf_op jit(solution)/shard_map/all_to_all | solution.py:303
  90.6 2.5 %fusion.1 = bf16[1024,256]{1,0:T(8,128)(2,1)S(1)} fusion(bf16[1024,1024]{1,0:T(8,128)(2,1)} %bitcast.121, bf16[1024,256]{1,0:T(8,128)(2,1)S(1)} %bitcast.124, f32[1024,256]{1,0:T(8,128)S(1)} %fusion.33), kind=kOutput, calls=%fused_computation.8 | convolution fusion | flops 539230208 | bytes 4194304 | tf_op jit(solution)/shard_map/dot_general | solution.py:330
  98.1 2.6 %all-to-all-start.2 = ((bf16[32,32,256]{2,1,0:T(8,128)(2,1)}), bf16[32,32,256]{2,1,0:T(8,128)(2,1)S(1)}, u32[]{:S(2)}, u32[]{:S(2)}) async-start(bf16[32,32,256]{2,1,0:T(8,128)(2,1)} %bitcast.25), calls=%async_computation.2 | async-start | bytes 1048576 | tf_op jit(solution)/shard_map/all_to_all | solution.py:303
  100.7 1.9 %convert_add_fusion.1 = f32[1024,512]{1,0:T(8,128)S(1)} fusion(bf16[1024,512]{1,0:T(8,128)(2,1)} %collective-permute-done.4, bf16[1024,256]{1,0:T(8,128)(2,1)} %bitcast.115, bf16[256,256]{1,0:T(8,128)(2,1)S(1)} %get-tuple-element.18, bf16[256,256]{1,0:T(8,128)(2,1)S(1)} %get-tuple-element.15), kind=kOutput, calls=%fused_computation.3 | convolution fusion | flops 270008320 | bytes 3932160 | tf_op jit(solution)/shard_map/dot_general | solution.py:15
  109.5 7.5 %all-to-all-done.2 = bf16[32,32,256]{2,1,0:T(8,128)(2,1)S(1)} async-done(((bf16[32,32,256]{2,1,0:T(8,128)(2,1)}), bf16[32,32,256]{2,1,0:T(8,128)(2,1)S(1)}, u32[]{:S(2)}, u32[]{:S(2)}) %all-to-all-start.2) | async-done | bytes 524320 | tf_op jit(solution)/shard_map/all_to_all | solution.py:303
  117.0 7.5 %shard_map.113 = bf16[8,32,1024]{2,1,0:T(8,128)(2,1)} custom-call(s32[1536]{0:T(1024)S(1)} %reshape.114.pick, s32[64]{0:T(128)S(1)} %and_select_fusion.trips, f32[64]{0:T(128)S(1)} %convert_rsqrt_fusion.weight, bf16[4,8,32,256]{3,2,1,0:T(8,128)(2,1)S(1)} %bitcast.112, bf16[16,128,128]{2,1,0:T(8,128)(2,1)S(1)} %copy-done), custom_call_target="tpu_custom_call" | custom-call | flops 1073741824 | bytes 16777216 | tf_op jit(solution)/shard_map/pallas_call | solution.py:184
  124.6 3.5 %all-to-all-start.3 = ((bf16[8,32,1024]{2,1,0:T(8,128)(2,1)}), bf16[8,32,1024]{2,1,0:T(8,128)(2,1)S(1)}, u32[]{:S(2)}, u32[]{:S(2)}) async-start(bf16[8,32,1024]{2,1,0:T(8,128)(2,1)} %shard_map.113), calls=%async_computation.3 | async-start | bytes 1048576 | tf_op jit(solution)/shard_map/all_to_all | solution.py:303
  129.5 2.0 %collective-permute-start.6 = (bf16[4,128,256]{2,1,0:T(8,128)(2,1)S(1)}, bf16[4,128,256]{2,1,0:T(8,128)(2,1)S(1)}, u32[]{:S(2)}, u32[]{:S(2)}) collective-permute-start(bf16[4,128,256]{2,1,0:T(8,128)(2,1)S(1)} %fusion.2), channel_id=1, source_target_pairs={{0,4},{4,0},{8,12},{12,8},{16,20},{20,16},{24,28},{28,24},{1,5},{5... | collective-permute-start | bytes 786440 | tf_op jit(solution)/shard_map/ppermute | solution.py:234
  135.0 7.8 %collective-permute-done.6 = bf16[4,128,256]{2,1,0:T(8,128)(2,1)S(1)} collective-permute-done((bf16[4,128,256]{2,1,0:T(8,128)(2,1)S(1)}, bf16[4,128,256]{2,1,0:T(8,128)(2,1)S(1)}, u32[]{:S(2)}, u32[]{:S(2)}) %collective-permute-start.6) | collective-permute-done | bytes 262176 | tf_op jit(solution)/shard_map/ppermute | solution.py:234
  143.0 1.8 %collective-permute-start.7 = (bf16[2,128,256]{2,1,0:T(8,128)(2,1)S(1)}, bf16[2,128,256]{2,1,0:T(8,128)(2,1)S(1)}, u32[]{:S(2)}, u32[]{:S(2)}) collective-permute-start(bf16[2,128,256]{2,1,0:T(8,128)(2,1)S(1)} %fusion.22), channel_id=1, source_target_pairs={{0,16},{4,20},{8,24},{12,28},{16,0},{20,4},{24,8},{28,12},{1,17},{... | collective-permute-start | bytes 393224 | tf_op jit(solution)/shard_map/ppermute | solution.py:234
  144.8 3.1 %collective-permute-done.11 = bf16[4,128,256]{2,1,0:T(8,128)(2,1)S(1)} collective-permute-done((bf16[4,128,256]{2,1,0:T(8,128)(2,1)S(1)}, bf16[4,128,256]{2,1,0:T(8,128)(2,1)S(1)}, u32[]{:S(2)}, u32[]{:S(2)}) %collective-permute-start.11) | collective-permute-done | bytes 262176 | tf_op jit(solution)/shard_map/ppermute | solution.py:234
  148.0 1.8 %collective-permute-start.12 = (bf16[2,128,256]{2,1,0:T(8,128)(2,1)S(1)}, bf16[2,128,256]{2,1,0:T(8,128)(2,1)S(1)}, u32[]{:S(2)}, u32[]{:S(2)}) collective-permute-start(bf16[2,128,256]{2,1,0:T(8,128)(2,1)S(1)} %fusion.23), channel_id=1, source_target_pairs={{0,16},{4,20},{8,24},{12,28},{16,0},{20,4},{24,8},{28,12},{1,17},{... | collective-permute-start | bytes 393224 | tf_op jit(solution)/shard_map/ppermute | solution.py:234
  152.9 3.8 %collective-permute-done.12 = bf16[2,128,256]{2,1,0:T(8,128)(2,1)S(1)} collective-permute-done((bf16[2,128,256]{2,1,0:T(8,128)(2,1)S(1)}, bf16[2,128,256]{2,1,0:T(8,128)(2,1)S(1)}, u32[]{:S(2)}, u32[]{:S(2)}) %collective-permute-start.12) | collective-permute-done | bytes 131104 | tf_op jit(solution)/shard_map/ppermute | solution.py:234
  157.5 3.6 %collective-permute-done.13 = bf16[1,128,256]{2,1,0:T(8,128)(2,1)S(1)} collective-permute-done((bf16[1,128,256]{2,1,0:T(8,128)(2,1)S(1)}, bf16[1,128,256]{2,1,0:T(8,128)(2,1)S(1)}, u32[]{:S(2)}, u32[]{:S(2)}) %collective-permute-start.13) | collective-permute-done | bytes 65568 | tf_op jit(solution)/shard_map/ppermute | solution.py:234
  (111 shorter events, 42.3 us)
Async XLA Ops:
  0.6 13.5 %copy-start.9 = (bf16[1024,256]{1,0:T(8,128)(2,1)S(1)}, bf16[1024,256]{1,0:T(8,128)(2,1)}, u32[]{:S(2)}) copy-start(bf16[1024,256]{1,0:T(8,128)(2,1)} %param.15) | copy-start | bytes 1572868
  4.6 11.3 %copy-start.10 = (bf16[1024,256]{1,0:T(8,128)(2,1)S(1)}, bf16[1024,256]{1,0:T(8,128)(2,1)}, u32[]{:S(2)}) copy-start(bf16[1024,256]{1,0:T(8,128)(2,1)} %param.16) | copy-start | bytes 1572868
  6.8 23.6 %all-to-all-start = ((bf16[8,32,1152]{2,1,0:T(8,128)(2,1)}), bf16[8,32,1152]{2,1,0:T(8,128)(2,1)S(1)}, u32[]{:S(2)}, u32[]{:S(2)}) async-start(bf16[8,32,1152]{2,1,0:T(8,128)(2,1)} %pad_maximum_fusion.2), calls=%async_computation | async-start | bytes 1179648 | tf_op jit(solution)/shard_map/all_to_all | solution.py:303
  14.3 14.9 %collective-permute-start.2 = (bf16[1,256,1024]{2,1,0:T(8,128)(2,1)S(1)}, bf16[1,256,1024]{2,1,0:T(8,128)(2,1)S(1)}, u32[]{:S(2)}, u32[]{:S(2)}) collective-permute-start(bf16[1,256,1024]{2,1,0:T(8,128)(2,1)S(1)} %bitcast.120), channel_id=1, source_target_pairs={{0,2},{1,3},{2,0},{3,1},{4,6},{5,7},{6,4},{7,5},{8,10},{9,11},{10,... | collective-permute-start | bytes 1572872 | tf_op jit(solution)/shard_map/ppermute | solution.py:234
  16.9 38.4 %collective-permute-start = (bf16[1,256,1024]{2,1,0:T(8,128)(2,1)}, bf16[1,256,1024]{2,1,0:T(8,128)(2,1)S(1)}, u32[]{:S(2)}, u32[]{:S(2)}) collective-permute-start(bf16[1,256,1024]{2,1,0:T(8,128)(2,1)} %bitcast.5), channel_id=1, source_target_pairs={{0,2},{1,3},{2,0},{3,1},{4,6},{5,7},{6,4},{7,5},{8,10},{9,11},{10,... | collective-permute-start | bytes 1572872 | tf_op jit(solution)/shard_map/ppermute | solution.py:234
  30.4 43.8 %collective-permute-start.3 = (bf16[2,256,1024]{2,1,0:T(8,128)(2,1)}, bf16[2,256,1024]{2,1,0:T(8,128)(2,1)}, u32[]{:S(2)}, u32[]{:S(2)}) collective-permute-start(bf16[2,256,1024]{2,1,0:T(8,128)(2,1)} %maximum_bitcast_fusion.1), channel_id=1, source_target_pairs={{0,1},{1,0},{2,3},{3,2},{4,5},{5,4},{6,7},{7,6},{8,9},{9,8},{10,11... | collective-permute-start | bytes 3145736 | tf_op jit(solution)/shard_map/ppermute | solution.py:234
  30.4 21.2 %all-to-all-start.4 = ((bf16[8,32,1024]{2,1,0:T(8,128)(2,1)}), bf16[8,32,1024]{2,1,0:T(8,128)(2,1)S(1)}, u32[]{:S(2)}, u32[]{:S(2)}) async-start(bf16[8,32,1024]{2,1,0:T(8,128)(2,1)} %bitcast.30), calls=%async_computation.4 | async-start | bytes 1048576 | tf_op jit(solution)/shard_map/all_to_all | solution.py:303
  51.6 20.0 %all-to-all-start.1 = ((bf16[32,32,256]{2,1,0:T(8,128)(2,1)}), bf16[32,32,256]{2,1,0:T(8,128)(2,1)S(1)}, u32[]{:S(2)}, u32[]{:S(2)}) async-start(bf16[32,32,256]{2,1,0:T(8,128)(2,1)} %bitcast.23), calls=%async_computation.1 | async-start | bytes 1048576 | tf_op jit(solution)/shard_map/all_to_all | solution.py:303
  58.3 17.7 %collective-permute-start.1 = (bf16[2,256,1024]{2,1,0:T(8,128)(2,1)}, bf16[2,256,1024]{2,1,0:T(8,128)(2,1)}, u32[]{:S(2)}, u32[]{:S(2)}) collective-permute-start(bf16[2,256,1024]{2,1,0:T(8,128)(2,1)} %maximum_bitcast_fusion), channel_id=1, source_target_pairs={{0,1},{1,0},{2,3},{3,2},{4,5},{5,4},{6,7},{7,6},{8,9},{9,8},{10,11... | collective-permute-start | bytes 3145736 | tf_op jit(solution)/shard_map/ppermute | solution.py:234
  71.6 21.6 %copy-start.1 = (bf16[32,32,256]{2,1,0:T(8,128)(2,1)}, bf16[32,32,256]{2,1,0:T(8,128)(2,1)S(1)}, u32[]{:S(2)}) copy-start(bf16[32,32,256]{2,1,0:T(8,128)(2,1)S(1)} %all-to-all-done.1) | copy-start | bytes 1572868
  71.6 19.0 %all-to-all-start.5 = ((bf16[32,32,256]{2,1,0:T(8,128)(2,1)}), bf16[32,32,256]{2,1,0:T(8,128)(2,1)S(1)}, u32[]{:S(2)}, u32[]{:S(2)}) async-start(bf16[32,32,256]{2,1,0:T(8,128)(2,1)} %bitcast.31), calls=%async_computation.5 | async-start | bytes 1048576 | tf_op jit(solution)/shard_map/all_to_all | solution.py:303
  80.7 12.4 %copy-start.12 = (f32[1024,256]{1,0:T(8,128)}, f32[1024,256]{1,0:T(8,128)S(1)}, u32[]{:S(2)}) copy-start(f32[1024,256]{1,0:T(8,128)S(1)} %fusion.33) | copy-start | bytes 3145732
  93.7 7.0 %collective-permute-start.4 = (bf16[1024,512]{1,0:T(8,128)(2,1)S(1)}, bf16[1024,512]{1,0:T(8,128)(2,1)}, u32[]{:S(2)}, u32[]{:S(2)}) collective-permute-start(bf16[1024,512]{1,0:T(8,128)(2,1)S(1)} %convolution_convert_fusion.1), channel_id=1, source_target_pairs={{0,1},{1,0},{2,3},{3,2},{4,5},{5,4},{6,7},{7,6},{8,9},{9,8},{10,11... | collective-permute-start | bytes 3145736 | tf_op jit(solution)/shard_map/ppermute | solution.py:234
  95.9 9.2 %collective-permute-start.9 = (bf16[1024,512]{1,0:T(8,128)(2,1)}, bf16[1024,512]{1,0:T(8,128)(2,1)}, u32[]{:S(2)}, u32[]{:S(2)}) collective-permute-start(bf16[1024,512]{1,0:T(8,128)(2,1)} %convolution_convert_fusion), channel_id=1, source_target_pairs={{0,1},{1,0},{2,3},{3,2},{4,5},{5,4},{6,7},{7,6},{8,9},{9,8},{10,11... | collective-permute-start | bytes 3145736 | tf_op jit(solution)/shard_map/ppermute | solution.py:234
  98.1 19.0 %all-to-all-start.2 = ((bf16[32,32,256]{2,1,0:T(8,128)(2,1)}), bf16[32,32,256]{2,1,0:T(8,128)(2,1)S(1)}, u32[]{:S(2)}, u32[]{:S(2)}) async-start(bf16[32,32,256]{2,1,0:T(8,128)(2,1)} %bitcast.25), calls=%async_computation.2 | async-start | bytes 1048576 | tf_op jit(solution)/shard_map/all_to_all | solution.py:303
  103.5 24.5 %collective-permute-start.5 = (bf16[1024,256]{1,0:T(8,128)(2,1)}, bf16[1024,256]{1,0:T(8,128)(2,1)}, u32[]{:S(2)}, u32[]{:S(2)}) collective-permute-start(bf16[1024,256]{1,0:T(8,128)(2,1)} %slice.61), channel_id=1, source_target_pairs={{0,2},{1,3},{2,0},{3,1},{4,6},{5,7},{6,4},{7,5},{8,10},{9,11},{10,... | collective-permute-start | bytes 1572872 | tf_op jit(solution)/shard_map/ppermute | solution.py:234
  109.2 23.0 %collective-permute-start.10 = (bf16[1024,256]{1,0:T(8,128)(2,1)}, bf16[1024,256]{1,0:T(8,128)(2,1)}, u32[]{:S(2)}, u32[]{:S(2)}) collective-permute-start(bf16[1024,256]{1,0:T(8,128)(2,1)} %slice.60), channel_id=1, source_target_pairs={{0,2},{1,3},{2,0},{3,1},{4,6},{5,7},{6,4},{7,5},{8,10},{9,11},{10,... | collective-permute-start | bytes 1572872 | tf_op jit(solution)/shard_map/ppermute | solution.py:234
  124.6 25.2 %all-to-all-start.3 = ((bf16[8,32,1024]{2,1,0:T(8,128)(2,1)}), bf16[8,32,1024]{2,1,0:T(8,128)(2,1)S(1)}, u32[]{:S(2)}, u32[]{:S(2)}) async-start(bf16[8,32,1024]{2,1,0:T(8,128)(2,1)} %shard_map.113), calls=%async_computation.3 | async-start | bytes 1048576 | tf_op jit(solution)/shard_map/all_to_all | solution.py:303
  129.5 13.4 %collective-permute-start.6 = (bf16[4,128,256]{2,1,0:T(8,128)(2,1)S(1)}, bf16[4,128,256]{2,1,0:T(8,128)(2,1)S(1)}, u32[]{:S(2)}, u32[]{:S(2)}) collective-permute-start(bf16[4,128,256]{2,1,0:T(8,128)(2,1)S(1)} %fusion.2), channel_id=1, source_target_pairs={{0,4},{4,0},{8,12},{12,8},{16,20},{20,16},{24,28},{28,24},{1,5},{5... | collective-permute-start | bytes 786440 | tf_op jit(solution)/shard_map/ppermute | solution.py:234
  133.4 14.5 %collective-permute-start.11 = (bf16[4,128,256]{2,1,0:T(8,128)(2,1)S(1)}, bf16[4,128,256]{2,1,0:T(8,128)(2,1)S(1)}, u32[]{:S(2)}, u32[]{:S(2)}) collective-permute-start(bf16[4,128,256]{2,1,0:T(8,128)(2,1)S(1)} %fusion.3), channel_id=1, source_target_pairs={{0,4},{4,0},{8,12},{12,8},{16,20},{20,16},{24,28},{28,24},{1,5},{5... | collective-permute-start | bytes 786440 | tf_op jit(solution)/shard_map/ppermute | solution.py:234
  143.0 8.1 %collective-permute-start.7 = (bf16[2,128,256]{2,1,0:T(8,128)(2,1)S(1)}, bf16[2,128,256]{2,1,0:T(8,128)(2,1)S(1)}, u32[]{:S(2)}, u32[]{:S(2)}) collective-permute-start(bf16[2,128,256]{2,1,0:T(8,128)(2,1)S(1)} %fusion.22), channel_id=1, source_target_pairs={{0,16},{4,20},{8,24},{12,28},{16,0},{20,4},{24,8},{28,12},{1,17},{... | collective-permute-start | bytes 393224 | tf_op jit(solution)/shard_map/ppermute | solution.py:234
  148.0 8.7 %collective-permute-start.12 = (bf16[2,128,256]{2,1,0:T(8,128)(2,1)S(1)}, bf16[2,128,256]{2,1,0:T(8,128)(2,1)S(1)}, u32[]{:S(2)}, u32[]{:S(2)}) collective-permute-start(bf16[2,128,256]{2,1,0:T(8,128)(2,1)S(1)} %fusion.23), channel_id=1, source_target_pairs={{0,16},{4,20},{8,24},{12,28},{16,0},{20,4},{24,8},{28,12},{1,17},{... | collective-permute-start | bytes 393224 | tf_op jit(solution)/shard_map/ppermute | solution.py:234
  151.1 5.7 %collective-permute-start.8 = (bf16[1,128,256]{2,1,0:T(8,128)(2,1)S(1)}, bf16[1,128,256]{2,1,0:T(8,128)(2,1)S(1)}, u32[]{:S(2)}, u32[]{:S(2)}) collective-permute-start(bf16[1,128,256]{2,1,0:T(8,128)(2,1)S(1)} %dynamic-slice_convert_fusion.5), channel_id=1, source_target_pairs={{0,8},{4,12},{8,0},{12,4},{16,24},{20,28},{24,16},{28,20},{1,9},{5... | collective-permute-start | bytes 196616 | tf_op jit(solution)/shard_map/ppermute | solution.py:234
  156.7 4.3 %collective-permute-start.13 = (bf16[1,128,256]{2,1,0:T(8,128)(2,1)S(1)}, bf16[1,128,256]{2,1,0:T(8,128)(2,1)S(1)}, u32[]{:S(2)}, u32[]{:S(2)}) collective-permute-start(bf16[1,128,256]{2,1,0:T(8,128)(2,1)S(1)} %dynamic-slice_convert_fusion.4), channel_id=1, source_target_pairs={{0,8},{4,12},{8,0},{12,4},{16,24},{20,28},{24,16},{28,20},{1,9},{5... | collective-permute-start | bytes 196616 | tf_op jit(solution)/shard_map/ppermute | solution.py:234
  (11 other events, 30.4 us)

commit v2 on v0

v2 whole, which is shorter than its diff:
```python
import functools

import jax
import jax.numpy as jnp
from jax import lax
from jax.experimental import pallas as pl
from jax.experimental.pallas import tpu as pltpu
from jax.sharding import PartitionSpec as P

unroll = 4
meta_rows = 16
bf16, f32 = jnp.bfloat16, jnp.float32
vmem = pl.BlockSpec(memory_space=pltpu.VMEM)
smem = pl.BlockSpec(memory_space=pltpu.SMEM)


def nt_dot(a, b):
    return lax.dot_general(a, b, (((1,), (1,)), ((), ())), preferred_element_type=f32)


def call(body, outs, in_specs, args, scratch=(), flops=0, out_specs=None):
    return pl.pallas_call(
        body,
        out_shape=[jax.ShapeDtypeStruct(s, d) for s, d in outs],
        in_specs=in_specs,
        out_specs=out_specs or [vmem] * len(outs),
        scratch_shapes=list(scratch),
        compiler_params=pltpu.CompilerParams(vmem_limit_bytes=48 * 1024 * 1024),
        cost_estimate=pl.CostEstimate(flops=flops, bytes_accessed=4 << 20, transcendentals=0),
    )(*args)


def meta_tile(ghost_at, degree_at, slots, tile_ids, owners, held, size):
    per, width_k = slots.shape
    near = jnp.zeros((per, width_k), jnp.int32)
    for s in range(owners * held):
        near = jnp.where(slots == s, (s // held) * per + ghost_at(s // held, s % held), near)
    row = lax.broadcasted_iota(jnp.int32, (per, size), 0)
    lane = lax.broadcasted_iota(jnp.int32, (per, size), 1)
    degree = jnp.zeros((per, size), jnp.int32)
    for r in range(per):
        degree = jnp.where(row == r, degree_at(r), degree)
    widen = lambda v: jnp.concatenate([v, jnp.zeros((per, size - width_k), jnp.int32)], axis=1)
    top = jnp.where(lane == width_k, degree, widen(near))
    return jnp.concatenate([top, widen(tile_ids)], axis=0).astype(f32).astype(bf16)


def pack_kernel(owners, held, ghosts, degrees, slots_ref, tiles_ref, feat_ref, cot_ref, o_ref):
    nodes, rows, size = o_ref.shape
    width = feat_ref.shape[1] // nodes
    per = feat_ref.shape[0] // size
    for which, ref in enumerate((feat_ref, cot_ref)):
        for b in range(per):
            turned = ref[b * size : (b + 1) * size, :].T
            first = (which * per + b) * width
            for n in range(nodes):
                o_ref[n, first : first + width, :] = turned[n * width : (n + 1) * width]
    tile = meta_tile(
        lambda p, c: ghosts[p, c], lambda r: degrees[r], slots_ref[...], tiles_ref[...], owners, held, size
    )
    for n in range(nodes):
        o_ref[n, rows - meta_rows :, :] = tile


def pack(features, cotangent, ghosts, slots, tile_ids, degrees, nodes, size):
    owners, held = ghosts.shape
    per = slots.shape[0]
    width = features.shape[1] // nodes
    if width % 16:
        turn = lambda v: v.reshape(per, size, nodes, width).transpose(2, 0, 3, 1).reshape(nodes, per * width, size)
        tile = meta_tile(lambda p, c: ghosts[p, c], lambda r: degrees[r], slots, tile_ids, owners, held, size)
        tile = jnp.broadcast_to(tile, (nodes,) + tile.shape)
        return jnp.concatenate([turn(features), turn(cotangent), tile], axis=1)
    shape = (nodes, 2 * per * width + meta_rows, size)
    return call(
        functools.partial(pack_kernel, owners, held),
        [(shape, bf16)],
        [smem, smem, vmem, vmem, vmem, vmem],
        (ghosts, degrees, slots, tile_ids, features, cotangent),
    )[0]


def form_products(left_at, count, width, tiles_ref, p_ref, transposed):
    tile_count, size = tiles_ref.shape[0], tiles_ref.shape[1]

    def pair(turn, carry):
        two = tiles_ref[pl.ds(2 * turn, 2)]
        if transposed:
            right = jnp.concatenate([two[0], two[1]], axis=1)
        else:
            right = two.reshape(2 * size, size)
        for first, left in left_at():
            res = jnp.dot(left, right, preferred_element_type=f32) if transposed else nt_dot(left, right)
            group = left.shape[0] // width
            for half in range(2):
                part = res[:, half * size : (half + 1) * size].reshape(group, width, size)
                p_ref[pl.ds((2 * turn + half) * count + first, group)] = part
        return carry

    lax.fori_loop(0, tile_count // 2, pair, 0)
    p_ref[tile_count * count] = jnp.zeros((width, size), f32)


def sum_entries(pick, near, r, width_k, p_ref):
    def chunk(c, acc):
        base = c * unroll
        terms = [p_ref[pick[r, base + u]] for u in range(unroll)]
        return acc + ((terms[0] + terms[1]) + (terms[2] + terms[3]))

    trips = (near[r, width_k] + (unroll - 1)) // unroll
    return lax.fori_loop(0, trips, chunk, jnp.zeros(p_ref.shape[1:], f32))


def first_kernel(per, width_k, v_ref, tiles_ref, o_ref, ids_ref, weight_ref, pick, pick_back, near, p_ref, sem, *sums):
    nodes, _, size = v_ref.shape
    width = o_ref.shape[2]
    share = o_ref.shape[3] // size
    count = nodes * per
    span = per * width
    empty = tiles_ref.shape[0] * count
    lane = lax.broadcasted_iota(jnp.int32, (per, size), 1)
    row = lax.broadcasted_iota(jnp.int32, (per, size), 0)
    for n in range(nodes):
        raw = v_ref[n, 2 * span :, :].astype(f32).astype(jnp.int32)
        links, tile = raw[:per], raw[per:]
        degree = jnp.broadcast_to(links[:, width_k : width_k + 1], (per, size))
        live = lane < degree
        block = slice(n * per, (n + 1) * per)
        ids_ref[0, block] = jnp.where(live, tile * count + links, empty)
        ids_ref[1, block] = jnp.where(live, tile * count + (row + n * per), empty)
        ids_ref[2, block] = links
        weight_ref[block] = lax.rsqrt(degree.astype(f32))
    copies = [pltpu.make_async_copy(ids_ref.at[i], ref, sem.at[i]) for i, ref in enumerate((pick, pick_back, near))]
    for copy in copies:
        copy.start()

    def lefts(first_row):
        def at():
            for n in range(0, nodes, 2):
                yield n * per, v_ref[n : n + 2, first_row : first_row + span, :].reshape(2 * span, size)

        return at

    form_products(lefts(0), count, width, tiles_ref, p_ref, False)
    for copy in copies:
        copy.wait()

    def forward_rows(n, carry):
        for b in range(per):
            r = n * per + b
            acc = sum_entries(pick, near, r, width_k, p_ref)
            own = v_ref[n, b * width : (b + 1) * width, :].astype(f32)
            j = b % share
            value = (own + weight_ref[pl.ds(r, 1), :] * acc).astype(bf16)
            o_ref[(b // share) * nodes + n, 0, :, j * size : (j + 1) * size] = value
        return carry

    lax.fori_loop(0, nodes, forward_rows, 0)

    form_products(lefts(span), count, width, tiles_ref, p_ref, True)
    for n in range(nodes):
        sums[0][n * per : (n + 1) * per] = v_ref[n, span : 2 * span, :].astype(f32).reshape(per, width, size)
    for total in sums[1:]:
        total[...] = jnp.zeros(total.shape, f32)

    def entry_row(r, carry):
        scale = weight_ref[pl.ds(r, 1), :]

        def chunk(c, inner):
            base = c * unroll
            for u in range(unroll):
                g = near[r, base + u]
                sums[u][g] = sums[u][g] + scale * p_ref[pick_back[r, base + u]]
            return inner

        return lax.fori_loop(0, (near[r, width_k] + (unroll - 1)) // unroll, chunk, carry)

    lax.fori_loop(0, count, entry_row, 0)

    def back_rows(n, carry):
        for b in range(per):
            r = n * per + b
            j = b % share
            value = ((sums[0][r] + sums[1][r]) + (sums[2][r] + sums[3][r])).astype(bf16)
            o_ref[(b // share) * nodes + n, 1, :, j * size : (j + 1) * size] = value
        return carry

    lax.fori_loop(0, nodes, back_rows, 0)


def last_kernel(per, width_k, pick, near, weight_ref, v_ref, tiles_ref, o_ref, x_ref, p_ref):
    nodes = o_ref.shape[0]
    count, width, size = x_ref.shape
    share = v_ref.shape[2] // size
    for f in range(per // share):
        for n in range(nodes):
            for j in range(share):
                x_ref[n * per + f * share + j] = v_ref[f * nodes + n, :, j * size : (j + 1) * size]

    def lefts():
        group = 512 // width
        for first in range(0, count, group):
            yield first, x_ref[first : first + group].reshape(group * width, size)

    form_products(lefts, count, width, tiles_ref, p_ref, False)

    def rows(n, carry):
        for b in range(per):
            r = n * per + b
            acc = sum_entries(pick, near, r, width_k, p_ref)
            value = x_ref[r].astype(f32) + weight_ref[pl.ds(r, 1), :] * acc
            o_ref[n, :, b * size : (b + 1) * size] = value.astype(bf16)
        return carry

    lax.fori_loop(0, nodes, rows, 0)


def plain_spread(x, ids, tiles, transposed):
    near, tile_ids, degrees = ids
    rows = jnp.arange(x.shape[0])
    kind = "gfi,tij->tgfj" if transposed else "gfj,tij->tgfi"
    products = jnp.einsum(kind, x, tiles, preferred_element_type=f32)
    weight = lax.rsqrt(degrees.astype(f32))

    def step(k, acc):
        g, t = near[:, k], tile_ids[:, k]
        scale = jnp.where(k < degrees, weight, 0.0)[:, None, None]
        if transposed:
            return acc.at[g].add(scale * products[t, rows])
        return acc + scale * products[t, g]

    return lax.fori_loop(0, near.shape[1], step, x.astype(f32)).astype(bf16)


def spread_first(v, tiles, per, width_k, feat_count):
    nodes, rows, size = v.shape
    width = (rows - meta_rows) // (2 * per)
    count, share = nodes * per, per // feat_count
    if width % 16:
        raw = v[:, rows - meta_rows :, :].astype(jnp.int32)
        links = raw[:, :per].reshape(count, size)
        ids = (links[:, :width_k], raw[:, per:].reshape(count, size)[:, :width_k], links[:, width_k])
        both = v[:, : rows - meta_rows].reshape(nodes, 2, per, width, size).transpose(1, 0, 2, 3, 4)
        both = both.reshape(2, count, width, size)
        out = jnp.stack([plain_spread(both[0], ids, tiles, False), plain_spread(both[1], ids, tiles, True)])
        out = out.reshape(2, nodes, feat_count, share, width, size).transpose(2, 1, 0, 4, 3, 5)
        return out.reshape(feat_count * nodes, 2, width, share * size), ids
    scratch = [pltpu.SMEM((count, size), jnp.int32)] * 3
    scratch += [pltpu.VMEM((tiles.shape[0] * count + 1, width, size), f32), pltpu.SemaphoreType.DMA((3,))]
    scratch += [pltpu.VMEM((count, width, size), f32)] * unroll
    out, ids, weight = call(
        functools.partial(first_kernel, per, width_k),
        [
            ((feat_count * nodes, 2, width, share * size), bf16),
            ((3, count, size), jnp.int32),
            ((count, size), f32),
        ],
        [vmem, vmem],
        (v, tiles),
        scratch,
        4 * tiles.shape[0] * count * width * size * size,
    )
    return out, (ids[0], ids[2], weight)


def spread_last(v, ids, tiles, per, width_k, nodes):
    size = tiles.shape[1]
    every, width, held = v.shape
    feat_count, share, count = every // nodes, held // size, nodes * per
    if width % 16:
        x = v.reshape(feat_count, nodes, width, share, size).transpose(1, 0, 3, 2, 4).reshape(count, width, size)
        out = plain_spread(x, ids, tiles, False)
        return out.reshape(nodes, per, width, size).transpose(0, 2, 1, 3).reshape(nodes, width, per * size)
    pick, near, weight = ids
    return call(
        functools.partial(last_kernel, per, width_k),
        [((nodes, width, per * size), bf16)],
        [smem, smem, vmem, vmem, vmem],
        (pick, near, weight, v, tiles),
        [
            pltpu.VMEM((count, width, size), bf16),
            pltpu.VMEM((tiles.shape[0] * count + 1, width, size), f32),
        ],
        2 * tiles.shape[0] * count * width * size * size,
    )[0]


def swap(values, axis, mask):
    return lax.ppermute(values, axis, [(i, i ^ mask) for i in range(lax.axis_size(axis))])


def gather_parts(values, axis):
    parts, offsets = [values], [0]
    bit = lax.axis_size(axis) // 2
    while bit:
        parts = parts + [swap(v, axis, bit) for v in parts]
        offsets = offsets + [o ^ bit for o in offsets]
        bit //= 2
    return parts, offsets


def project_kernel(offsets, *refs):
    count = len(offsets)
    v_ref, weights = refs[0], refs[1 : 1 + count]
    pre_ref, hidden_ref, y_ref, agg_ref = refs[1 + count : 5 + count]
    backs = refs[5 + count :]
    me = lax.axis_index("feat")
    wide = weights[0].shape[1]
    chunks, _, height, rows = v_ref.shape
    agg_ref[...] = v_ref[:, 0].reshape(chunks * height, rows)
    agg = agg_ref[...]
    place = [pl.ds(pl.multiple_of((me ^ o) * wide, wide), wide) for o in offsets]
    for at, w_ref in zip(place, weights):
        pre = jnp.dot(w_ref[0], agg, preferred_element_type=f32)
        pre_ref[at, :] = pre
        hidden_ref[at, :] = (pre * jax.nn.sigmoid(pre)).astype(bf16)
    hidden = hidden_ref[...]
    for at, w_ref in zip(place, weights):
        y_ref[at, :] = jnp.dot(w_ref[1], hidden, preferred_element_type=f32).astype(bf16)
    split = chunks // count
    for o, b_ref in zip(offsets, backs):
        if split:
            b_ref[...] = v_ref[pl.ds((me ^ o) * split, split), 1].reshape(wide, rows)
        else:
            b_ref[...] = v_ref[0, 1, pl.ds(pl.multiple_of((me ^ o) * wide, wide), wide), :]


def back_kernel(offsets, *refs):
    count = len(offsets)
    pre_ref, weights, backs, outs = refs[0], refs[1 : 1 + count], refs[1 + count : 1 + 2 * count], refs[1 + 2 * count :]
    me = lax.axis_index("feat")
    wide = weights[0].shape[1]
    for o, o_ref in zip(offsets, outs):
        at = pl.ds(pl.multiple_of((me ^ o) * wide, wide), wide)
        total = None
        for w_ref, b_ref in zip(weights, backs):
            term = lax.dot_general(
                w_ref[1, :, at], b_ref[...], (((0,), (0,)), ((), ())), preferred_element_type=f32
            )
            total = term if total is None else total + term
        pre = pre_ref[at, :]
        sigma = jax.nn.sigmoid(pre)
        o_ref[...] = (total * sigma * (1.0 + pre * (1.0 - sigma))).astype(bf16)


def grad_kernel(count, *refs):
    lefts, rights, give_ref, keep_ref = refs[:count], refs[count : 2 * count], refs[2 * count], refs[2 * count + 1]
    side = lax.axis_index("nodes") % 2
    half, tall, _ = keep_ref.shape
    for h in range(half):
        for mine in (False, True):
            row = (2 * h + (side if mine else 1 - side)) * tall
            at = pl.ds(pl.multiple_of(row, tall), tall)
            total = None
            for left, right in zip(lefts, rights):
                term = nt_dot(left[at, :], right[...])
                total = term if total is None else total + term
            if mine:
                keep_ref[h] = total
            else:
                give_ref[h] = total.astype(bf16)


def split_kernel(keep_ref, came_ref, mine_ref, *outs):
    me = lax.axis_index("nodes") // 2
    mine_ref[...] = keep_ref[me] + came_ref[me].astype(f32)
    for i, o_ref in enumerate(outs):
        to = me ^ (i + 1)
        o_ref[...] = (keep_ref[to] + came_ref[to].astype(f32)).astype(bf16)


def weight_grad(lefts, rights):
    nodes = lax.axis_size("nodes")
    count = len(lefts)
    half, tall, wide = nodes // 2, lefts[0].shape[0] // nodes, rights[0].shape[0]
    flops = 2 * count * lefts[0].shape[0] * lefts[0].shape[1] * wide
    give, keep = call(
        functools.partial(grad_kernel, count),
        [((half, tall, wide), bf16), ((half, tall, wide), f32)],
        [vmem] * (2 * count),
        (*lefts, *rights),
        flops=flops,
    )
    came = swap(give, "nodes", 1)
    mine, *rest = call(
        split_kernel,
        [((tall, wide), f32)] + [((tall, wide), bf16)] * (half - 1),
        [vmem] * 2,
        (keep, came),
    )
    for i, part in enumerate(rest):
        mine = mine + swap(part, "nodes", 2 * (i + 1)).astype(f32)
    return mine


def on_device(
    features, ghosts, slots, tile_ids, degrees, tile_table, weight_one, weight_two, cotangent
):
    nodes, feat_count = lax.axis_size("nodes"), lax.axis_size("feat")
    every = ("feat", "nodes")
    per, width_k = slots.shape
    size = tile_table.shape[1]
    rows, wide = features.shape
    held = rows // feat_count
    hidden_width = wide * feat_count
    exchange = lambda v, axes: lax.all_to_all(v, axes, split_axis=0, concat_axis=0, tiled=True)

    sent = pack(features, cotangent, ghosts, slots, tile_ids, degrees, nodes, size)
    came = exchange(sent, "nodes")
    weights, offsets = gather_parts(jnp.stack([weight_one.T, weight_two.T]), "feat")
    spreads, ids = spread_first(came, tile_table, per, width_k, feat_count)
    gathered = exchange(spreads, every)
    if gathered.shape[2] % 16:
        gathered = gathered.transpose(1, 0, 2, 3).reshape(1, 2, hidden_width, held)

    parts = len(offsets)
    pre, hidden, wide_out, agg, *backs = call(
        functools.partial(project_kernel, offsets),
        [((hidden_width, held), f32)] + [((hidden_width, held), bf16)] * 3 + [((wide, held), bf16)] * parts,
        [vmem] * (1 + parts),
        (gathered, *weights),
        flops=4 * hidden_width * hidden_width * held,
    )
    out_t = exchange(wide_out.reshape(feat_count * nodes, wide // nodes, held), every)

    turn = lambda blocks: [blocks[0]] + [swap(b, "feat", o) for b, o in zip(blocks[1:], offsets[1:])]
    hidden_parts, _ = gather_parts(hidden, "feat")
    grad_two = weight_grad(hidden_parts, turn(backs))
    agg_parts, _ = gather_parts(agg, "feat")
    back_pre = call(
        functools.partial(back_kernel, offsets),
        [((wide, held), bf16)] * parts,
        [vmem] * (1 + 2 * parts),
        (pre, *weights, *backs),
        flops=2 * hidden_width * hidden_width * held,
    )
    grad_one = weight_grad(agg_parts, turn(back_pre))

    out_n = exchange(spread_last(out_t, ids, tile_table, per, width_k, nodes), "nodes")
    output = out_n.reshape(wide, rows).T
    return (output, grad_one, grad_two)


def solution(mesh):
    return jax.shard_map(
        on_device,
        mesh=mesh,
        in_specs=(
            P("nodes", "feat"),
            P("nodes", None),
            P("nodes", None),
            P("nodes", None),
            P("nodes"),
            P(),
            P(None, "feat"),
            P(None, "feat"),
            P("nodes", "feat"),
        ),
        out_specs=(P("nodes", "feat"), P("nodes", "feat"), P("nodes", "feat")),
        check_vma=False,
    )
```

time: 419 us -> 197 us (0.47)
  waiting for transfers between devices: 217 us -> 90.7 us
  matrix products: 59.6 us -> 0 us
  other arithmetic: 54.5 us -> 1.47 us
  Pallas kernels: 0 us -> 38.3 us
  starting transfers between devices: 11.8 us -> 40.4 us
  local copies, waits for them, and re-layouts: 44.4 us -> 24.5 us
  between operations: 14.7 us -> 0.87 us
  blocking collectives: 13.5 us -> 0 us
    reduce_scatter x3 -> x0, waiting for transfers between devices: 129 us -> none  [the longest x2 129 us: weight_grad(): lax.psum_scatter(lax.dot_general(wide_rows, local_rows, (((0,), (0,)), ((...]
    dot_general x14 -> x0, matrix products: 59.6 us -> none  [the longest x6 24.9 us: collect_advance(): jnp.einsum('bkij,bkjf->bkif', picked, near_rows, preferred_element_type=j...]
    ppermute x0 -> x23, waiting for transfers between devices: none -> 43 us  [swap(): lax.ppermute(values, axis, [(i, i ^ mask) for i in range(lax.axis_size(ax...]
    scatter-add x4 -> x0, other arithmetic: 40.8 us -> none  [the longest x3 37.3 us: scatter_advance(): jax.ops.segment_sum(scaled.reshape(-1, block_size, feat_width), near_ids....]
    gather x17 -> x0, local copies, waits for them, and re-layouts: 39.3 us -> none  [the longest x6 16.6 us: collect_advance(): near_rows = ghost_rows[near_ids]]
    pallas_call x0 -> x9, Pallas kernels: none -> 38.3 us  [call(): pl.pallas_call(body, out_shape=[jax.ShapeDtypeStruct(s, d) for s, d in ou...]
    all_to_all x3 -> x4, waiting for transfers between devices: 70.2 us -> 47.7 us  [on_device(): lax.all_to_all(v, axes, split_axis=0, concat_axis=0, tiled=True)]
    unnamed x26 -> x71, local copies, waits for them, and re-layouts: 1.7 us -> 22.5 us
  transfers between devices with their start and end apart: 8 -> 27, of which waited for: 6 -> 12; matrix products, arithmetic and copies ran while one was open for 28% -> 1% of each run, Pallas kernels for 0% -> 17%
where the time goes in v2:
time: 197 us; the launch traced here: 196 us
  waiting for transfers between devices  90.7 us (46%)
  starting transfers between devices  40.4 us (21%)
  Pallas kernels  38.3 us (19%)
  local copies, waits for them, and re-layouts  24.5 us (12%)
    all_to_all x4, waiting for transfers between devices, on_device(): lax.all_to_all(v, axes, split_axis=0, concat_axis=0, tiled=True)  47.7 us
    ppermute x23, waiting for transfers between devices, swap(): lax.ppermute(values, axis, [(i, i ^ mask) for i in range(lax.axis_size(ax...  43 us
    pallas_call x9, Pallas kernels, call(): pl.pallas_call(body, out_shape=[jax.ShapeDtypeStruct(s, d) for s, d in ou...  38.3 us
    unnamed x71, local copies, waits for them, and re-layouts  22.5 us
    all_to_all x4, starting transfers between devices, on_device(): lax.all_to_all(v, axes, split_axis=0, concat_axis=0, tiled=True)  20.5 us
    ppermute x23, starting transfers between devices, swap(): lax.ppermute(values, axis, [(i, i ^ mask) for i in range(lax.axis_size(ax...  19.9 us
  transfers between devices with their start and end apart: 27, of which 12 were waited for; matrix products, arithmetic and copies ran while one was open for 1% of the time, Pallas kernels for 17%

profile of v2, /device:TPU:0, one launch (start us, length us, event | category | flops | bytes accessed | tf_op | source)
XLA Modules:
  0.0 196.3 jit_solution(2754015813533002227)
XLA Ops:
  5.5 1.9 shard_map.112
  7.4 7.4 %all-to-all-start = ((bf16[8,528,128]{2,1,0:T(8,128)(2,1)}), bf16[8,528,128]{2,1,0:T(8,128)(2,1)}, u32[]{:S(2)}, u32[]{:S(2)}) async-start(bf16[8,528,128]{2,1,0:T(8,128)(2,1)} %shard_map.112), calls=%async_computation | async-start | bytes 2162688 | tf_op jit(solution)/shard_map/all_to_all | solution.py:406
  16.9 24.5 %all-to-all-done.v_ref = bf16[8,528,128]{2,1,0:T(8,128)(2,1)} async-done(((bf16[8,528,128]{2,1,0:T(8,128)(2,1)}), bf16[8,528,128]{2,1,0:T(8,128)(2,1)}, u32[]{:S(2)}, u32[]{:S(2)}) %all-to-all-start) | async-done | bytes 1081376 | tf_op jit(solution)/shard_map/all_to_all | solution.py:406
  41.4 16.3 %shard_map.113 = (bf16[32,2,32,256]{3,2,1,0:T(8,128)(2,1)S(1)}, s32[3,64,128]{2,1,0:T(8,128)S(1)}, f32[64,128]{1,0:T(8,128)S(1)}) custom-call(bf16[8,528,128]{2,1,0:T(8,128)(2,1)} %all-to-all-done.v_ref, bf16[16,128,128]{2,1,0:T(8,128)(2,1)S(1)} %copy-done.28), custom_call_target="tpu_custom_call" | custom-call | flops 2147483648 | bytes 4194304 | tf_op jit(solution)/shard_map/pallas_call | solution.py:22
  60.0 3.6 %all-to-all-start.1 = ((bf16[32,2,32,256]{3,2,1,0:T(8,128)(2,1)}), bf16[32,2,32,256]{3,2,1,0:T(8,128)(2,1)S(1)}, u32[]{:S(2)}, u32[]{:S(2)}) async-start(bf16[32,2,32,256]{3,2,1,0:T(8,128)(2,1)} %copy-done.4), calls=%async_computation.1 | async-start | bytes 2097152 | tf_op jit(solution)/shard_map/all_to_all | solution.py:406
  64.2 2.1 %collective-permute-done.1.refs_3_ = bf16[2,256,1024]{2,1,0:T(8,128)(2,1)S(1)} collective-permute-done((bf16[2,256,1024]{2,1,0:T(8,128)(2,1)S(1)}, bf16[2,256,1024]{2,1,0:T(8,128)(2,1)S(1)}, u32[]{:S(2)}, u32[]{:S(2)}) %collective-permute-start.1) | collective-permute-done | bytes 1048608 | tf_op jit(solution)/shard_map/ppermute | solution.py:289
  68.0 23.2 %all-to-all-done.1.refs_0_ = bf16[32,2,32,256]{3,2,1,0:T(8,128)(2,1)S(1)} async-done(((bf16[32,2,32,256]{3,2,1,0:T(8,128)(2,1)}), bf16[32,2,32,256]{3,2,1,0:T(8,128)(2,1)S(1)}, u32[]{:S(2)}, u32[]{:S(2)}) %all-to-all-start.1) | async-done | bytes 1048608 | tf_op jit(solution)/shard_map/all_to_all | solution.py:406
  91.2 3.9 %shard_map.114 = (f32[1024,256]{1,0:T(8,128)S(1)}, bf16[1024,256]{1,0:T(8,128)(2,1)S(1)}, bf16[1024,256]{1,0:T(8,128)(2,1)S(1)}, bf16[1024,256]{1,0:T(8,128)(2,1...) custom-call(bf16[32,2,32,256]{3,2,1,0:T(8,128)(2,1)S(1)} %all-to-all, ...), custom_call_target="tpu_custom_call" | custom-call | flops 1073741824 | bytes 4194304 | tf_op jit(solution)/shard_map/pallas_call | solution.py:22
  98.4 3.5 %all-to-all-start.2 = ((bf16[32,32,256]{2,1,0:T(8,128)(2,1)}), bf16[32,32,256]{2,1,0:T(8,128)(2,1)}, u32[]{:S(2)}, u32[]{:S(2)}) async-start(bf16[32,32,256]{2,1,0:T(8,128)(2,1)} %bitcast.13), calls=%async_computation.2 | async-start | bytes 1048576 | tf_op jit(solution)/shard_map/all_to_all | solution.py:406
  106.5 2.3 %shard_map.116 = (bf16[256,256]{1,0:T(8,128)(2,1)S(1)}, bf16[256,256]{1,0:T(8,128)(2,1)S(1)}, bf16[256,256]{1,0:T(8,128)(2,1)S(1)}, bf16[256,256]{1,0:T(8,128)(2,1)S(1)}) custom-call(f32[1024,256]{1,0:T(8,128)S(1)} %copy-done.6, bf16[2,256,1024]{2,1,0:T(8,128)(2,1)S(1)} %pad_maximum_fusion.refs_1_, bf16[2,256,1024]{2,1,0:T(8,128)(2,1)S(1)} %copy-done.1, ...), custom_call_target="tpu_custom_call" | custom-call | flops 536870912 | bytes 4194304 | tf_op jit(solution)/shard_map/pallas_call | solution.py:22
  111.0 10.9 %collective-permute-done.3.refs_1_ = bf16[1024,256]{1,0:T(8,128)(2,1)} collective-permute-done((bf16[1024,256]{1,0:T(8,128)(2,1)}, bf16[1024,256]{1,0:T(8,128)(2,1)}, u32[]{:S(2)}, u32[]{:S(2)}) %collective-permute-start.3) | collective-permute-done | bytes 524320 | tf_op jit(solution)/shard_map/ppermute | solution.py:289
  122.4 13.0 %collective-permute-done.6.refs_5_ = bf16[256,256]{1,0:T(8,128)(2,1)S(1)} collective-permute-done((bf16[256,256]{1,0:T(8,128)(2,1)S(1)}, bf16[256,256]{1,0:T(8,128)(2,1)S(1)}, u32[]{:S(2)}, u32[]{:S(2)}) %collective-permute-start.6) | collective-permute-done | bytes 131104 | tf_op jit(solution)/shard_map/ppermute | solution.py:289
  136.6 5.5 %collective-permute-done.8.refs_7_ = bf16[256,256]{1,0:T(8,128)(2,1)S(1)} collective-permute-done((bf16[256,256]{1,0:T(8,128)(2,1)S(1)}, bf16[256,256]{1,0:T(8,128)(2,1)S(1)}, u32[]{:S(2)}, u32[]{:S(2)}) %collective-permute-start.8) | collective-permute-done | bytes 131104 | tf_op jit(solution)/shard_map/ppermute | solution.py:289
  144.9 8.8 %shard_map.115 = bf16[8,32,1024]{2,1,0:T(8,128)(2,1)S(1)} custom-call(s32[64,128]{1,0:T(8,128)S(1)} %get-tuple-element.58.pick, s32[64,128]{1,0:T(8,128)S(1)} %get-tuple-element.57.near, f32[64,128]{1,0:T(8,128)S(1)} %copy-done.31, bf16[32,32,256]{2,1,0:T(8,128)(2,1)} %all-to-all-done.2.v_ref, bf16[16,128,128]{2,1,0:T(8,128)(2,1)S(1)} %copy-done.29), custom_call_target="tpu_custom_call" | custom-call | flops 1073741824 | bytes 4194304 | tf_op jit(solution)/shard_map/pallas_call | solution.py:22
  154.5 6.0 %all-to-all-start.3 = ((bf16[8,32,1024]{2,1,0:T(8,128)(2,1)}), bf16[8,32,1024]{2,1,0:T(8,128)(2,1)}, u32[]{:S(2)}, u32[]{:S(2)}) async-start(bf16[8,32,1024]{2,1,0:T(8,128)(2,1)} %copy-done.13), calls=%async_computation.3 | async-start | bytes 1048576 | tf_op jit(solution)/shard_map/all_to_all | solution.py:406
  165.8 2.6 %shard_map.117 = (bf16[4,128,256]{2,1,0:T(8,128)(2,1)S(1)}, f32[4,128,256]{2,1,0:T(8,128)S(1)}) custom-call(bf16[1024,256]{1,0:T(8,128)(2,1)S(1)} %copy-done.12, bf16[1024,256]{1,0:T(8,128)(2,1)} %collective-permute-done.3.refs_1_, bf16[1024,256]{1,0:T(8,128)(2,1)} %collective-permute-done.4.refs_2_, bf16[1024,256]{1,0:T(8,128)(2,1)S(1)} %collective-permute-done.5.refs_3_, ...), custom_call_target="tpu_custom_call" | custom-call | flops 536870912 | bytes 4194304 | tf_op jit(solution)/shard_map/pallas_call | solution.py:22
  168.5 2.0 %collective-permute-start.9 = (bf16[4,128,256]{2,1,0:T(8,128)(2,1)S(1)}, bf16[4,128,256]{2,1,0:T(8,128)(2,1)S(1)}, u32[]{:S(2)}, u32[]{:S(2)}) collective-permute-start(bf16[4,128,256]{2,1,0:T(8,128)(2,1)S(1)} %get-tuple-element.45), channel_id=1, source_target_pairs={{0,4},{4,0},{8,12},{12,8},{16,20},{20,16},{24,28},{28,24},{1,5},{5... | collective-permute-start | bytes 786440 | tf_op jit(solution)/shard_map/ppermute | solution.py:289
  170.5 2.3 %shard_map.119 = (bf16[4,128,256]{2,1,0:T(8,128)(2,1)S(1)}, f32[4,128,256]{2,1,0:T(8,128)S(1)}) custom-call(bf16[1024,256]{1,0:T(8,128)(2,1)S(1)} %copy-done.10, bf16[1024,256]{1,0:T(8,128)(2,1)S(1)} %collective-permute-done.13.refs_1_, bf16[1024,256]{1,0:T(8,128)(2,1)S(1)} %collective-permute-done.14.refs_2_, ...), custom_call_target="tpu_custom_call" | custom-call | flops 536870912 | bytes 4194304 | tf_op jit(solution)/shard_map/pallas_call | solution.py:22
  173.0 5.4 %collective-permute-done.9.came_ref = bf16[4,128,256]{2,1,0:T(8,128)(2,1)S(1)} collective-permute-done((bf16[4,128,256]{2,1,0:T(8,128)(2,1)S(1)}, bf16[4,128,256]{2,1,0:T(8,128)(2,1)S(1)}, u32[]{:S(2)}, u32[]{:S(2)}) %collective-permute-start.9) | collective-permute-done | bytes 262176 | tf_op jit(solution)/shard_map/ppermute | solution.py:289
  178.4 2.0 %collective-permute-start.10 = (bf16[128,256]{1,0:T(8,128)(2,1)S(1)}, bf16[128,256]{1,0:T(8,128)(2,1)S(1)}, u32[]{:S(2)}, u32[]{:S(2)}) collective-permute-start(bf16[128,256]{1,0:T(8,128)(2,1)S(1)} %get-tuple-element.47), channel_id=1, source_target_pairs={{0,8},{4,12},{8,0},{12,4},{16,24},{20,28},{24,16},{28,20},{1,9},{5... | collective-permute-start | bytes 196616 | tf_op jit(solution)/shard_map/ppermute | solution.py:289
  180.5 1.7 collective-permute-start.11
  183.4 1.8 collective-permute-start.20
  189.3 4.2 %collective-permute-done.21 = bf16[128,256]{1,0:T(8,128)(2,1)S(1)} collective-permute-done((bf16[128,256]{1,0:T(8,128)(2,1)S(1)}, bf16[128,256]{1,0:T(8,128)(2,1)S(1)}, u32[]{:S(2)}, u32[]{:S(2)}) %collective-permute-start.21) | collective-permute-done | bytes 65568 | tf_op jit(solution)/shard_map/ppermute | solution.py:289
  194.2 2.0 %copy.15 = bf16[256,1024]{0,1:T(8,128)(2,1)} copy(bf16[256,1024]{1,0:T(8,128)(2,1)} %bitcast.7) | data formatting | bytes 1048576 | tf_op jit(solution)/shard_map/reshape | solution.py:440
  (115 shorter events, 38.3 us)
Async XLA Ops:
  7.4 34.0 %all-to-all-start = ((bf16[8,528,128]{2,1,0:T(8,128)(2,1)}), bf16[8,528,128]{2,1,0:T(8,128)(2,1)}, u32[]{:S(2)}, u32[]{:S(2)}) async-start(bf16[8,528,128]{2,1,0:T(8,128)(2,1)} %shard_map.112), calls=%async_computation | async-start | bytes 2162688 | tf_op jit(solution)/shard_map/all_to_all | solution.py:406
  15.4 48.5 %collective-permute-start = (bf16[2,256,1024]{2,1,0:T(8,128)(2,1)S(1)}, bf16[2,256,1024]{2,1,0:T(8,128)(2,1)S(1)}, u32[]{:S(2)}, u32[]{:S(2)}) collective-permute-start(bf16[2,256,1024]{2,1,0:T(8,128)(2,1)S(1)} %pad_maximum_fusion.refs_1_), channel_id=1, source_target_pairs={{0,2},{1,3},{2,0},{3,1},{4,6},{5,7},{6,4},{7,5},{8,10},{9,11},{10,... | collective-permute-start | bytes 3145736 | tf_op jit(solution)/shard_map/ppermute | solution.py:289
  60.0 31.2 %all-to-all-start.1 = ((bf16[32,2,32,256]{3,2,1,0:T(8,128)(2,1)}), bf16[32,2,32,256]{3,2,1,0:T(8,128)(2,1)S(1)}, u32[]{:S(2)}, u32[]{:S(2)}) async-start(bf16[32,2,32,256]{3,2,1,0:T(8,128)(2,1)} %copy-done.4), calls=%async_computation.1 | async-start | bytes 2097152 | tf_op jit(solution)/shard_map/all_to_all | solution.py:406
  98.4 44.7 %all-to-all-start.2 = ((bf16[32,32,256]{2,1,0:T(8,128)(2,1)}), bf16[32,32,256]{2,1,0:T(8,128)(2,1)}, u32[]{:S(2)}, u32[]{:S(2)}) async-start(bf16[32,32,256]{2,1,0:T(8,128)(2,1)} %bitcast.13), calls=%async_computation.2 | async-start | bytes 1048576 | tf_op jit(solution)/shard_map/all_to_all | solution.py:406
  101.9 20.0 %collective-permute-start.3 = (bf16[1024,256]{1,0:T(8,128)(2,1)}, bf16[1024,256]{1,0:T(8,128)(2,1)}, u32[]{:S(2)}, u32[]{:S(2)}) collective-permute-start(bf16[1024,256]{1,0:T(8,128)(2,1)} %copy-done.11), channel_id=1, source_target_pairs={{0,2},{1,3},{2,0},{3,1},{4,6},{5,7},{6,4},{7,5},{8,10},{9,11},{10,... | collective-permute-start | bytes 1572872 | tf_op jit(solution)/shard_map/ppermute | solution.py:289
  103.5 31.9 %collective-permute-start.13 = (bf16[1024,256]{1,0:T(8,128)(2,1)}, bf16[1024,256]{1,0:T(8,128)(2,1)S(1)}, u32[]{:S(2)}, u32[]{:S(2)}) collective-permute-start(bf16[1024,256]{1,0:T(8,128)(2,1)} %copy-done.9), channel_id=1, source_target_pairs={{0,2},{1,3},{2,0},{3,1},{4,6},{5,7},{6,4},{7,5},{8,10},{9,11},{10,... | collective-permute-start | bytes 1572872 | tf_op jit(solution)/shard_map/ppermute | solution.py:289
  104.0 56.5 %collective-permute-start.4 = (bf16[1024,256]{1,0:T(8,128)(2,1)}, bf16[1024,256]{1,0:T(8,128)(2,1)}, u32[]{:S(2)}, u32[]{:S(2)}) collective-permute-start(bf16[1024,256]{1,0:T(8,128)(2,1)} %copy-done.11), channel_id=1, source_target_pairs={{0,1},{1,0},{2,3},{3,2},{4,5},{5,4},{6,7},{7,6},{8,9},{9,8},{10,11... | collective-permute-start | bytes 1572872 | tf_op jit(solution)/shard_map/ppermute | solution.py:289
  109.4 26.0 %collective-permute-start.6 = (bf16[256,256]{1,0:T(8,128)(2,1)S(1)}, bf16[256,256]{1,0:T(8,128)(2,1)S(1)}, u32[]{:S(2)}, u32[]{:S(2)}) collective-permute-start(bf16[256,256]{1,0:T(8,128)(2,1)S(1)} %get-tuple-element.41), channel_id=1, source_target_pairs={{0,2},{1,3},{2,0},{3,1},{4,6},{5,7},{6,4},{7,5},{8,10},{9,11},{10,... | collective-permute-start | bytes 393224 | tf_op jit(solution)/shard_map/ppermute | solution.py:289
  121.9 38.7 %collective-permute-start.5 = (bf16[1024,256]{1,0:T(8,128)(2,1)}, bf16[1024,256]{1,0:T(8,128)(2,1)S(1)}, u32[]{:S(2)}, u32[]{:S(2)}) collective-permute-start(bf16[1024,256]{1,0:T(8,128)(2,1)} %collective-permute-done.3.refs_1_), channel_id=1, source_target_pairs={{0,1},{1,0},{2,3},{3,2},{4,5},{5,4},{6,7},{7,6},{8,9},{9,8},{10,11... | collective-permute-start | bytes 1572872 | tf_op jit(solution)/shard_map/ppermute | solution.py:289
  121.9 14.0 %collective-permute-start.7 = (bf16[256,256]{1,0:T(8,128)(2,1)S(1)}, bf16[256,256]{1,0:T(8,128)(2,1)S(1)}, u32[]{:S(2)}, u32[]{:S(2)}) collective-permute-start(bf16[256,256]{1,0:T(8,128)(2,1)S(1)} %get-tuple-element.42), channel_id=1, source_target_pairs={{0,1},{1,0},{2,3},{3,2},{4,5},{5,4},{6,7},{7,6},{8,9},{9,8},{10,11... | collective-permute-start | bytes 393224 | tf_op jit(solution)/shard_map/ppermute | solution.py:289
  135.4 35.1 %collective-permute-start.14 = (bf16[1024,256]{1,0:T(8,128)(2,1)S(1)}, bf16[1024,256]{1,0:T(8,128)(2,1)S(1)}, u32[]{:S(2)}, u32[]{:S(2)}) collective-permute-start(bf16[1024,256]{1,0:T(8,128)(2,1)S(1)} %copy-done.10), channel_id=1, source_target_pairs={{0,1},{1,0},{2,3},{3,2},{4,5},{5,4},{6,7},{7,6},{8,9},{9,8},{10,11... | collective-permute-start | bytes 1572872 | tf_op jit(solution)/shard_map/ppermute | solution.py:289
  135.4 35.1 %collective-permute-start.15 = (bf16[1024,256]{1,0:T(8,128)(2,1)S(1)}, bf16[1024,256]{1,0:T(8,128)(2,1)S(1)}, u32[]{:S(2)}, u32[]{:S(2)}) collective-permute-start(bf16[1024,256]{1,0:T(8,128)(2,1)S(1)} %collective-permute-done.13.refs_1_), channel_id=1, source_target_pairs={{0,1},{1,0},{2,3},{3,2},{4,5},{5,4},{6,7},{7,6},{8,9},{9,8},{10,11... | collective-permute-start | bytes 1572872 | tf_op jit(solution)/shard_map/ppermute | solution.py:289
  142.8 25.7 %collective-permute-start.16 = (bf16[256,256]{1,0:T(8,128)(2,1)}, bf16[256,256]{1,0:T(8,128)(2,1)}, u32[]{:S(2)}, u32[]{:S(2)}) collective-permute-start(bf16[256,256]{1,0:T(8,128)(2,1)} %get-tuple-element.37.refs_6_), channel_id=1, source_target_pairs={{0,2},{1,3},{2,0},{3,1},{4,6},{5,7},{6,4},{7,5},{8,10},{9,11},{10,... | collective-permute-start | bytes 393224 | tf_op jit(solution)/shard_map/ppermute | solution.py:289
  154.5 39.7 %all-to-all-start.3 = ((bf16[8,32,1024]{2,1,0:T(8,128)(2,1)}), bf16[8,32,1024]{2,1,0:T(8,128)(2,1)}, u32[]{:S(2)}, u32[]{:S(2)}) async-start(bf16[8,32,1024]{2,1,0:T(8,128)(2,1)} %copy-done.13), calls=%async_computation.3 | async-start | bytes 1048576 | tf_op jit(solution)/shard_map/all_to_all | solution.py:406
  160.5 10.0 %collective-permute-start.17 = (bf16[256,256]{1,0:T(8,128)(2,1)S(1)}, bf16[256,256]{1,0:T(8,128)(2,1)S(1)}, u32[]{:S(2)}, u32[]{:S(2)}) collective-permute-start(bf16[256,256]{1,0:T(8,128)(2,1)S(1)} %get-tuple-element.38.refs_7_), channel_id=1, source_target_pairs={{0,1},{1,0},{2,3},{3,2},{4,5},{5,4},{6,7},{7,6},{8,9},{9,8},{10,11... | collective-permute-start | bytes 393224 | tf_op jit(solution)/shard_map/ppermute | solution.py:289
  160.6 9.9 %collective-permute-start.18 = (bf16[256,256]{1,0:T(8,128)(2,1)S(1)}, bf16[256,256]{1,0:T(8,128)(2,1)S(1)}, u32[]{:S(2)}, u32[]{:S(2)}) collective-permute-start(bf16[256,256]{1,0:T(8,128)(2,1)S(1)} %get-tuple-element.39.refs_8_), channel_id=1, source_target_pairs={{0,3},{1,2},{2,1},{3,0},{4,7},{5,6},{6,5},{7,4},{8,11},{9,10},{10,... | collective-permute-start | bytes 393224 | tf_op jit(solution)/shard_map/ppermute | solution.py:289
  168.5 9.9 %collective-permute-start.9 = (bf16[4,128,256]{2,1,0:T(8,128)(2,1)S(1)}, bf16[4,128,256]{2,1,0:T(8,128)(2,1)S(1)}, u32[]{:S(2)}, u32[]{:S(2)}) collective-permute-start(bf16[4,128,256]{2,1,0:T(8,128)(2,1)S(1)} %get-tuple-element.45), channel_id=1, source_target_pairs={{0,4},{4,0},{8,12},{12,8},{16,20},{20,16},{24,28},{28,24},{1,5},{5... | collective-permute-start | bytes 786440 | tf_op jit(solution)/shard_map/ppermute | solution.py:289
  172.9 10.5 %collective-permute-start.19 = (bf16[4,128,256]{2,1,0:T(8,128)(2,1)S(1)}, bf16[4,128,256]{2,1,0:T(8,128)(2,1)S(1)}, u32[]{:S(2)}, u32[]{:S(2)}) collective-permute-start(bf16[4,128,256]{2,1,0:T(8,128)(2,1)S(1)} %get-tuple-element.52), channel_id=1, source_target_pairs={{0,4},{4,0},{8,12},{12,8},{16,20},{20,16},{24,28},{28,24},{1,5},{5... | collective-permute-start | bytes 786440 | tf_op jit(solution)/shard_map/ppermute | solution.py:289
  178.4 8.4 %collective-permute-start.10 = (bf16[128,256]{1,0:T(8,128)(2,1)S(1)}, bf16[128,256]{1,0:T(8,128)(2,1)S(1)}, u32[]{:S(2)}, u32[]{:S(2)}) collective-permute-start(bf16[128,256]{1,0:T(8,128)(2,1)S(1)} %get-tuple-element.47), channel_id=1, source_target_pairs={{0,8},{4,12},{8,0},{12,4},{16,24},{20,28},{24,16},{28,20},{1,9},{5... | collective-permute-start | bytes 196616 | tf_op jit(solution)/shard_map/ppermute | solution.py:289
  180.5 7.4 %collective-permute-start.11 = (bf16[128,256]{1,0:T(8,128)(2,1)S(1)}, bf16[128,256]{1,0:T(8,128)(2,1)S(1)}, u32[]{:S(2)}, u32[]{:S(2)}) collective-permute-start(bf16[128,256]{1,0:T(8,128)(2,1)S(1)} %get-tuple-element.48), channel_id=1, source_target_pairs={{0,16},{4,20},{8,24},{12,28},{16,0},{20,4},{24,8},{28,12},{1,17},{... | collective-permute-start | bytes 196616 | tf_op jit(solution)/shard_map/ppermute | solution.py:289
  182.1 6.2 %collective-permute-start.12 = (bf16[128,256]{1,0:T(8,128)(2,1)S(1)}, bf16[128,256]{1,0:T(8,128)(2,1)S(1)}, u32[]{:S(2)}, u32[]{:S(2)}) collective-permute-start(bf16[128,256]{1,0:T(8,128)(2,1)S(1)} %get-tuple-element.49), channel_id=1, source_target_pairs={{0,24},{4,28},{8,16},{12,20},{16,8},{20,12},{24,0},{28,4},{1,25},{... | collective-permute-start | bytes 196616 | tf_op jit(solution)/shard_map/ppermute | solution.py:289
  183.4 5.9 %collective-permute-start.20 = (bf16[128,256]{1,0:T(8,128)(2,1)S(1)}, bf16[128,256]{1,0:T(8,128)(2,1)S(1)}, u32[]{:S(2)}, u32[]{:S(2)}) collective-permute-start(bf16[128,256]{1,0:T(8,128)(2,1)S(1)} %get-tuple-element.54), channel_id=1, source_target_pairs={{0,8},{4,12},{8,0},{12,4},{16,24},{20,28},{24,16},{28,20},{1,9},{5... | collective-permute-start | bytes 196616 | tf_op jit(solution)/shard_map/ppermute | solution.py:289
  185.2 8.3 %collective-permute-start.21 = (bf16[128,256]{1,0:T(8,128)(2,1)S(1)}, bf16[128,256]{1,0:T(8,128)(2,1)S(1)}, u32[]{:S(2)}, u32[]{:S(2)}) collective-permute-start(bf16[128,256]{1,0:T(8,128)(2,1)S(1)} %get-tuple-element.55), channel_id=1, source_target_pairs={{0,16},{4,20},{8,24},{12,28},{16,0},{20,4},{24,8},{28,12},{1,17},{... | collective-permute-start | bytes 196616 | tf_op jit(solution)/shard_map/ppermute | solution.py:289
  186.9 6.7 %collective-permute-start.22 = (bf16[128,256]{1,0:T(8,128)(2,1)S(1)}, bf16[128,256]{1,0:T(8,128)(2,1)S(1)}, u32[]{:S(2)}, u32[]{:S(2)}) collective-permute-start(bf16[128,256]{1,0:T(8,128)(2,1)S(1)} %get-tuple-element.56), channel_id=1, source_target_pairs={{0,24},{4,28},{8,16},{12,20},{16,8},{20,12},{24,0},{28,4},{1,25},{... | collective-permute-start | bytes 196616 | tf_op jit(solution)/shard_map/ppermute | solution.py:289
  (37 other events, 182.2 us)

commit v3 on v2

v3 whole, which is shorter than its diff:
```python
import functools

import jax
import jax.numpy as jnp
from jax import lax
from jax.experimental import pallas as pl
from jax.experimental.pallas import tpu as pltpu
from jax.sharding import PartitionSpec as P

unroll = 4
tile_step = 4
meta_rows = 16
bf16, f32 = jnp.bfloat16, jnp.float32
vmem = pl.BlockSpec(memory_space=pltpu.VMEM)
smem = pl.BlockSpec(memory_space=pltpu.SMEM)


def nt_dot(a, b):
    return lax.dot_general(a, b, (((1,), (1,)), ((), ())), preferred_element_type=f32)


def call(body, outs, in_specs, args, scratch=(), flops=0, limit=56):
    return pl.pallas_call(
        body,
        out_shape=[jax.ShapeDtypeStruct(s, d) for s, d in outs],
        in_specs=in_specs,
        out_specs=[vmem] * len(outs),
        scratch_shapes=list(scratch),
        compiler_params=pltpu.CompilerParams(vmem_limit_bytes=limit * 1024 * 1024),
        cost_estimate=pl.CostEstimate(flops=flops, bytes_accessed=4 << 20, transcendentals=0),
    )(*args)


def meta_tile(ghost_at, degree_at, slots, tile_ids, owners, held, size):
    per, width_k = slots.shape
    near = jnp.zeros((per, width_k), jnp.int32)
    for s in range(owners * held):
        near = jnp.where(slots == s, (s // held) * per + ghost_at(s // held, s % held), near)
    row = lax.broadcasted_iota(jnp.int32, (per, size), 0)
    lane = lax.broadcasted_iota(jnp.int32, (per, size), 1)
    degree = jnp.zeros((per, size), jnp.int32)
    for r in range(per):
        degree = jnp.where(row == r, degree_at(r), degree)
    widen = lambda v: jnp.concatenate([v, jnp.zeros((per, size - width_k), jnp.int32)], axis=1)
    top = jnp.where(lane == width_k, degree, widen(near))
    return jnp.concatenate([top, widen(tile_ids)], axis=0).astype(f32).astype(bf16)


def pack_kernel(owners, held, ghosts, degrees, slots_ref, tiles_ref, feat_ref, o_ref):
    nodes, rows, size = o_ref.shape
    width = feat_ref.shape[1] // nodes
    per = feat_ref.shape[0] // size
    for b in range(per):
        turned = feat_ref[b * size : (b + 1) * size, :].T
        for n in range(nodes):
            o_ref[n, b * width : (b + 1) * width, :] = turned[n * width : (n + 1) * width]
    tile = meta_tile(
        lambda p, c: ghosts[p, c], lambda r: degrees[r], slots_ref[...], tiles_ref[...], owners, held, size
    )
    for n in range(nodes):
        o_ref[n, rows - meta_rows :, :] = tile


def turn_blocks(values, nodes, size):
    per, width = values.shape[0] // size, values.shape[1] // nodes
    return values.reshape(per, size, nodes, width).transpose(2, 0, 3, 1).reshape(nodes, per * width, size)


def pack(features, ghosts, slots, tile_ids, degrees, nodes, size):
    owners, held = ghosts.shape
    per = slots.shape[0]
    width = features.shape[1] // nodes
    if width % 16:
        tile = meta_tile(lambda p, c: ghosts[p, c], lambda r: degrees[r], slots, tile_ids, owners, held, size)
        tile = jnp.broadcast_to(tile, (nodes,) + tile.shape)
        return jnp.concatenate([turn_blocks(features, nodes, size), tile], axis=1)
    return call(
        functools.partial(pack_kernel, owners, held),
        [((nodes, per * width + meta_rows, size), bf16)],
        [smem, smem, vmem, vmem, vmem],
        (ghosts, degrees, slots, tile_ids, features),
    )[0]


def turn_kernel(v_ref, *refs):
    outs, turned_ref = refs[:-1], refs[-1]
    size = outs[0].shape[1]
    per = v_ref.shape[0] // size
    width = v_ref.shape[1] // len(outs)
    me = lax.axis_index("nodes")
    for b in range(per):
        turned_ref[b] = v_ref[b * size : (b + 1) * size, :].T
    for i, o_ref in enumerate(outs):
        at = pl.ds(pl.multiple_of((me ^ i) * width, width), width)
        for b in range(per):
            o_ref[b * width : (b + 1) * width, :] = turned_ref[b, at, :]


def pack_parts(values, nodes, size):
    per, width = values.shape[0] // size, values.shape[1] // nodes
    if width % 16:
        me = lax.axis_index("nodes")
        turned = turn_blocks(values, nodes, size)
        return [lax.dynamic_index_in_dim(turned, me ^ i, 0, keepdims=False) for i in range(nodes)]
    return call(
        turn_kernel,
        [((per * width, size), bf16)] * nodes,
        [vmem],
        (values,),
        [pltpu.VMEM((per, values.shape[1], size), bf16)],
    )


def form_products(lefts, count, width, tiles_ref, p_ref, transposed):
    tile_count, size = tiles_ref.shape[0], tiles_ref.shape[1]

    def step(turn, carry):
        some = tiles_ref[pl.ds(tile_step * turn, tile_step)]
        if transposed:
            right = jnp.concatenate([some[i] for i in range(tile_step)], axis=1)
        else:
            right = some.reshape(tile_step * size, size)
        for first, load in lefts:
            left = load()
            res = jnp.dot(left, right, preferred_element_type=f32) if transposed else nt_dot(left, right)
            group = left.shape[0] // width
            for i in range(tile_step):
                part = res[:, i * size : (i + 1) * size].reshape(group, width, size)
                p_ref[pl.ds((tile_step * turn + i) * count + first, group)] = part
        return carry

    lax.fori_loop(0, tile_count // tile_step, step, 0)
    p_ref[tile_count * count] = jnp.zeros((width, size), f32)


def sum_entries(pick, r, width_k, p_ref):
    terms = [p_ref[pick[r, k]] for k in range(width_k)]
    while len(terms) > 1:
        terms = [terms[i] + terms[i + 1] for i in range(0, len(terms) - 1, 2)] + terms[len(terms) & ~1 :]
    return terms[0]


def first_kernel(per, width_k, v_ref, tiles_ref, o_ref, ids_ref, weight_ref, pick, p_ref, sem):
    nodes, _, size = v_ref.shape
    width = o_ref.shape[1]
    share = o_ref.shape[2] // size
    count = nodes * per
    span = per * width
    empty = tiles_ref.shape[0] * count
    lane = lax.broadcasted_iota(jnp.int32, (per, size), 1)
    row = lax.broadcasted_iota(jnp.int32, (per, size), 0)
    for n in range(nodes):
        raw = v_ref[n, span:, :].astype(f32).astype(jnp.int32)
        links, tile = raw[:per], raw[per:]
        degree = jnp.broadcast_to(links[:, width_k : width_k + 1], (per, size))
        live = lane < degree
        block = slice(n * per, (n + 1) * per)
        ids_ref[0, block] = jnp.where(live, tile * count + links, empty)
        ids_ref[1, block] = jnp.where(live, tile * count + (row + n * per), empty)
        ids_ref[2, block] = links
        weight_ref[block] = lax.rsqrt(degree.astype(f32))
    copy = pltpu.make_async_copy(ids_ref.at[0], pick, sem)
    copy.start()
    lefts = [(n * per, lambda n=n: v_ref[n, :span, :]) for n in range(nodes)]
    form_products(lefts, count, width, tiles_ref, p_ref, False)
    copy.wait()

    def rows(n, carry):
        for b in range(per):
            r = n * per + b
            own = v_ref[n, b * width : (b + 1) * width, :].astype(f32)
            j = b % share
            value = (own + weight_ref[pl.ds(r, 1), :] * sum_entries(pick, r, width_k, p_ref)).astype(bf16)
            o_ref[(b // share) * nodes + n, :, j * size : (j + 1) * size] = value
        return carry

    lax.fori_loop(0, nodes, rows, 0)


def back_spread_kernel(per, width_k, nodes, pick, near, weight_ref, tiles_ref, *refs):
    parts, outs, p_ref, sums = refs[:nodes], refs[nodes : 2 * nodes], refs[2 * nodes], refs[2 * nodes + 1 :]
    me = lax.axis_index("nodes")
    size = tiles_ref.shape[1]
    width = outs[0].shape[0]
    count = nodes * per
    block = [pl.multiple_of((me ^ i) * per, per) for i in range(nodes)]
    form_products(
        [(block[i], lambda i=i: parts[i][...]) for i in range(nodes)], count, width, tiles_ref, p_ref, True
    )
    for i in range(nodes):
        sums[0][pl.ds(block[i], per)] = parts[i][...].astype(f32).reshape(per, width, size)
    for total in sums[1:]:
        total[...] = jnp.zeros(total.shape, f32)

    def entry_row(r, carry):
        scale = weight_ref[pl.ds(r, 1), :]

        def chunk(c, inner):
            base = c * unroll
            for u in range(unroll):
                g = near[r, base + u]
                sums[u][g] = sums[u][g] + scale * p_ref[pick[r, base + u]]
            return inner

        return lax.fori_loop(0, (near[r, width_k] + (unroll - 1)) // unroll, chunk, carry)

    lax.fori_loop(0, count, entry_row, 0)
    for i in range(nodes):
        for b in range(per):
            r = block[i] + b
            value = ((sums[0][r] + sums[1][r]) + (sums[2][r] + sums[3][r])).astype(bf16)
            outs[i][:, b * size : (b + 1) * size] = value


def last_kernel(per, width_k, pick, weight_ref, v_ref, tiles_ref, o_ref, x_ref, p_ref):
    nodes = o_ref.shape[0]
    count, width, size = x_ref.shape
    share = v_ref.shape[2] // size
    for f in range(per // share):
        for n in range(nodes):
            for j in range(share):
                x_ref[n * per + f * share + j] = v_ref[f * nodes + n, :, j * size : (j + 1) * size]
    group = 256 // width
    lefts = [
        (first, lambda first=first: x_ref[first : first + group].reshape(group * width, size))
        for first in range(0, count, group)
    ]
    form_products(lefts, count, width, tiles_ref, p_ref, False)

    def rows(n, carry):
        for b in range(per):
            r = n * per + b
            acc = sum_entries(pick, r, width_k, p_ref)
            value = x_ref[r].astype(f32) + weight_ref[pl.ds(r, 1), :] * acc
            o_ref[n, :, b * size : (b + 1) * size] = value.astype(bf16)
        return carry

    lax.fori_loop(0, nodes, rows, 0)


def plain_spread(x, ids, tiles, transposed):
    near, tile_ids, degrees = ids
    rows = jnp.arange(x.shape[0])
    kind = "gfi,tij->tgfj" if transposed else "gfj,tij->tgfi"
    products = jnp.einsum(kind, x, tiles, preferred_element_type=f32)
    weight = lax.rsqrt(degrees.astype(f32))

    def step(k, acc):
        g, t = near[:, k], tile_ids[:, k]
        scale = jnp.where(k < degrees, weight, 0.0)[:, None, None]
        if transposed:
            return acc.at[g].add(scale * products[t, rows])
        return acc + scale * products[t, g]

    return lax.fori_loop(0, near.shape[1], step, x.astype(f32)).astype(bf16)


def product_flops(tiles, count, width):
    return 2 * tiles.shape[0] * count * width * tiles.shape[1] * tiles.shape[1]


def product_scratch(tiles, count, width):
    return pltpu.VMEM((tiles.shape[0] * count + 1, width, tiles.shape[1]), f32)


def spread_first(v, tiles, per, width_k, feat_count):
    nodes, rows, size = v.shape
    width = (rows - meta_rows) // per
    count, share = nodes * per, per // feat_count
    if width % 16:
        raw = v[:, rows - meta_rows :, :].astype(jnp.int32)
        links = raw[:, :per].reshape(count, size)
        ids = (links[:, :width_k], raw[:, per:].reshape(count, size)[:, :width_k], links[:, width_k])
        out = plain_spread(v[:, : rows - meta_rows].reshape(count, width, size), ids, tiles, False)
        out = out.reshape(nodes, feat_count, share, width, size).transpose(1, 0, 3, 2, 4)
        return out.reshape(feat_count * nodes, width, share * size), ids
    return_ids = ((3, count, size), jnp.int32)
    out, ids, weight = call(
        functools.partial(first_kernel, per, width_k),
        [((feat_count * nodes, width, share * size), bf16), return_ids, ((count, size), f32)],
        [vmem, vmem],
        (v, tiles),
        [
            pltpu.SMEM((count, size), jnp.int32),
            product_scratch(tiles, count, width),
            pltpu.SemaphoreType.DMA,
        ],
        product_flops(tiles, count, width),
    )
    return out, (ids[0], ids[1], ids[2], weight)


def spread_back(parts, ids, tiles, per, width_k):
    nodes, size = len(parts), tiles.shape[1]
    width, count = parts[0].shape[0] // per, len(parts) * per
    if width % 16:
        me = lax.axis_index("nodes")
        order = me ^ jnp.arange(nodes)
        x = jnp.stack(parts)[order].reshape(count, width, size)
        out = plain_spread(x, ids, tiles, True)
        out = out.reshape(nodes, per, width, size).transpose(0, 2, 1, 3).reshape(nodes, width, per * size)[order]
        return [out[i] for i in range(nodes)]
    _, pick_back, near, weight = ids
    return call(
        functools.partial(back_spread_kernel, per, width_k, nodes),
        [((width, per * size), bf16)] * nodes,
        [smem, smem, vmem, vmem] + [vmem] * nodes,
        (pick_back, near, weight, tiles, *parts),
        [product_scratch(tiles, count, width)] + [pltpu.VMEM((count, width, size), f32)] * unroll,
        product_flops(tiles, count, width),
    )


def spread_last(v, ids, tiles, per, width_k, nodes):
    size = tiles.shape[1]
    every, width, held = v.shape
    feat_count, share, count = every // nodes, held // size, nodes * per
    if width % 16:
        x = v.reshape(feat_count, nodes, width, share, size).transpose(1, 0, 3, 2, 4).reshape(count, width, size)
        out = plain_spread(x, ids, tiles, False)
        return out.reshape(nodes, per, width, size).transpose(0, 2, 1, 3).reshape(nodes, width, per * size)
    pick, _, _, weight = ids
    return call(
        functools.partial(last_kernel, per, width_k),
        [((nodes, width, per * size), bf16)],
        [smem, vmem, vmem, vmem],
        (pick, weight, v, tiles),
        [pltpu.VMEM((count, width, size), bf16), product_scratch(tiles, count, width)],
        product_flops(tiles, count, width),
    )[0]


def swap(values, axis, mask):
    return lax.ppermute(values, axis, [(i, i ^ mask) for i in range(lax.axis_size(axis))])


def gather_parts(values, axis):
    parts, offsets = [values], [0]
    bit = lax.axis_size(axis) // 2
    while bit:
        parts = parts + [swap(v, axis, bit) for v in parts]
        offsets = offsets + [o ^ bit for o in offsets]
        bit //= 2
    return parts, offsets


def join_kernel(nodes, offsets, *refs):
    parts, outs = refs[:nodes], refs[nodes:]
    me_n, me_f = lax.axis_index("nodes"), lax.axis_index("feat")
    width = parts[0].shape[0]
    held = outs[0].shape[1]
    for o, o_ref in zip(offsets, outs):
        cols = pl.ds(pl.multiple_of((me_f ^ o) * held, held), held)
        for i, part in enumerate(parts):
            o_ref[pl.ds(pl.multiple_of((me_n ^ i) * width, width), width), :] = part[:, cols]


def join_parts(parts, offsets, held):
    nodes, width = len(parts), parts[0].shape[0]
    if width % 16:
        whole = jnp.stack(parts)[lax.axis_index("nodes") ^ jnp.arange(nodes)].reshape(nodes * width, -1)
        first = lax.axis_index("feat")
        return [lax.dynamic_slice_in_dim(whole, (first ^ o) * held, held, 1) for o in offsets]
    return call(
        functools.partial(join_kernel, nodes, offsets),
        [((nodes * width, held), bf16)] * len(offsets),
        [vmem] * nodes,
        parts,
    )


def project_kernel(offsets, agg_ref, *refs):
    count = len(offsets)
    weights, (pre_ref, hidden_ref, y_ref) = refs[:count], refs[count:]
    me = lax.axis_index("feat")
    wide = weights[0].shape[1]
    agg = agg_ref[...]
    place = [pl.ds(pl.multiple_of((me ^ o) * wide, wide), wide) for o in offsets]
    for at, w_ref in zip(place, weights):
        pre = jnp.dot(w_ref[0], agg, preferred_element_type=f32)
        pre_ref[at, :] = pre
        hidden_ref[at, :] = (pre * jax.nn.sigmoid(pre)).astype(bf16)
    hidden = hidden_ref[...]
    for at, w_ref in zip(place, weights):
        y_ref[at, :] = jnp.dot(w_ref[1], hidden, preferred_element_type=f32).astype(bf16)


def back_kernel(offsets, *refs):
    count = len(offsets)
    pre_ref, weights, backs, outs = refs[0], refs[1 : 1 + count], refs[1 + count : 1 + 2 * count], refs[1 + 2 * count :]
    me = lax.axis_index("feat")
    wide = weights[0].shape[1]
    for o, o_ref in zip(offsets, outs):
        at = pl.ds(pl.multiple_of((me ^ o) * wide, wide), wide)
        total = None
        for w_ref, b_ref in zip(weights, backs):
            term = lax.dot_general(
                w_ref[1, :, at], b_ref[...], (((0,), (0,)), ((), ())), preferred_element_type=f32
            )
            total = term if total is None else total + term
        pre = pre_ref[at, :]
        sigma = jax.nn.sigmoid(pre)
        o_ref[...] = (total * sigma * (1.0 + pre * (1.0 - sigma))).astype(bf16)


def grad_kernel(count, *refs):
    lefts, rights, give_ref, keep_ref = refs[:count], refs[count : 2 * count], refs[2 * count], refs[2 * count + 1]
    side = lax.axis_index("nodes") % 2
    half, tall, _ = keep_ref.shape
    for h in range(half):
        for mine in (False, True):
            row = (2 * h + (side if mine else 1 - side)) * tall
            at = pl.ds(pl.multiple_of(row, tall), tall)
            total = None
            for left, right in zip(lefts, rights):
                term = nt_dot(left[at, :], right[...])
                total = term if total is None else total + term
            if mine:
                keep_ref[h] = total
            else:
                give_ref[h] = total.astype(bf16)


def split_kernel(keep_ref, came_ref, mine_ref, *outs):
    me = lax.axis_index("nodes") // 2
    mine_ref[...] = keep_ref[me] + came_ref[me].astype(f32)
    for i, o_ref in enumerate(outs):
        to = me ^ (i + 1)
        o_ref[...] = (keep_ref[to] + came_ref[to].astype(f32)).astype(bf16)


def weight_grad(lefts, rights):
    nodes = lax.axis_size("nodes")
    count = len(lefts)
    half, tall, wide = nodes // 2, lefts[0].shape[0] // nodes, rights[0].shape[0]
    flops = 2 * count * lefts[0].shape[0] * lefts[0].shape[1] * wide
    give, keep = call(
        functools.partial(grad_kernel, count),
        [((half, tall, wide), bf16), ((half, tall, wide), f32)],
        [vmem] * (2 * count),
        (*lefts, *rights),
        flops=flops,
    )
    came = swap(give, "nodes", 1)
    mine, *rest = call(
        split_kernel,
        [((tall, wide), f32)] + [((tall, wide), bf16)] * (half - 1),
        [vmem] * 2,
        (keep, came),
    )
    for i, part in enumerate(rest):
        mine = mine + swap(part, "nodes", 2 * (i + 1)).astype(f32)
    return mine


def on_device(
    features, ghosts, slots, tile_ids, degrees, tile_table, weight_one, weight_two, cotangent
):
    nodes, feat_count = lax.axis_size("nodes"), lax.axis_size("feat")
    every = ("feat", "nodes")
    per, width_k = slots.shape
    size = tile_table.shape[1]
    rows, wide = features.shape
    held = rows // feat_count
    hidden_width = wide * feat_count
    exchange = lambda v, axes: lax.all_to_all(v, axes, split_axis=0, concat_axis=0, tiled=True)

    sent = pack(features, ghosts, slots, tile_ids, degrees, nodes, size)
    came = exchange(sent, "nodes")
    weights, offsets = gather_parts(jnp.stack([weight_one.T, weight_two.T]), "feat")
    around = lambda parts: [parts[0]] + [swap(p, "nodes", i) for i, p in enumerate(parts) if i]
    turn = lambda blocks: [blocks[0]] + [swap(b, "feat", o) for b, o in zip(blocks[1:], offsets[1:])]
    cot_parts = around(pack_parts(cotangent, nodes, size))

    spread, ids = spread_first(came, tile_table, per, width_k, feat_count)
    agg = exchange(spread, every).reshape(hidden_width, held)
    rights = join_parts(around(spread_back(cot_parts, ids, tile_table, per, width_k)), offsets, held)
    backs = turn(rights)

    parts = len(offsets)
    pre, hidden, wide_out = call(
        functools.partial(project_kernel, offsets),
        [((hidden_width, held), f32)] + [((hidden_width, held), bf16)] * 2,
        [vmem] * (1 + parts),
        (agg, *weights),
        flops=4 * hidden_width * hidden_width * held,
    )
    out_t = exchange(wide_out.reshape(feat_count * nodes, wide // nodes, held), every)

    hidden_parts, _ = gather_parts(hidden, "feat")
    grad_two = weight_grad(hidden_parts, rights)
    agg_parts, _ = gather_parts(agg, "feat")
    back_pre = call(
        functools.partial(back_kernel, offsets),
        [((wide, held), bf16)] * parts,
        [vmem] * (1 + 2 * parts),
        (pre, *weights, *backs),
        flops=2 * hidden_width * hidden_width * held,
    )
    grad_one = weight_grad(agg_parts, turn(back_pre))

    out_n = exchange(spread_last(out_t, ids, tile_table, per, width_k, nodes), "nodes")
    output = out_n.reshape(wide, rows).T
    return (output, grad_one, grad_two)


def solution(mesh):
    return jax.shard_map(
        on_device,
        mesh=mesh,
        in_specs=(
            P("nodes", "feat"),
            P("nodes", None),
            P("nodes", None),
            P("nodes", None),
            P("nodes"),
            P(),
            P(None, "feat"),
            P(None, "feat"),
            P("nodes", "feat"),
        ),
        out_specs=(P("nodes", "feat"), P("nodes", "feat"), P("nodes", "feat")),
        check_vma=False,
    )
```

time: 197 us -> 194 us (0.985)
  waiting for transfers between devices: 90.7 us -> 63.6 us
  starting transfers between devices: 40.4 us -> 65.5 us
  local copies, waits for them, and re-layouts: 24.5 us -> 11 us
  Pallas kernels: 38.3 us -> 50.4 us
    all_to_all x4, waiting for transfers between devices: 47.7 us -> 10.2 us  [on_device(): lax.all_to_all(v, axes, split_axis=0, concat_axis=0, tiled=True)]
    ppermute x23 -> x37, starting transfers between devices: 19.9 us -> 47.2 us  [swap(): lax.ppermute(values, axis, [(i, i ^ mask) for i in range(lax.axis_size(ax...]
    unnamed x71 -> x83, local copies, waits for them, and re-layouts: 22.5 us -> 9.34 us
    pallas_call x9 -> x12, Pallas kernels: 38.3 us -> 50.4 us  [call(): pl.pallas_call(body, out_shape=[jax.ShapeDtypeStruct(s, d) for s, d in ou...]
    ppermute x23 -> x37, waiting for transfers between devices: 43 us -> 53.3 us  [swap(): lax.ppermute(values, axis, [(i, i ^ mask) for i in range(lax.axis_size(ax...]
    all_to_all x4, starting transfers between devices: 20.5 us -> 18.3 us  [on_device(): lax.all_to_all(v, axes, split_axis=0, concat_axis=0, tiled=True)]
  transfers between devices with their start and end apart: 27 -> 41, of which waited for: 12 -> 17; matrix products, arithmetic and copies ran while one was open for 1% -> 1% of each run, Pallas kernels for 17% -> 26%
where the time goes in v3:
time: 194 us; the launch traced here: 193 us
  starting transfers between devices  65.5 us (34%)
  waiting for transfers between devices  63.6 us (33%)
  Pallas kernels  50.4 us (26%)
  local copies, waits for them, and re-layouts  11 us (6%)
    ppermute x37, waiting for transfers between devices, swap(): lax.ppermute(values, axis, [(i, i ^ mask) for i in range(lax.axis_size(ax...  53.3 us
    pallas_call x12, Pallas kernels, call(): pl.pallas_call(body, out_shape=[jax.ShapeDtypeStruct(s, d) for s, d in ou...  50.4 us
    ppermute x37, starting transfers between devices, swap(): lax.ppermute(values, axis, [(i, i ^ mask) for i in range(lax.axis_size(ax...  47.2 us
    all_to_all x4, starting transfers between devices, on_device(): lax.all_to_all(v, axes, split_axis=0, concat_axis=0, tiled=True)  18.3 us
    all_to_all x4, waiting for transfers between devices, on_device(): lax.all_to_all(v, axes, split_axis=0, concat_axis=0, tiled=True)  10.2 us
    unnamed x83, local copies, waits for them, and re-layouts  9.34 us
  transfers between devices with their start and end apart: 41, of which 17 were waited for; matrix products, arithmetic and copies ran while one was open for 1% of the time, Pallas kernels for 26%

profile of v3, /device:TPU:0, one launch (start us, length us, event | category | flops | bytes accessed | tf_op | source)
XLA Modules:
  0.0 192.8 jit_solution(76911537790443912)
XLA Ops:
  2.3 3.0 %collective-permute-start = (bf16[2,256,1024]{2,1,0:T(8,128)(2,1)S(1)}, bf16[2,256,1024]{2,1,0:T(8,128)(2,1)S(1)}, u32[]{:S(2)}, u32[]{:S(2)}) collective-permute-start(bf16[2,256,1024]{2,1,0:T(8,128)(2,1)S(1)} %pad_maximum_fusion.refs_0_.refs_1_), channel_id=1, source_target_pairs={{0,2},{1,3},{2,0},{3,1},{4,6},{5,7},{6,4},{7,5},{8,10},{9,11},{10,... | collective-permute-start | bytes 3145736 | tf_op jit(solution)/shard_map/ppermute | solution.py:334
  8.1 5.8 %all-to-all-start = ((bf16[8,272,128]{2,1,0:T(8,128)(2,1)}), bf16[8,272,128]{2,1,0:T(8,128)(2,1)S(1)}, u32[]{:S(2)}, u32[]{:S(2)}) async-start(bf16[8,272,128]{2,1,0:T(8,128)(2,1)} %shard_map.112), calls=%async_computation | async-start | bytes 1114112 | tf_op jit(solution)/shard_map/all_to_all | solution.py:466
  14.0 14.5 %collective-permute-done.refs_1_.refs_2_ = bf16[2,256,1024]{2,1,0:T(8,128)(2,1)S(1)} collective-permute-done((bf16[2,256,1024]{2,1,0:T(8,128)(2,1)S(1)}, bf16[2,256,1024]{2,1,0:T(8,128)(2,1)S(1)}, u32[]{:S(2)}, u32[]{:S(2)}) %collective-permute-start) | collective-permute-done | bytes 1048608 | tf_op jit(solution)/shard_map/ppermute | solution.py:334
  29.7 6.7 %shard_map.113 = (bf16[32,32,256]{2,1,0:T(8,128)(2,1)}, s32[3,64,128]{2,1,0:T(8,128)}, f32[64,128]{1,0:T(8,128)}) custom-call(bf16[8,272,128]{2,1,0:T(8,128)(2,1)} %copy-done.4, bf16[16,128,128]{2,1,0:T(8,128)(2,1)} %tiles_ref.7), custom_call_target="tpu_custom_call" | custom-call | flops 1073741824 | bytes 4194304 | tf_op jit(solution)/shard_map/pallas_call | solution.py:23
  36.4 5.8 %all-to-all-start.1 = ((bf16[32,32,256]{2,1,0:T(8,128)(2,1)}), bf16[32,32,256]{2,1,0:T(8,128)(2,1)S(1)}, u32[]{:S(2)}, u32[]{:S(2)}) async-start(bf16[32,32,256]{2,1,0:T(8,128)(2,1)} %get-tuple-element.47), calls=%async_computation.1 | async-start | bytes 1048576 | tf_op jit(solution)/shard_map/all_to_all | solution.py:466
  44.3 3.6 %collective-permute-start.10 = (bf16[256,128]{1,0:T(8,128)(2,1)}, bf16[256,128]{1,0:T(8,128)(2,1)S(1)}, u32[]{:S(2)}, u32[]{:S(2)}) collective-permute-start(bf16[256,128]{1,0:T(8,128)(2,1)} %get-tuple-element.55), channel_id=1, source_target_pairs={{0,20},{4,16},{8,28},{12,24},{16,4},{20,0},{24,12},{28,8},{1,21},{... | collective-permute-start | bytes 196616 | tf_op jit(solution)/shard_map/ppermute | solution.py:334
  53.1 9.8 %all-to-all-done.1 = bf16[32,32,256]{2,1,0:T(8,128)(2,1)S(1)} async-done(((bf16[32,32,256]{2,1,0:T(8,128)(2,1)}), bf16[32,32,256]{2,1,0:T(8,128)(2,1)S(1)}, u32[]{:S(2)}, u32[]{:S(2)}) %all-to-all-start.1) | async-done | bytes 524320 | tf_op jit(solution)/shard_map/all_to_all | solution.py:466
  63.8 4.7 %shard_map.114 = (f32[1024,256]{1,0:T(8,128)}, bf16[1024,256]{1,0:T(8,128)(2,1)}, bf16[1024,256]{1,0:T(8,128)(2,1)}) custom-call(bf16[1024,256]{1,0:T(8,128)(2,1)} %bitcast.16, bf16[2,256,1024]{2,1,0:T(8,128)(2,1)} %copy-done, bf16[2,256,1024]{2,1,0:T(8,128)(2,1)} %copy-done.3, bf16[2,256,1024]{2,1,0:T(8,128)(2,1)} %collective-permute-done.1.refs_2_.refs_3_, ...), custom_call_target="tpu_custom_call" | custom-call | flops 1073741824 | bytes 4194304 | tf_op jit(solution)/shard_map/pallas_call | solution.py:23
  68.5 2.7 %all-to-all-start.2 = ((bf16[32,32,256]{2,1,0:T(8,128)(2,1)}), bf16[32,32,256]{2,1,0:T(8,128)(2,1)S(1)}, u32[]{:S(2)}, u32[]{:S(2)}) async-start(bf16[32,32,256]{2,1,0:T(8,128)(2,1)} %bitcast.23), calls=%async_computation.2 | async-start | bytes 1048576 | tf_op jit(solution)/shard_map/all_to_all | solution.py:466
  82.0 3.5 %collective-permute-done.8.refs_3_ = bf16[256,128]{1,0:T(8,128)(2,1)S(1)} collective-permute-done((bf16[256,128]{1,0:T(8,128)(2,1)S(1)}, bf16[256,128]{1,0:T(8,128)(2,1)S(1)}, u32[]{:S(2)}, u32[]{:S(2)}) %collective-permute-start.8) | collective-permute-done | bytes 65568 | tf_op jit(solution)/shard_map/ppermute | solution.py:334
  85.5 3.5 %collective-permute-done.9.refs_4_ = bf16[256,128]{1,0:T(8,128)(2,1)S(1)} collective-permute-done((bf16[256,128]{1,0:T(8,128)(2,1)S(1)}, bf16[256,128]{1,0:T(8,128)(2,1)S(1)}, u32[]{:S(2)}, u32[]{:S(2)}) %collective-permute-start.9) | collective-permute-done | bytes 65568 | tf_op jit(solution)/shard_map/ppermute | solution.py:334
  89.6 10.1 %shard_map.117 = (bf16[32,1024]{1,0:T(8,128)(2,1)}, bf16[32,1024]{1,0:T(8,128)(2,1)}, bf16[32,1024]{1,0:T(8,128)(2,1)}, bf16[32,1024]{1,0:T(8,128)(2,1)}, bf16[3...) custom-call(s32[64,128]{1,0:T(8,128)} %get-tuple-element.88.pick, ...), custom_call_target="tpu_custom_call" | custom-call | flops 1073741824 | bytes 4194304 | tf_op jit(solution)/shard_map/pallas_call | solution.py:23
  105.8 2.7 %collective-permute-start.17 = (bf16[32,1024]{1,0:T(8,128)(2,1)}, bf16[32,1024]{1,0:T(8,128)(2,1)S(1)}, u32[]{:S(2)}, u32[]{:S(2)}) collective-permute-start(bf16[32,1024]{1,0:T(8,128)(2,1)} %get-tuple-element.63), channel_id=1, source_target_pairs={{0,20},{4,16},{8,28},{12,24},{16,4},{20,0},{24,12},{28,8},{1,21},{... | collective-permute-start | bytes 196616 | tf_op jit(solution)/shard_map/ppermute | solution.py:334
  109.5 4.1 %collective-permute-done.16.refs_4_ = bf16[32,1024]{1,0:T(8,128)(2,1)S(1)} collective-permute-done((bf16[32,1024]{1,0:T(8,128)(2,1)}, bf16[32,1024]{1,0:T(8,128)(2,1)S(1)}, u32[]{:S(2)}, u32[]{:S(2)}) %collective-permute-start.16) | collective-permute-done | bytes 65568 | tf_op jit(solution)/shard_map/ppermute | solution.py:334
  116.1 4.6 %collective-permute-done.19.refs_7_ = bf16[32,1024]{1,0:T(8,128)(2,1)S(1)} collective-permute-done((bf16[32,1024]{1,0:T(8,128)(2,1)}, bf16[32,1024]{1,0:T(8,128)(2,1)S(1)}, u32[]{:S(2)}, u32[]{:S(2)}) %collective-permute-start.19) | collective-permute-done | bytes 65568 | tf_op jit(solution)/shard_map/ppermute | solution.py:334
  125.4 3.6 %collective-permute-done.20.refs_6_ = bf16[256,256]{1,0:T(8,128)(2,1)S(1)} collective-permute-done((bf16[256,256]{1,0:T(8,128)(2,1)}, bf16[256,256]{1,0:T(8,128)(2,1)S(1)}, u32[]{:S(2)}, u32[]{:S(2)}) %collective-permute-start.20) | collective-permute-done | bytes 131104 | tf_op jit(solution)/shard_map/ppermute | solution.py:334
  131.3 4.3 %shard_map.119 = (bf16[256,256]{1,0:T(8,128)(2,1)}, bf16[256,256]{1,0:T(8,128)(2,1)}, bf16[256,256]{1,0:T(8,128)(2,1)}, bf16[256,256]{1,0:T(8,128)(2,1)}) custom-call(f32[1024,256]{1,0:T(8,128)} %get-tuple-element.49.refs_0_, bf16[2,256,1024]{2,1,0:T(8,128)(2,1)} %copy-done, bf16[2,256,1024]{2,1,0:T(8,128)(2,1)} %copy-done.3, ...), custom_call_target="tpu_custom_call" | custom-call | flops 536870912 | bytes 4194304 | tf_op jit(solution)/shard_map/pallas_call | solution.py:23
  137.4 4.3 %collective-permute-done.23.refs_5_ = bf16[256,256]{1,0:T(8,128)(2,1)S(1)} collective-permute-done((bf16[256,256]{1,0:T(8,128)(2,1)}, bf16[256,256]{1,0:T(8,128)(2,1)S(1)}, u32[]{:S(2)}, u32[]{:S(2)}) %collective-permute-start.23) | collective-permute-done | bytes 131104 | tf_op jit(solution)/shard_map/ppermute | solution.py:334
  145.3 6.8 %shard_map.115 = bf16[8,32,1024]{2,1,0:T(8,128)(2,1)} custom-call(s32[64,128]{1,0:T(8,128)} %get-tuple-element.89.pick, f32[64,128]{1,0:T(8,128)} %get-tuple-element.46.weight_ref, bf16[32,32,256]{2,1,0:T(8,128)(2,1)} %copy-done.10, bf16[16,128,128]{2,1,0:T(8,128)(2,1)} %tiles_ref.7), custom_call_target="tpu_custom_call" | custom-call | flops 1073741824 | bytes 4194304 | tf_op jit(solution)/shard_map/pallas_call | solution.py:23
  152.1 3.9 %all-to-all-start.3 = ((bf16[8,32,1024]{2,1,0:T(8,128)(2,1)}), bf16[8,32,1024]{2,1,0:T(8,128)(2,1)S(1)}, u32[]{:S(2)}, u32[]{:S(2)}) async-start(bf16[8,32,1024]{2,1,0:T(8,128)(2,1)} %shard_map.115), calls=%async_computation.3 | async-start | bytes 1048576 | tf_op jit(solution)/shard_map/all_to_all | solution.py:466
  156.6 4.0 %shard_map.120 = (bf16[4,128,256]{2,1,0:T(8,128)(2,1)}, f32[4,128,256]{2,1,0:T(8,128)}) custom-call(bf16[1024,256]{1,0:T(8,128)(2,1)} %bitcast.17, bf16[1024,256]{1,0:T(8,128)(2,1)} %copy-done.7, bf16[1024,256]{1,0:T(8,128)(2,1)} %collective-permute-done.4.refs_2_, bf16[1024,256]{1,0:T(8,128)(2,1)} %collective-permute-done.5.refs_3_, ...), custom_call_target="tpu_custom_call" | custom-call | flops 536870912 | bytes 4194304 | tf_op jit(solution)/shard_map/pallas_call | solution.py:23
  163.5 4.0 %shard_map.122 = (bf16[4,128,256]{2,1,0:T(8,128)(2,1)}, f32[4,128,256]{2,1,0:T(8,128)}) custom-call(bf16[1024,256]{1,0:T(8,128)(2,1)} %get-tuple-element.80.refs_0_, bf16[1024,256]{1,0:T(8,128)(2,1)} %copy-done.6, bf16[1024,256]{1,0:T(8,128)(2,1)} %copy-done.8, bf16[1024,256]{1,0:T(8,128)(2,1)} %collective-permute-done.32.refs_3_, ...), custom_call_target="tpu_custom_call" | custom-call | flops 536870912 | bytes 4194304 | tf_op jit(solution)/shard_map/pallas_call | solution.py:23
  167.5 4.1 %collective-permute-done.26.came_ref = bf16[4,128,256]{2,1,0:T(8,128)(2,1)S(1)} collective-permute-done((bf16[4,128,256]{2,1,0:T(8,128)(2,1)}, bf16[4,128,256]{2,1,0:T(8,128)(2,1)S(1)}, u32[]{:S(2)}, u32[]{:S(2)}) %collective-permute-start.26) | collective-permute-done | bytes 262176 | tf_op jit(solution)/shard_map/ppermute | solution.py:334
  186.7 2.6 %collective-permute-done.35 = bf16[128,256]{1,0:T(8,128)(2,1)S(1)} collective-permute-done((bf16[128,256]{1,0:T(8,128)(2,1)}, bf16[128,256]{1,0:T(8,128)(2,1)S(1)}, u32[]{:S(2)}, u32[]{:S(2)}) %collective-permute-start.35) | collective-permute-done | bytes 65568 | tf_op jit(solution)/shard_map/ppermute | solution.py:334
  (158 shorter events, 69.1 us)
Async XLA Ops:
  2.3 26.2 %collective-permute-start = (bf16[2,256,1024]{2,1,0:T(8,128)(2,1)S(1)}, bf16[2,256,1024]{2,1,0:T(8,128)(2,1)S(1)}, u32[]{:S(2)}, u32[]{:S(2)}) collective-permute-start(bf16[2,256,1024]{2,1,0:T(8,128)(2,1)S(1)} %pad_maximum_fusion.refs_0_.refs_1_), channel_id=1, source_target_pairs={{0,2},{1,3},{2,0},{3,1},{4,6},{5,7},{6,4},{7,5},{8,10},{9,11},{10,... | collective-permute-start | bytes 3145736 | tf_op jit(solution)/shard_map/ppermute | solution.py:334
  8.1 20.8 %all-to-all-start = ((bf16[8,272,128]{2,1,0:T(8,128)(2,1)}), bf16[8,272,128]{2,1,0:T(8,128)(2,1)S(1)}, u32[]{:S(2)}, u32[]{:S(2)}) async-start(bf16[8,272,128]{2,1,0:T(8,128)(2,1)} %shard_map.112), calls=%async_computation | async-start | bytes 1114112 | tf_op jit(solution)/shard_map/all_to_all | solution.py:466
  13.9 37.8 %collective-permute-start.1 = (bf16[2,256,1024]{2,1,0:T(8,128)(2,1)S(1)}, bf16[2,256,1024]{2,1,0:T(8,128)(2,1)}, u32[]{:S(2)}, u32[]{:S(2)}) collective-permute-start(bf16[2,256,1024]{2,1,0:T(8,128)(2,1)S(1)} %pad_maximum_fusion.refs_0_.refs_1_), channel_id=1, source_target_pairs={{0,1},{1,0},{2,3},{3,2},{4,5},{5,4},{6,7},{7,6},{8,9},{9,8},{10,11... | collective-permute-start | bytes 3145736 | tf_op jit(solution)/shard_map/ppermute | solution.py:334
  28.5 34.5 %collective-permute-start.2 = (bf16[2,256,1024]{2,1,0:T(8,128)(2,1)S(1)}, bf16[2,256,1024]{2,1,0:T(8,128)(2,1)}, u32[]{:S(2)}, u32[]{:S(2)}) collective-permute-start(bf16[2,256,1024]{2,1,0:T(8,128)(2,1)S(1)} %collective-permute-done.refs_1_.refs_2_), channel_id=1, source_target_pairs={{0,1},{1,0},{2,3},{3,2},{4,5},{5,4},{6,7},{7,6},{8,9},{9,8},{10,11... | collective-permute-start | bytes 3145736 | tf_op jit(solution)/shard_map/ppermute | solution.py:334
  36.4 26.6 %all-to-all-start.1 = ((bf16[32,32,256]{2,1,0:T(8,128)(2,1)}), bf16[32,32,256]{2,1,0:T(8,128)(2,1)S(1)}, u32[]{:S(2)}, u32[]{:S(2)}) async-start(bf16[32,32,256]{2,1,0:T(8,128)(2,1)} %get-tuple-element.47), calls=%async_computation.1 | async-start | bytes 1048576 | tf_op jit(solution)/shard_map/all_to_all | solution.py:466
  44.3 28.7 %collective-permute-start.10 = (bf16[256,128]{1,0:T(8,128)(2,1)}, bf16[256,128]{1,0:T(8,128)(2,1)S(1)}, u32[]{:S(2)}, u32[]{:S(2)}) collective-permute-start(bf16[256,128]{1,0:T(8,128)(2,1)} %get-tuple-element.55), channel_id=1, source_target_pairs={{0,20},{4,16},{8,28},{12,24},{16,4},{20,0},{24,12},{28,8},{1,21},{... | collective-permute-start | bytes 196616 | tf_op jit(solution)/shard_map/ppermute | solution.py:334
  47.8 26.6 %collective-permute-start.11 = (bf16[256,128]{1,0:T(8,128)(2,1)}, bf16[256,128]{1,0:T(8,128)(2,1)S(1)}, u32[]{:S(2)}, u32[]{:S(2)}) collective-permute-start(bf16[256,128]{1,0:T(8,128)(2,1)} %get-tuple-element.56), channel_id=1, source_target_pairs={{0,24},{4,28},{8,16},{12,20},{16,8},{20,12},{24,0},{28,4},{1,25},{... | collective-permute-start | bytes 196616 | tf_op jit(solution)/shard_map/ppermute | solution.py:334
  49.3 27.7 %collective-permute-start.12 = (bf16[256,128]{1,0:T(8,128)(2,1)}, bf16[256,128]{1,0:T(8,128)(2,1)S(1)}, u32[]{:S(2)}, u32[]{:S(2)}) collective-permute-start(bf16[256,128]{1,0:T(8,128)(2,1)} %get-tuple-element.57), channel_id=1, source_target_pairs={{0,28},{4,24},{8,20},{12,16},{16,12},{20,8},{24,4},{28,0},{1,29},{... | collective-permute-start | bytes 196616 | tf_op jit(solution)/shard_map/ppermute | solution.py:334
  51.7 26.9 %collective-permute-start.6 = (bf16[256,128]{1,0:T(8,128)(2,1)}, bf16[256,128]{1,0:T(8,128)(2,1)S(1)}, u32[]{:S(2)}, u32[]{:S(2)}) collective-permute-start(bf16[256,128]{1,0:T(8,128)(2,1)} %get-tuple-element.51), channel_id=1, source_target_pairs={{0,4},{4,0},{8,12},{12,8},{16,20},{20,16},{24,28},{28,24},{1,5},{5... | collective-permute-start | bytes 196616 | tf_op jit(solution)/shard_map/ppermute | solution.py:334
  68.5 76.0 %all-to-all-start.2 = ((bf16[32,32,256]{2,1,0:T(8,128)(2,1)}), bf16[32,32,256]{2,1,0:T(8,128)(2,1)S(1)}, u32[]{:S(2)}, u32[]{:S(2)}) async-start(bf16[32,32,256]{2,1,0:T(8,128)(2,1)} %bitcast.23), calls=%async_computation.2 | async-start | bytes 1048576 | tf_op jit(solution)/shard_map/all_to_all | solution.py:466
  71.2 10.8 %collective-permute-start.7 = (bf16[256,128]{1,0:T(8,128)(2,1)S(1)}, bf16[256,128]{1,0:T(8,128)(2,1)S(1)}, u32[]{:S(2)}, u32[]{:S(2)}) collective-permute-start(bf16[256,128]{1,0:T(8,128)(2,1)S(1)} %copy-done.36), channel_id=1, source_target_pairs={{0,8},{4,12},{8,0},{12,4},{16,24},{20,28},{24,16},{28,20},{1,9},{5... | collective-permute-start | bytes 196616 | tf_op jit(solution)/shard_map/ppermute | solution.py:334
  73.0 12.6 %collective-permute-start.8 = (bf16[256,128]{1,0:T(8,128)(2,1)S(1)}, bf16[256,128]{1,0:T(8,128)(2,1)S(1)}, u32[]{:S(2)}, u32[]{:S(2)}) collective-permute-start(bf16[256,128]{1,0:T(8,128)(2,1)S(1)} %copy-done.35), channel_id=1, source_target_pairs={{0,12},{4,8},{8,4},{12,0},{16,28},{20,24},{24,20},{28,16},{1,13},{... | collective-permute-start | bytes 196616 | tf_op jit(solution)/shard_map/ppermute | solution.py:334
  74.5 14.5 %collective-permute-start.9 = (bf16[256,128]{1,0:T(8,128)(2,1)S(1)}, bf16[256,128]{1,0:T(8,128)(2,1)S(1)}, u32[]{:S(2)}, u32[]{:S(2)}) collective-permute-start(bf16[256,128]{1,0:T(8,128)(2,1)S(1)} %copy-done.33), channel_id=1, source_target_pairs={{0,16},{4,20},{8,24},{12,28},{16,0},{20,4},{24,8},{28,12},{1,17},{... | collective-permute-start | bytes 196616 | tf_op jit(solution)/shard_map/ppermute | solution.py:334
  77.0 51.9 %collective-permute-start.3 = (bf16[1024,256]{1,0:T(8,128)(2,1)S(1)}, bf16[1024,256]{1,0:T(8,128)(2,1)S(1)}, u32[]{:S(2)}, u32[]{:S(2)}) collective-permute-start(bf16[1024,256]{1,0:T(8,128)(2,1)S(1)} %bitcast.18), channel_id=1, source_target_pairs={{0,2},{1,3},{2,0},{3,1},{4,6},{5,7},{6,4},{7,5},{8,10},{9,11},{10,... | collective-permute-start | bytes 1572872 | tf_op jit(solution)/shard_map/ppermute | solution.py:334
  78.6 51.0 %collective-permute-start.30 = (bf16[1024,256]{1,0:T(8,128)(2,1)S(1)}, bf16[1024,256]{1,0:T(8,128)(2,1)S(1)}, u32[]{:S(2)}, u32[]{:S(2)}) collective-permute-start(bf16[1024,256]{1,0:T(8,128)(2,1)S(1)} %copy-done.5), channel_id=1, source_target_pairs={{0,2},{1,3},{2,0},{3,1},{4,6},{5,7},{6,4},{7,5},{8,10},{9,11},{10,... | collective-permute-start | bytes 1572872 | tf_op jit(solution)/shard_map/ppermute | solution.py:334
  128.9 27.1 %collective-permute-start.4 = (bf16[1024,256]{1,0:T(8,128)(2,1)S(1)}, bf16[1024,256]{1,0:T(8,128)(2,1)}, u32[]{:S(2)}, u32[]{:S(2)}) collective-permute-start(bf16[1024,256]{1,0:T(8,128)(2,1)S(1)} %bitcast.19), channel_id=1, source_target_pairs={{0,1},{1,0},{2,3},{3,2},{4,5},{5,4},{6,7},{7,6},{8,9},{9,8},{10,11... | collective-permute-start | bytes 1572872 | tf_op jit(solution)/shard_map/ppermute | solution.py:334
  129.0 27.1 %collective-permute-start.5 = (bf16[1024,256]{1,0:T(8,128)(2,1)S(1)}, bf16[1024,256]{1,0:T(8,128)(2,1)}, u32[]{:S(2)}, u32[]{:S(2)}) collective-permute-start(bf16[1024,256]{1,0:T(8,128)(2,1)S(1)} %collective-permute-done.3.refs_1_), channel_id=1, source_target_pairs={{0,1},{1,0},{2,3},{3,2},{4,5},{5,4},{6,7},{7,6},{8,9},{9,8},{10,11... | collective-permute-start | bytes 1572872 | tf_op jit(solution)/shard_map/ppermute | solution.py:334
  129.5 33.2 %collective-permute-start.31 = (bf16[1024,256]{1,0:T(8,128)(2,1)S(1)}, bf16[1024,256]{1,0:T(8,128)(2,1)S(1)}, u32[]{:S(2)}, u32[]{:S(2)}) collective-permute-start(bf16[1024,256]{1,0:T(8,128)(2,1)S(1)} %copy-done.5), channel_id=1, source_target_pairs={{0,1},{1,0},{2,3},{3,2},{4,5},{5,4},{6,7},{7,6},{8,9},{9,8},{10,11... | collective-permute-start | bytes 1572872 | tf_op jit(solution)/shard_map/ppermute | solution.py:334
  129.5 33.1 %collective-permute-start.32 = (bf16[1024,256]{1,0:T(8,128)(2,1)S(1)}, bf16[1024,256]{1,0:T(8,128)(2,1)}, u32[]{:S(2)}, u32[]{:S(2)}) collective-permute-start(bf16[1024,256]{1,0:T(8,128)(2,1)S(1)} %collective-permute-done.30.refs_1_), channel_id=1, source_target_pairs={{0,1},{1,0},{2,3},{3,2},{4,5},{5,4},{6,7},{7,6},{8,9},{9,8},{10,11... | collective-permute-start | bytes 1572872 | tf_op jit(solution)/shard_map/ppermute | solution.py:334
  143.2 12.7 %collective-permute-start.25 = (bf16[256,256]{1,0:T(8,128)(2,1)}, bf16[256,256]{1,0:T(8,128)(2,1)S(1)}, u32[]{:S(2)}, u32[]{:S(2)}) collective-permute-start(bf16[256,256]{1,0:T(8,128)(2,1)} %get-tuple-element.73), channel_id=1, source_target_pairs={{0,3},{1,2},{2,1},{3,0},{4,7},{5,6},{6,5},{7,4},{8,11},{9,10},{10,... | collective-permute-start | bytes 393224 | tf_op jit(solution)/shard_map/ppermute | solution.py:334
  152.1 39.7 %all-to-all-start.3 = ((bf16[8,32,1024]{2,1,0:T(8,128)(2,1)}), bf16[8,32,1024]{2,1,0:T(8,128)(2,1)S(1)}, u32[]{:S(2)}, u32[]{:S(2)}) async-start(bf16[8,32,1024]{2,1,0:T(8,128)(2,1)} %shard_map.115), calls=%async_computation.3 | async-start | bytes 1048576 | tf_op jit(solution)/shard_map/all_to_all | solution.py:466
  160.6 11.0 %collective-permute-start.26 = (bf16[4,128,256]{2,1,0:T(8,128)(2,1)}, bf16[4,128,256]{2,1,0:T(8,128)(2,1)S(1)}, u32[]{:S(2)}, u32[]{:S(2)}) collective-permute-start(bf16[4,128,256]{2,1,0:T(8,128)(2,1)} %get-tuple-element.75), channel_id=1, source_target_pairs={{0,4},{4,0},{8,12},{12,8},{16,20},{20,16},{24,28},{28,24},{1,5},{5... | collective-permute-start | bytes 786440 | tf_op jit(solution)/shard_map/ppermute | solution.py:334
  167.5 11.6 %collective-permute-start.33 = (bf16[4,128,256]{2,1,0:T(8,128)(2,1)}, bf16[4,128,256]{2,1,0:T(8,128)(2,1)S(1)}, u32[]{:S(2)}, u32[]{:S(2)}) collective-permute-start(bf16[4,128,256]{2,1,0:T(8,128)(2,1)} %get-tuple-element.82), channel_id=1, source_target_pairs={{0,4},{4,0},{8,12},{12,8},{16,20},{20,16},{24,28},{28,24},{1,5},{5... | collective-permute-start | bytes 786440 | tf_op jit(solution)/shard_map/ppermute | solution.py:334
  174.2 10.7 %collective-permute-start.27 = (bf16[128,256]{1,0:T(8,128)(2,1)}, bf16[128,256]{1,0:T(8,128)(2,1)S(1)}, u32[]{:S(2)}, u32[]{:S(2)}) collective-permute-start(bf16[128,256]{1,0:T(8,128)(2,1)} %get-tuple-element.77), channel_id=1, source_target_pairs={{0,8},{4,12},{8,0},{12,4},{16,24},{20,28},{24,16},{28,20},{1,9},{5... | collective-permute-start | bytes 196616 | tf_op jit(solution)/shard_map/ppermute | solution.py:334
  (57 other events, 345.8 us)

commit v4 on v3

--- a/solution.py
+++ b/solution.py
@@ -19,7 +19,7 @@
     return lax.dot_general(a, b, (((1,), (1,)), ((), ())), preferred_element_type=f32)
 
 
-def call(body, outs, in_specs, args, scratch=(), flops=0, limit=56):
+def call(body, outs, in_specs, args, scratch=(), flops=0, limit=16, moved=0):
     return pl.pallas_call(
         body,
         out_shape=[jax.ShapeDtypeStruct(s, d) for s, d in outs],
@@ -27,8 +27,12 @@
         out_specs=[vmem] * len(outs),
         scratch_shapes=list(scratch),
         compiler_params=pltpu.CompilerParams(vmem_limit_bytes=limit * 1024 * 1024),
-        cost_estimate=pl.CostEstimate(flops=flops, bytes_accessed=4 << 20, transcendentals=0),
+        cost_estimate=pl.CostEstimate(flops=flops, bytes_accessed=moved, transcendentals=0),
     )(*args)
+
+
+def after(values, *earlier):
+    return lax.optimization_barrier((values, earlier))[0]
 
 
 def meta_tile(ghost_at, degree_at, slots, tile_ids, owners, held, size):
@@ -178,10 +182,11 @@
 
 
 def back_spread_kernel(per, width_k, nodes, pick, near, weight_ref, tiles_ref, *refs):
-    parts, outs, p_ref, sums = refs[:nodes], refs[nodes : 2 * nodes], refs[2 * nodes], refs[2 * nodes + 1 :]
+    parts, o_ref, p_ref, sums = refs[:nodes], refs[nodes], refs[nodes + 1], refs[nodes + 2 :]
     me = lax.axis_index("nodes")
     size = tiles_ref.shape[1]
-    width = outs[0].shape[0]
+    width = o_ref.shape[1]
+    share = o_ref.shape[2] // size
     count = nodes * per
     block = [pl.multiple_of((me ^ i) * per, per) for i in range(nodes)]
     form_products(
@@ -205,11 +210,16 @@
         return lax.fori_loop(0, (near[r, width_k] + (unroll - 1)) // unroll, chunk, carry)
 
     lax.fori_loop(0, count, entry_row, 0)
-    for i in range(nodes):
+
+    def rows(n, carry):
         for b in range(per):
-            r = block[i] + b
+            r = n * per + b
+            j = b % share
             value = ((sums[0][r] + sums[1][r]) + (sums[2][r] + sums[3][r])).astype(bf16)
-            outs[i][:, b * size : (b + 1) * size] = value
+            o_ref[(b // share) * nodes + n, :, j * size : (j + 1) * size] = value
+        return carry
+
+    lax.fori_loop(0, nodes, rows, 0)
 
 
 def last_kernel(per, width_k, pick, weight_ref, v_ref, tiles_ref, o_ref, x_ref, p_ref):
@@ -285,30 +295,31 @@
             product_scratch(tiles, count, width),
             pltpu.SemaphoreType.DMA,
         ],
-        product_flops(tiles, count, width),
+        0,
+        28,
     )
     return out, (ids[0], ids[1], ids[2], weight)
 
 
-def spread_back(parts, ids, tiles, per, width_k):
+def spread_back(parts, ids, tiles, per, width_k, feat_count):
     nodes, size = len(parts), tiles.shape[1]
-    width, count = parts[0].shape[0] // per, len(parts) * per
+    width, count, share = parts[0].shape[0] // per, len(parts) * per, per // feat_count
     if width % 16:
-        me = lax.axis_index("nodes")
-        order = me ^ jnp.arange(nodes)
-        x = jnp.stack(parts)[order].reshape(count, width, size)
-        out = plain_spread(x, ids, tiles, True)
-        out = out.reshape(nodes, per, width, size).transpose(0, 2, 1, 3).reshape(nodes, width, per * size)[order]
-        return [out[i] for i in range(nodes)]
+        order = lax.axis_index("nodes") ^ jnp.arange(nodes)
+        out = plain_spread(jnp.stack(parts)[order].reshape(count, width, size), ids, tiles, True)
+        out = out.reshape(nodes, feat_count, share, width, size).transpose(1, 0, 3, 2, 4)
+        return out.reshape(feat_count * nodes, width, share * size)
     _, pick_back, near, weight = ids
     return call(
         functools.partial(back_spread_kernel, per, width_k, nodes),
-        [((width, per * size), bf16)] * nodes,
+        [((feat_count * nodes, width, share * size), bf16)],
         [smem, smem, vmem, vmem] + [vmem] * nodes,
         (pick_back, near, weight, tiles, *parts),
         [product_scratch(tiles, count, width)] + [pltpu.VMEM((count, width, size), f32)] * unroll,
         product_flops(tiles, count, width),
-    )
+        28,
+        4 << 20,
+    )[0]
 
 
 def spread_last(v, ids, tiles, per, width_k, nodes):
@@ -326,7 +337,8 @@
         [smem, vmem, vmem, vmem],
         (pick, weight, v, tiles),
         [pltpu.VMEM((count, width, size), bf16), product_scratch(tiles, count, width)],
-        product_flops(tiles, count, width),
+        0,
+        28,
     )[0]
 
 
@@ -342,31 +354,6 @@
         offsets = offsets + [o ^ bit for o in offsets]
         bit //= 2
     return parts, offsets
-
-
-def join_kernel(nodes, offsets, *refs):
-    parts, outs = refs[:nodes], refs[nodes:]
-    me_n, me_f = lax.axis_index("nodes"), lax.axis_index("feat")
-    width = parts[0].shape[0]
-    held = outs[0].shape[1]
-    for o, o_ref in zip(offsets, outs):
-        cols = pl.ds(pl.multiple_of((me_f ^ o) * held, held), held)
-        for i, part in enumerate(parts):
-            o_ref[pl.ds(pl.multiple_of((me_n ^ i) * width, width), width), :] = part[:, cols]
-
-
-def join_parts(parts, offsets, held):
-    nodes, width = len(parts), parts[0].shape[0]
-    if width % 16:
-        whole = jnp.stack(parts)[lax.axis_index("nodes") ^ jnp.arange(nodes)].reshape(nodes * width, -1)
-        first = lax.axis_index("feat")
-        return [lax.dynamic_slice_in_dim(whole, (first ^ o) * held, held, 1) for o in offsets]
-    return call(
-        functools.partial(join_kernel, nodes, offsets),
-        [((nodes * width, held), bf16)] * len(offsets),
-        [vmem] * nodes,
-        parts,
-    )
 
 
 def project_kernel(offsets, agg_ref, *refs):
@@ -385,68 +372,95 @@
         y_ref[at, :] = jnp.dot(w_ref[1], hidden, preferred_element_type=f32).astype(bf16)
 
 
-def back_kernel(offsets, *refs):
+def halves_of(left_ref, right_ref, give_ref, keep_ref, offsets):
+    me = lax.axis_index("feat")
+    nodes, tall, wide = give_ref.shape[1:]
+    left = left_ref[...]
+    for i, o in enumerate(offsets):
+        for out, to in ((give_ref, me ^ o ^ 1), (keep_ref, me ^ o)):
+            right = right_ref[pl.ds(pl.multiple_of(to * wide, wide), wide), :]
+            out[i] = nt_dot(left, right).reshape(nodes, tall, wide).astype(out.dtype)
+
+
+def product_kernel(offsets, left_ref, right_ref, give_ref, keep_ref):
+    halves_of(left_ref, right_ref, give_ref, keep_ref, offsets)
+
+
+def back_kernel(offsets, evens, pre_ref, back_ref, left_ref, *refs):
     count = len(offsets)
-    pre_ref, weights, backs, outs = refs[0], refs[1 : 1 + count], refs[1 + count : 1 + 2 * count], refs[1 + 2 * count :]
+    weights, (give_ref, keep_ref, out_ref) = refs[:count], refs[count:]
     me = lax.axis_index("feat")
     wide = weights[0].shape[1]
-    for o, o_ref in zip(offsets, outs):
-        at = pl.ds(pl.multiple_of((me ^ o) * wide, wide), wide)
+    place = [pl.ds(pl.multiple_of((me ^ o) * wide, wide), wide) for o in offsets]
+    for at in place:
         total = None
-        for w_ref, b_ref in zip(weights, backs):
+        for w_ref, rows in zip(weights, place):
             term = lax.dot_general(
-                w_ref[1, :, at], b_ref[...], (((0,), (0,)), ((), ())), preferred_element_type=f32
+                w_ref[1, :, at], back_ref[rows, :], (((0,), (0,)), ((), ())), preferred_element_type=f32
             )
             total = term if total is None else total + term
         pre = pre_ref[at, :]
         sigma = jax.nn.sigmoid(pre)
-        o_ref[...] = (total * sigma * (1.0 + pre * (1.0 - sigma))).astype(bf16)
-
-
-def grad_kernel(count, *refs):
-    lefts, rights, give_ref, keep_ref = refs[:count], refs[count : 2 * count], refs[2 * count], refs[2 * count + 1]
+        out_ref[at, :] = (total * sigma * (1.0 + pre * (1.0 - sigma))).astype(bf16)
+    halves_of(left_ref, out_ref, give_ref, keep_ref, evens)
+
+
+def quarter_kernel(keep_ref, came_ref, mine_ref, *outs):
     side = lax.axis_index("nodes") % 2
-    half, tall, _ = keep_ref.shape
-    for h in range(half):
-        for mine in (False, True):
-            row = (2 * h + (side if mine else 1 - side)) * tall
-            at = pl.ds(pl.multiple_of(row, tall), tall)
-            total = None
-            for left, right in zip(lefts, rights):
-                term = nt_dot(left[at, :], right[...])
-                total = term if total is None else total + term
-            if mine:
-                keep_ref[h] = total
-            else:
-                give_ref[h] = total.astype(bf16)
-
-
-def split_kernel(keep_ref, came_ref, mine_ref, *outs):
+    half = mine_ref.shape[0]
+    spots = [(i, b) for i in range(keep_ref.shape[0]) for b in range(2)]
+    for (i, b), o_ref in zip(spots, (mine_ref,) + outs):
+        for h in range(half):
+            row = 2 * h + (side ^ b)
+            o_ref[h] = (keep_ref[i, row] + came_ref[i, row].astype(f32)).astype(o_ref.dtype)
+
+
+def split_kernel(keep_ref, *refs):
+    half = keep_ref.shape[0]
+    came, mine_ref, outs = refs[:-half], refs[-half], refs[len(refs) - half + 1 :]
     me = lax.axis_index("nodes") // 2
-    mine_ref[...] = keep_ref[me] + came_ref[me].astype(f32)
-    for i, o_ref in enumerate(outs):
-        to = me ^ (i + 1)
-        o_ref[...] = (keep_ref[to] + came_ref[to].astype(f32)).astype(bf16)
-
-
-def weight_grad(lefts, rights):
-    nodes = lax.axis_size("nodes")
-    count = len(lefts)
-    half, tall, wide = nodes // 2, lefts[0].shape[0] // nodes, rights[0].shape[0]
-    flops = 2 * count * lefts[0].shape[0] * lefts[0].shape[1] * wide
-    give, keep = call(
-        functools.partial(grad_kernel, count),
-        [((half, tall, wide), bf16), ((half, tall, wide), f32)],
-        [vmem] * (2 * count),
-        (*lefts, *rights),
-        flops=flops,
-    )
-    came = swap(give, "nodes", 1)
+    for i, o_ref in enumerate((mine_ref,) + outs):
+        total = keep_ref[me ^ i]
+        for ref in came:
+            total = total + ref[me ^ i].astype(f32)
+        o_ref[...] = total.astype(o_ref.dtype)
+
+
+def even_offsets():
+    return list(range(0, lax.axis_size("feat"), 2))
+
+
+def grad_shapes(left, right):
+    nodes, count = lax.axis_size("nodes"), lax.axis_size("feat")
+    shape = (count // 2, nodes, left.shape[0] // nodes, right.shape[0] // count)
+    return [(shape, bf16), (shape, f32)]
+
+
+def quarters(swapped, keep):
+    _, nodes, tall, wide = keep.shape
+    evens, feat_count = even_offsets(), lax.axis_size("feat")
+    spots = [(o, b) for o in evens for b in range(2)][1:]
+    shape = (nodes // 2, tall, wide)
+    mine, *rest = call(
+        quarter_kernel,
+        [(shape, f32)] + [(shape, bf16)] * len(spots),
+        [vmem] * 2,
+        (keep, swapped),
+    )
+    ring = range(nodes * feat_count)
+    moved = [
+        lax.ppermute(v, ("nodes", "feat"), [(i, i ^ (b * feat_count + o)) for i in ring]) for v, (o, b) in zip(rest, spots)
+    ]
+    return mine, *moved
+
+
+def grad_sum(keep, *came):
+    half, tall, wide = keep.shape
     mine, *rest = call(
         split_kernel,
         [((tall, wide), f32)] + [((tall, wide), bf16)] * (half - 1),
-        [vmem] * 2,
-        (keep, came),
+        [vmem] * (1 + len(came)),
+        (keep, *came),
     )
     for i, part in enumerate(rest):
         mine = mine + swap(part, "nodes", 2 * (i + 1)).astype(f32)
@@ -467,15 +481,16 @@
 
     sent = pack(features, ghosts, slots, tile_ids, degrees, nodes, size)
     came = exchange(sent, "nodes")
-    weights, offsets = gather_parts(jnp.stack([weight_one.T, weight_two.T]), "feat")
-    around = lambda parts: [parts[0]] + [swap(p, "nodes", i) for i, p in enumerate(parts) if i]
-    turn = lambda blocks: [blocks[0]] + [swap(b, "feat", o) for b, o in zip(blocks[1:], offsets[1:])]
-    cot_parts = around(pack_parts(cotangent, nodes, size))
-
-    spread, ids = spread_first(came, tile_table, per, width_k, feat_count)
-    agg = exchange(spread, every).reshape(hidden_width, held)
-    rights = join_parts(around(spread_back(cot_parts, ids, tile_table, per, width_k)), offsets, held)
-    backs = turn(rights)
+    packed = pack_parts(after(cotangent, sent), nodes, size)
+    first, second = after((weight_one, weight_two), sent)
+    weights, offsets = gather_parts(jnp.stack([first.T, second.T]), "feat")
+
+    spread, ids = spread_first(after(came, packed), tile_table, per, width_k, feat_count)
+    cot_parts = [packed[0]] + [swap(p, "nodes", i) for i, p in enumerate(packed) if i]
+    agg = exchange(after(spread, *cot_parts), every).reshape(hidden_width, held)
+    back = spread_back(cot_parts, ids, tile_table, per, width_k, feat_count)
+    agg = after(agg, back)
+    back = exchange(back, every).reshape(hidden_width, held)
 
     parts = len(offsets)
     pre, hidden, wide_out = call(
@@ -484,22 +499,33 @@
         [vmem] * (1 + parts),
         (agg, *weights),
         flops=4 * hidden_width * hidden_width * held,
-    )
+        moved=4 << 20,
+    )
+    wide_out = after(wide_out, back)
     out_t = exchange(wide_out.reshape(feat_count * nodes, wide // nodes, held), every)
 
-    hidden_parts, _ = gather_parts(hidden, "feat")
-    grad_two = weight_grad(hidden_parts, rights)
-    agg_parts, _ = gather_parts(agg, "feat")
-    back_pre = call(
-        functools.partial(back_kernel, offsets),
-        [((wide, held), bf16)] * parts,
-        [vmem] * (1 + 2 * parts),
-        (pre, *weights, *backs),
-        flops=2 * hidden_width * hidden_width * held,
-    )
-    grad_one = weight_grad(agg_parts, turn(back_pre))
-
-    out_n = exchange(spread_last(out_t, ids, tile_table, per, width_k, nodes), "nodes")
+    evens = even_offsets()
+    flops = 2 * hidden_width * hidden_width * held
+    give_two, keep_two = call(
+        functools.partial(product_kernel, evens), grad_shapes(hidden, back), [vmem] * 2, (hidden, back), flops=flops, moved=4 << 20
+    )
+    swapped_two = swap(give_two, "feat", 1)
+    give_one, keep_one, _ = call(
+        functools.partial(back_kernel, offsets, evens),
+        grad_shapes(agg, back) + [((hidden_width, held), bf16)],
+        [vmem] * (3 + parts),
+        (pre, after(back, swapped_two), agg, *weights),
+        flops=2 * flops,
+        moved=4 << 20,
+    )
+    quarters_two = quarters(swapped_two, keep_two)
+    quarters_one = quarters(swap(give_one, "feat", 1), keep_one)
+
+    out_t = after(out_t, quarters_two[0])
+    last = spread_last(out_t, ids, tile_table, per, width_k, nodes)
+    out_n = exchange(after(last, *quarters_two), "nodes")
+    grad_two = grad_sum(*after(quarters_two, last))
+    grad_one = grad_sum(*after(quarters_one, last))
     output = out_n.reshape(wide, rows).T
     return (output, grad_one, grad_two)
 

time: 194 us -> 149 us (0.77)
  waiting for transfers between devices: 63.6 us -> 31.9 us
  Pallas kernels: 50.4 us -> 37.7 us
  starting transfers between devices: 65.5 us -> 55.6 us
  local copies, waits for them, and re-layouts: 11 us -> 20.5 us
    ppermute x37 -> x18, waiting for transfers between devices: 53.3 us -> 0.82 us  [swap(): lax.ppermute(values, axis, [(i, i ^ mask) for i in range(lax.axis_size(ax...]
    ppermute x37 -> x18, starting transfers between devices: 47.2 us -> 28.3 us  [swap(): lax.ppermute(values, axis, [(i, i ^ mask) for i in range(lax.axis_size(ax...]
    pallas_call x12, Pallas kernels: 50.4 us -> 37.7 us  [call(): pl.pallas_call(body, out_shape=[jax.ShapeDtypeStruct(s, d) for s, d in ou...]
    ppermute x0 -> x6, waiting for transfers between devices: none -> 12.3 us  [quarters(): lax.ppermute(v, ('nodes', 'feat'), [(i, i ^ b * feat_count + o) for i in...]
    unnamed x83 -> x59, local copies, waits for them, and re-layouts: 9.34 us -> 18 us
    all_to_all x4 -> x5, waiting for transfers between devices: 10.2 us -> 18.8 us  [on_device(): lax.all_to_all(v, axes, split_axis=0, concat_axis=0, tiled=True)]
    ppermute x0 -> x6, starting transfers between devices: none -> 7.11 us  [quarters(): lax.ppermute(v, ('nodes', 'feat'), [(i, i ^ b * feat_count + o) for i in...]
    all_to_all x4 -> x5, starting transfers between devices: 18.3 us -> 20.2 us  [on_device(): lax.all_to_all(v, axes, split_axis=0, concat_axis=0, tiled=True)]
  transfers between devices with their start and end apart: 41 -> 29, of which waited for: 17 -> 8; matrix products, arithmetic and copies ran while one was open for 1% -> 2% of each run, Pallas kernels for 26% -> 23%
where the time goes in v4:
time: 149 us; the launch traced here: 148 us
  starting transfers between devices  55.6 us (37%)
  Pallas kernels  37.7 us (25%)
  waiting for transfers between devices  31.9 us (21%)
  local copies, waits for them, and re-layouts  20.5 us (14%)
    pallas_call x12, Pallas kernels, call(): pl.pallas_call(body, out_shape=[jax.ShapeDtypeStruct(s, d) for s, d in ou...  37.7 us
    ppermute x18, starting transfers between devices, swap(): lax.ppermute(values, axis, [(i, i ^ mask) for i in range(lax.axis_size(ax...  28.3 us
    all_to_all x5, starting transfers between devices, on_device(): lax.all_to_all(v, axes, split_axis=0, concat_axis=0, tiled=True)  20.2 us
    all_to_all x5, waiting for transfers between devices, on_device(): lax.all_to_all(v, axes, split_axis=0, concat_axis=0, tiled=True)  18.8 us
    unnamed x59, local copies, waits for them, and re-layouts  18 us
    ppermute x6, waiting for transfers between devices, quarters(): lax.ppermute(v, ('nodes', 'feat'), [(i, i ^ b * feat_count + o) for i in...  12.3 us
    ppermute x6, starting transfers between devices, quarters(): lax.ppermute(v, ('nodes', 'feat'), [(i, i ^ b * feat_count + o) for i in...  7.11 us
  transfers between devices with their start and end apart: 29, of which 8 were waited for; matrix products, arithmetic and copies ran while one was open for 2% of the time, Pallas kernels for 23%

profile of v4, /device:TPU:0, one launch (start us, length us, event | category | flops | bytes accessed | tf_op | source)
XLA Modules:
  0.0 148.0 jit_solution(11458440563094253062)
XLA Ops:
  6.1 7.3 %all-to-all-start = ((bf16[8,272,128]{2,1,0:T(8,128)(2,1)}), bf16[8,272,128]{2,1,0:T(8,128)(2,1)S(1)}, u32[]{:S(2)}, u32[]{:S(2)}) async-start(bf16[8,272,128]{2,1,0:T(8,128)(2,1)} %shard_map.112), calls=%async_computation | async-start | bytes 1114112 | tf_op jit(solution)/shard_map/all_to_all | solution.py:480
  20.9 2.9 %collective-permute-start.3 = (bf16[256,128]{1,0:T(8,128)(2,1)}, bf16[256,128]{1,0:T(8,128)(2,1)}, u32[]{:S(2)}, u32[]{:S(2)}) collective-permute-start(bf16[256,128]{1,0:T(8,128)(2,1)} %get-tuple-element.60), channel_id=1, source_target_pairs={{0,16},{4,20},{8,24},{12,28},{16,0},{20,4},{24,8},{28,12},{1,17},{... | collective-permute-start | bytes 196616 | tf_op jit(solution)/shard_map/ppermute | solution.py:346
  23.9 2.3 %collective-permute-start.4 = (bf16[256,128]{1,0:T(8,128)(2,1)}, bf16[256,128]{1,0:T(8,128)(2,1)}, u32[]{:S(2)}, u32[]{:S(2)}) collective-permute-start(bf16[256,128]{1,0:T(8,128)(2,1)} %get-tuple-element.61), channel_id=1, source_target_pairs={{0,20},{4,16},{8,28},{12,24},{16,4},{20,0},{24,12},{28,8},{1,21},{... | collective-permute-start | bytes 196616 | tf_op jit(solution)/shard_map/ppermute | solution.py:346
  26.1 2.8 %collective-permute-start.5 = (bf16[256,128]{1,0:T(8,128)(2,1)}, bf16[256,128]{1,0:T(8,128)(2,1)}, u32[]{:S(2)}, u32[]{:S(2)}) collective-permute-start(bf16[256,128]{1,0:T(8,128)(2,1)} %get-tuple-element.62), channel_id=1, source_target_pairs={{0,24},{4,28},{8,16},{12,20},{16,8},{20,12},{24,0},{28,4},{1,25},{... | collective-permute-start | bytes 196616 | tf_op jit(solution)/shard_map/ppermute | solution.py:346
  29.6 2.3 %collective-permute-start.6 = (bf16[256,128]{1,0:T(8,128)(2,1)}, bf16[256,128]{1,0:T(8,128)(2,1)}, u32[]{:S(2)}, u32[]{:S(2)}) collective-permute-start(bf16[256,128]{1,0:T(8,128)(2,1)} %get-tuple-element.63), channel_id=1, source_target_pairs={{0,28},{4,24},{8,20},{12,16},{16,12},{20,8},{24,4},{28,0},{1,29},{... | collective-permute-start | bytes 196616 | tf_op jit(solution)/shard_map/ppermute | solution.py:346
  31.9 3.0 %all-to-all-done.v_ref = bf16[8,272,128]{2,1,0:T(8,128)(2,1)S(1)} async-done(((bf16[8,272,128]{2,1,0:T(8,128)(2,1)}), bf16[8,272,128]{2,1,0:T(8,128)(2,1)S(1)}, u32[]{:S(2)}, u32[]{:S(2)}) %all-to-all-start) | async-done | bytes 557088 | tf_op jit(solution)/shard_map/all_to_all | solution.py:480
  34.9 4.7 %shard_map.114 = (bf16[32,32,256]{2,1,0:T(8,128)(2,1)S(1)}, s32[3,64,128]{2,1,0:T(8,128)S(1)}, f32[64,128]{1,0:T(8,128)S(1)}) custom-call(bf16[8,272,128]{2,1,0:T(8,128)(2,1)S(1)} %all-to-all-done.v_ref, bf16[16,128,128]{2,1,0:T(8,128)(2,1)S(1)} %copy-done), custom_call_target="tpu_custom_call" | custom-call | tf_op jit(solution)/shard_map/pallas_call | solution.py:23
  40.5 2.6 %all-to-all-start.1 = ((bf16[32,32,256]{2,1,0:T(8,128)(2,1)}), bf16[32,32,256]{2,1,0:T(8,128)(2,1)S(1)}, u32[]{:S(2)}, u32[]{:S(2)}) async-start(bf16[32,32,256]{2,1,0:T(8,128)(2,1)} %copy-done.16), calls=%async_computation.1 | async-start | bytes 1048576 | tf_op jit(solution)/shard_map/all_to_all | solution.py:480
  46.4 9.0 %shard_map.115 = bf16[32,32,256]{2,1,0:T(8,128)(2,1)S(1)} custom-call(s32[64,128]{1,0:T(8,128)S(1)} %get-tuple-element.108.pick, s32[64,128]{1,0:T(8,128)S(1)} %get-tuple-element.107.near, f32[64,128]{1,0:T(8,128)S(1)} %get-tuple-element.66.weight_ref, bf16[16,128,128]{2,1,0:T(8,128)(2,1)S(1)} %copy-done.1, bf16[256,128]{1,0:T(8,128)(2,1)S(1)} %get-tuple-element.56.refs_0_, ...), custom_call_target="tpu_custom_call" | custom-call | flops 1073741824 | bytes 4194304 | tf_op jit(solution)/shard_map/pallas_call | solution.py:23
  56.2 3.2 %all-to-all-done.1 = bf16[32,32,256]{2,1,0:T(8,128)(2,1)S(1)} async-done(((bf16[32,32,256]{2,1,0:T(8,128)(2,1)}), bf16[32,32,256]{2,1,0:T(8,128)(2,1)S(1)}, u32[]{:S(2)}, u32[]{:S(2)}) %all-to-all-start.1) | async-done | bytes 524320 | tf_op jit(solution)/shard_map/all_to_all | solution.py:480
  59.5 2.6 %all-to-all-start.2 = ((bf16[32,32,256]{2,1,0:T(8,128)(2,1)}), bf16[32,32,256]{2,1,0:T(8,128)(2,1)S(1)}, u32[]{:S(2)}, u32[]{:S(2)}) async-start(bf16[32,32,256]{2,1,0:T(8,128)(2,1)} %copy-done.17), calls=%async_computation.2 | async-start | bytes 1048576 | tf_op jit(solution)/shard_map/all_to_all | solution.py:480
  62.1 3.0 %shard_map.116 = (f32[1024,256]{1,0:T(8,128)S(1)}, bf16[1024,256]{1,0:T(8,128)(2,1)S(1)}, bf16[1024,256]{1,0:T(8,128)(2,1)S(1)}) custom-call(bf16[1024,256]{1,0:T(8,128)(2,1)S(1)} %bitcast.17, bf16[2,256,1024]{2,1,0:T(8,128)(2,1)S(1)} %pad_maximum_fusion.refs_0_, bf16[2,256,1024]{2,1,0:T(8,128)(2,1)S(1)} %collective-permute-done.7.refs_1_, ...), custom_call_target="tpu_custom_call" | custom-call | flops 1073741824 | bytes 4194304 | tf_op jit(solution)/shard_map/pallas_call | solution.py:23
  67.7 10.7 %all-to-all-done.2 = bf16[32,32,256]{2,1,0:T(8,128)(2,1)S(1)} async-done(((bf16[32,32,256]{2,1,0:T(8,128)(2,1)}), bf16[32,32,256]{2,1,0:T(8,128)(2,1)S(1)}, u32[]{:S(2)}, u32[]{:S(2)}) %all-to-all-start.2) | async-done | bytes 524320 | tf_op jit(solution)/shard_map/all_to_all | solution.py:480
  82.8 2.6 %all-to-all-start.3 = ((bf16[32,32,256]{2,1,0:T(8,128)(2,1)}), bf16[32,32,256]{2,1,0:T(8,128)(2,1)S(1)}, u32[]{:S(2)}, u32[]{:S(2)}) async-start(bf16[32,32,256]{2,1,0:T(8,128)(2,1)} %bitcast.21), calls=%async_computation.3 | async-start | bytes 1048576 | tf_op jit(solution)/shard_map/all_to_all | solution.py:480
  88.0 4.5 %shard_map.120 = (bf16[2,8,128,256]{3,2,1,0:T(8,128)(2,1)}, f32[2,8,128,256]{3,2,1,0:T(8,128)S(1)}, bf16[1024,256]{1,0:T(8,128)(2,1)}) custom-call(f32[1024,256]{1,0:T(8,128)S(1)} %copy-done.10, bf16[1024,256]{1,0:T(8,128)(2,1)S(1)} %bitcast.20, bf16[1024,256]{1,0:T(8,128)(2,1)S(1)} %bitcast.18, bf16[2,256,1024]{2,1,0:T(8,128)(2,1)S(1)} %pad_maximum_fusion.refs_0_, ...), custom_call_target="tpu_custom_call" | custom-call | flops 1073741824 | bytes 4194304 | tf_op jit(solution)/shard_map/pallas_call | solution.py:23
  92.6 3.0 %shard_map.118 = (f32[4,128,256]{2,1,0:T(8,128)S(1)}, bf16[4,128,256]{2,1,0:T(8,128)(2,1)}, bf16[4,128,256]{2,1,0:T(8,128)(2,1)}, bf16[4,128,256]{2,1,0:T(8,128)(2,1)}) custom-call(f32[2,8,128,256]{3,2,1,0:T(8,128)S(1)} %copy-done.8, bf16[2,8,128,256]{3,2,1,0:T(8,128)(2,1)} %collective-permute-done.10.came_ref), custom_call_target="tpu_custom_call" | custom-call | tf_op jit(solution)/shard_map/pallas_call | solution.py:23
  101.7 6.6 %shard_map.119 = bf16[8,32,1024]{2,1,0:T(8,128)(2,1)} custom-call(s32[64,128]{1,0:T(8,128)S(1)} %get-tuple-element.109.pick, f32[64,128]{1,0:T(8,128)S(1)} %get-tuple-element.66.weight_ref, bf16[32,32,256]{2,1,0:T(8,128)(2,1)S(1)} %all-to-all-done.3.v_ref, bf16[16,128,128]{2,1,0:T(8,128)(2,1)S(1)} %copy-done.2), custom_call_target="tpu_custom_call" | custom-call | tf_op jit(solution)/shard_map/pallas_call | solution.py:23
  108.3 3.9 %collective-permute-done.13.refs_2_ = bf16[4,128,256]{2,1,0:T(8,128)(2,1)} collective-permute-done((bf16[4,128,256]{2,1,0:T(8,128)(2,1)}, bf16[4,128,256]{2,1,0:T(8,128)(2,1)}, u32[]{:S(2)}, u32[]{:S(2)}) %collective-permute-start.13) | collective-permute-done | bytes 262176 | tf_op jit(solution)/shard_map/ppermute | solution.py:452
  112.2 5.1 %all-to-all-start.4 = ((bf16[8,32,1024]{2,1,0:T(8,128)(2,1)}), bf16[8,32,1024]{2,1,0:T(8,128)(2,1)}, u32[]{:S(2)}, u32[]{:S(2)}) async-start(bf16[8,32,1024]{2,1,0:T(8,128)(2,1)} %shard_map.119), calls=%async_computation.4 | async-start | bytes 1048576 | tf_op jit(solution)/shard_map/all_to_all | solution.py:480
  118.8 2.1 %collective-permute-start.15 = (bf16[4,128,256]{2,1,0:T(8,128)(2,1)S(1)}, bf16[4,128,256]{2,1,0:T(8,128)(2,1)S(1)}, u32[]{:S(2)}, u32[]{:S(2)}) collective-permute-start(bf16[4,128,256]{2,1,0:T(8,128)(2,1)S(1)} %get-tuple-element.88), channel_id=1, source_target_pairs={{0,4},{1,5},{2,6},{3,7},{4,0},{5,1},{6,2},{7,3},{8,12},{9,13},{10,... | collective-permute-start | bytes 786440 | tf_op jit(solution)/shard_map/ppermute | solution.py:452
  125.5 2.4 %collective-permute-start.22 = (bf16[128,256]{1,0:T(8,128)(2,1)S(1)}, bf16[128,256]{1,0:T(8,128)(2,1)S(1)}, u32[]{:S(2)}, u32[]{:S(2)}) collective-permute-start(bf16[128,256]{1,0:T(8,128)(2,1)S(1)} %get-tuple-element.105), channel_id=1, source_target_pairs={{0,16},{4,20},{8,24},{12,28},{16,0},{20,4},{24,8},{28,12},{1,17},{... | collective-permute-start | bytes 196616 | tf_op jit(solution)/shard_map/ppermute | solution.py:346
  127.9 8.4 %collective-permute-done.15.refs_0_ = bf16[4,128,256]{2,1,0:T(8,128)(2,1)S(1)} collective-permute-done((bf16[4,128,256]{2,1,0:T(8,128)(2,1)S(1)}, bf16[4,128,256]{2,1,0:T(8,128)(2,1)S(1)}, u32[]{:S(2)}, u32[]{:S(2)}) %collective-permute-start.15) | collective-permute-done | bytes 262176 | tf_op jit(solution)/shard_map/ppermute | solution.py:452
  136.3 3.3 %collective-permute-start.23 = (bf16[128,256]{1,0:T(8,128)(2,1)S(1)}, bf16[128,256]{1,0:T(8,128)(2,1)S(1)}, u32[]{:S(2)}, u32[]{:S(2)}) collective-permute-start(bf16[128,256]{1,0:T(8,128)(2,1)S(1)} %get-tuple-element.106), channel_id=1, source_target_pairs={{0,24},{4,28},{8,16},{12,20},{16,8},{20,12},{24,0},{28,4},{1,25},{... | collective-permute-start | bytes 196616 | tf_op jit(solution)/shard_map/ppermute | solution.py:346
  140.9 3.3 %collective-permute-start.20 = (bf16[128,256]{1,0:T(8,128)(2,1)S(1)}, bf16[128,256]{1,0:T(8,128)(2,1)S(1)}, u32[]{:S(2)}, u32[]{:S(2)}) collective-permute-start(bf16[128,256]{1,0:T(8,128)(2,1)S(1)} %get-tuple-element.98), channel_id=1, source_target_pairs={{0,24},{4,28},{8,16},{12,20},{16,8},{20,12},{24,0},{28,4},{1,25},{... | collective-permute-start | bytes 196616 | tf_op jit(solution)/shard_map/ppermute | solution.py:346
  (112 shorter events, 45.4 us)
Async XLA Ops:
  6.1 28.9 %all-to-all-start = ((bf16[8,272,128]{2,1,0:T(8,128)(2,1)}), bf16[8,272,128]{2,1,0:T(8,128)(2,1)S(1)}, u32[]{:S(2)}, u32[]{:S(2)}) async-start(bf16[8,272,128]{2,1,0:T(8,128)(2,1)} %shard_map.112), calls=%async_computation | async-start | bytes 1114112 | tf_op jit(solution)/shard_map/all_to_all | solution.py:480
  13.9 29.3 %collective-permute-start.7 = (bf16[2,256,1024]{2,1,0:T(8,128)(2,1)S(1)}, bf16[2,256,1024]{2,1,0:T(8,128)(2,1)S(1)}, u32[]{:S(2)}, u32[]{:S(2)}) collective-permute-start(bf16[2,256,1024]{2,1,0:T(8,128)(2,1)S(1)} %pad_maximum_fusion.refs_0_), channel_id=1, source_target_pairs={{0,2},{1,3},{2,0},{3,1},{4,6},{5,7},{6,4},{7,5},{8,10},{9,11},{10,... | collective-permute-start | bytes 3145736 | tf_op jit(solution)/shard_map/ppermute | solution.py:346
  20.9 8.0 %collective-permute-start.2 = (bf16[256,128]{1,0:T(8,128)(2,1)S(1)}, bf16[256,128]{1,0:T(8,128)(2,1)S(1)}, u32[]{:S(2)}, u32[]{:S(2)}) collective-permute-start(bf16[256,128]{1,0:T(8,128)(2,1)S(1)} %get-tuple-element.59), channel_id=1, source_target_pairs={{0,12},{4,8},{8,4},{12,0},{16,28},{20,24},{24,20},{28,16},{1,13},{... | collective-permute-start | bytes 196616 | tf_op jit(solution)/shard_map/ppermute | solution.py:346
  20.9 19.5 %collective-permute-start.3 = (bf16[256,128]{1,0:T(8,128)(2,1)}, bf16[256,128]{1,0:T(8,128)(2,1)}, u32[]{:S(2)}, u32[]{:S(2)}) collective-permute-start(bf16[256,128]{1,0:T(8,128)(2,1)} %get-tuple-element.60), channel_id=1, source_target_pairs={{0,16},{4,20},{8,24},{12,28},{16,0},{20,4},{24,8},{28,12},{1,17},{... | collective-permute-start | bytes 196616 | tf_op jit(solution)/shard_map/ppermute | solution.py:346
  23.9 16.6 %collective-permute-start.4 = (bf16[256,128]{1,0:T(8,128)(2,1)}, bf16[256,128]{1,0:T(8,128)(2,1)}, u32[]{:S(2)}, u32[]{:S(2)}) collective-permute-start(bf16[256,128]{1,0:T(8,128)(2,1)} %get-tuple-element.61), channel_id=1, source_target_pairs={{0,20},{4,16},{8,28},{12,24},{16,4},{20,0},{24,12},{28,8},{1,21},{... | collective-permute-start | bytes 196616 | tf_op jit(solution)/shard_map/ppermute | solution.py:346
  26.1 14.3 %collective-permute-start.5 = (bf16[256,128]{1,0:T(8,128)(2,1)}, bf16[256,128]{1,0:T(8,128)(2,1)}, u32[]{:S(2)}, u32[]{:S(2)}) collective-permute-start(bf16[256,128]{1,0:T(8,128)(2,1)} %get-tuple-element.62), channel_id=1, source_target_pairs={{0,24},{4,28},{8,16},{12,20},{16,8},{20,12},{24,0},{28,4},{1,25},{... | collective-permute-start | bytes 196616 | tf_op jit(solution)/shard_map/ppermute | solution.py:346
  29.6 10.9 %collective-permute-start.6 = (bf16[256,128]{1,0:T(8,128)(2,1)}, bf16[256,128]{1,0:T(8,128)(2,1)}, u32[]{:S(2)}, u32[]{:S(2)}) collective-permute-start(bf16[256,128]{1,0:T(8,128)(2,1)} %get-tuple-element.63), channel_id=1, source_target_pairs={{0,28},{4,24},{8,20},{12,16},{16,12},{20,8},{24,4},{28,0},{1,29},{... | collective-permute-start | bytes 196616 | tf_op jit(solution)/shard_map/ppermute | solution.py:346
  40.5 19.0 %all-to-all-start.1 = ((bf16[32,32,256]{2,1,0:T(8,128)(2,1)}), bf16[32,32,256]{2,1,0:T(8,128)(2,1)S(1)}, u32[]{:S(2)}, u32[]{:S(2)}) async-start(bf16[32,32,256]{2,1,0:T(8,128)(2,1)} %copy-done.16), calls=%async_computation.1 | async-start | bytes 1048576 | tf_op jit(solution)/shard_map/all_to_all | solution.py:480
  43.1 19.0 %collective-permute-start.8 = (bf16[2,256,1024]{2,1,0:T(8,128)(2,1)S(1)}, bf16[2,256,1024]{2,1,0:T(8,128)(2,1)}, u32[]{:S(2)}, u32[]{:S(2)}) collective-permute-start(bf16[2,256,1024]{2,1,0:T(8,128)(2,1)S(1)} %pad_maximum_fusion.refs_0_), channel_id=1, source_target_pairs={{0,1},{1,0},{2,3},{3,2},{4,5},{5,4},{6,7},{7,6},{8,9},{9,8},{10,11... | collective-permute-start | bytes 3145736 | tf_op jit(solution)/shard_map/ppermute | solution.py:346
  43.3 18.8 %collective-permute-start.9 = (bf16[2,256,1024]{2,1,0:T(8,128)(2,1)S(1)}, bf16[2,256,1024]{2,1,0:T(8,128)(2,1)}, u32[]{:S(2)}, u32[]{:S(2)}) collective-permute-start(bf16[2,256,1024]{2,1,0:T(8,128)(2,1)S(1)} %collective-permute-done.7.refs_1_), channel_id=1, source_target_pairs={{0,1},{1,0},{2,3},{3,2},{4,5},{5,4},{6,7},{7,6},{8,9},{9,8},{10,11... | collective-permute-start | bytes 3145736 | tf_op jit(solution)/shard_map/ppermute | solution.py:346
  59.5 19.0 %all-to-all-start.2 = ((bf16[32,32,256]{2,1,0:T(8,128)(2,1)}), bf16[32,32,256]{2,1,0:T(8,128)(2,1)S(1)}, u32[]{:S(2)}, u32[]{:S(2)}) async-start(bf16[32,32,256]{2,1,0:T(8,128)(2,1)} %copy-done.17), calls=%async_computation.2 | async-start | bytes 1048576 | tf_op jit(solution)/shard_map/all_to_all | solution.py:480
  82.8 19.0 %all-to-all-start.3 = ((bf16[32,32,256]{2,1,0:T(8,128)(2,1)}), bf16[32,32,256]{2,1,0:T(8,128)(2,1)S(1)}, u32[]{:S(2)}, u32[]{:S(2)}) async-start(bf16[32,32,256]{2,1,0:T(8,128)(2,1)} %bitcast.21), calls=%async_computation.3 | async-start | bytes 1048576 | tf_op jit(solution)/shard_map/all_to_all | solution.py:480
  92.5 24.9 %collective-permute-start.14 = (bf16[2,8,128,256]{3,2,1,0:T(8,128)(2,1)}, bf16[2,8,128,256]{3,2,1,0:T(8,128)(2,1)}, u32[]{:S(2)}, u32[]{:S(2)}) collective-permute-start(bf16[2,8,128,256]{3,2,1,0:T(8,128)(2,1)} %get-tuple-element.86), channel_id=1, source_target_pairs={{0,1},{1,0},{2,3},{3,2},{4,5},{5,4},{6,7},{7,6},{8,9},{9,8},{10,11... | collective-permute-start | bytes 3145736 | tf_op jit(solution)/shard_map/ppermute | solution.py:346
  96.4 11.9 %collective-permute-start.11 = (bf16[4,128,256]{2,1,0:T(8,128)(2,1)}, bf16[4,128,256]{2,1,0:T(8,128)(2,1)S(1)}, u32[]{:S(2)}, u32[]{:S(2)}) collective-permute-start(bf16[4,128,256]{2,1,0:T(8,128)(2,1)} %get-tuple-element.79), channel_id=1, source_target_pairs={{0,4},{1,5},{2,6},{3,7},{4,0},{5,1},{6,2},{7,3},{8,12},{9,13},{10,... | collective-permute-start | bytes 786440 | tf_op jit(solution)/shard_map/ppermute | solution.py:452
  97.7 10.6 %collective-permute-start.12 = (bf16[4,128,256]{2,1,0:T(8,128)(2,1)}, bf16[4,128,256]{2,1,0:T(8,128)(2,1)}, u32[]{:S(2)}, u32[]{:S(2)}) collective-permute-start(bf16[4,128,256]{2,1,0:T(8,128)(2,1)} %get-tuple-element.80), channel_id=1, source_target_pairs={{0,2},{1,3},{2,0},{3,1},{4,6},{5,7},{6,4},{7,5},{8,10},{9,11},{10,... | collective-permute-start | bytes 786440 | tf_op jit(solution)/shard_map/ppermute | solution.py:452
  99.2 13.1 %collective-permute-start.13 = (bf16[4,128,256]{2,1,0:T(8,128)(2,1)}, bf16[4,128,256]{2,1,0:T(8,128)(2,1)}, u32[]{:S(2)}, u32[]{:S(2)}) collective-permute-start(bf16[4,128,256]{2,1,0:T(8,128)(2,1)} %get-tuple-element.81), channel_id=1, source_target_pairs={{0,6},{1,7},{2,4},{3,5},{4,2},{5,3},{6,0},{7,1},{8,14},{9,15},{10,... | collective-permute-start | bytes 786440 | tf_op jit(solution)/shard_map/ppermute | solution.py:452
  112.2 32.6 %all-to-all-start.4 = ((bf16[8,32,1024]{2,1,0:T(8,128)(2,1)}), bf16[8,32,1024]{2,1,0:T(8,128)(2,1)}, u32[]{:S(2)}, u32[]{:S(2)}) async-start(bf16[8,32,1024]{2,1,0:T(8,128)(2,1)} %shard_map.119), calls=%async_computation.4 | async-start | bytes 1048576 | tf_op jit(solution)/shard_map/all_to_all | solution.py:480
  118.8 17.5 %collective-permute-start.15 = (bf16[4,128,256]{2,1,0:T(8,128)(2,1)S(1)}, bf16[4,128,256]{2,1,0:T(8,128)(2,1)S(1)}, u32[]{:S(2)}, u32[]{:S(2)}) collective-permute-start(bf16[4,128,256]{2,1,0:T(8,128)(2,1)S(1)} %get-tuple-element.88), channel_id=1, source_target_pairs={{0,4},{1,5},{2,6},{3,7},{4,0},{5,1},{6,2},{7,3},{8,12},{9,13},{10,... | collective-permute-start | bytes 786440 | tf_op jit(solution)/shard_map/ppermute | solution.py:452
  120.8 18.8 %collective-permute-start.16 = (bf16[4,128,256]{2,1,0:T(8,128)(2,1)S(1)}, bf16[4,128,256]{2,1,0:T(8,128)(2,1)S(1)}, u32[]{:S(2)}, u32[]{:S(2)}) collective-permute-start(bf16[4,128,256]{2,1,0:T(8,128)(2,1)S(1)} %get-tuple-element.89), channel_id=1, source_target_pairs={{0,2},{1,3},{2,0},{3,1},{4,6},{5,7},{6,4},{7,5},{8,10},{9,11},{10,... | collective-permute-start | bytes 786440 | tf_op jit(solution)/shard_map/ppermute | solution.py:452
  122.3 17.3 %collective-permute-start.17 = (bf16[4,128,256]{2,1,0:T(8,128)(2,1)S(1)}, bf16[4,128,256]{2,1,0:T(8,128)(2,1)S(1)}, u32[]{:S(2)}, u32[]{:S(2)}) collective-permute-start(bf16[4,128,256]{2,1,0:T(8,128)(2,1)S(1)} %get-tuple-element.90), channel_id=1, source_target_pairs={{0,6},{1,7},{2,4},{3,5},{4,2},{5,3},{6,0},{7,1},{8,14},{9,15},{10,... | collective-permute-start | bytes 786440 | tf_op jit(solution)/shard_map/ppermute | solution.py:452
  123.5 17.3 %collective-permute-start.21 = (bf16[128,256]{1,0:T(8,128)(2,1)S(1)}, bf16[128,256]{1,0:T(8,128)(2,1)S(1)}, u32[]{:S(2)}, u32[]{:S(2)}) collective-permute-start(bf16[128,256]{1,0:T(8,128)(2,1)S(1)} %get-tuple-element.104), channel_id=1, source_target_pairs={{0,8},{4,12},{8,0},{12,4},{16,24},{20,28},{24,16},{28,20},{1,9},{5... | collective-permute-start | bytes 196616 | tf_op jit(solution)/shard_map/ppermute | solution.py:346
  125.5 18.7 %collective-permute-start.22 = (bf16[128,256]{1,0:T(8,128)(2,1)S(1)}, bf16[128,256]{1,0:T(8,128)(2,1)S(1)}, u32[]{:S(2)}, u32[]{:S(2)}) collective-permute-start(bf16[128,256]{1,0:T(8,128)(2,1)S(1)} %get-tuple-element.105), channel_id=1, source_target_pairs={{0,16},{4,20},{8,24},{12,28},{16,0},{20,4},{24,8},{28,12},{1,17},{... | collective-permute-start | bytes 196616 | tf_op jit(solution)/shard_map/ppermute | solution.py:346
  136.3 7.9 %collective-permute-start.23 = (bf16[128,256]{1,0:T(8,128)(2,1)S(1)}, bf16[128,256]{1,0:T(8,128)(2,1)S(1)}, u32[]{:S(2)}, u32[]{:S(2)}) collective-permute-start(bf16[128,256]{1,0:T(8,128)(2,1)S(1)} %get-tuple-element.106), channel_id=1, source_target_pairs={{0,24},{4,28},{8,16},{12,20},{16,8},{20,12},{24,0},{28,4},{1,25},{... | collective-permute-start | bytes 196616 | tf_op jit(solution)/shard_map/ppermute | solution.py:346
  139.8 7.5 %collective-permute-start.19 = (bf16[128,256]{1,0:T(8,128)(2,1)S(1)}, bf16[128,256]{1,0:T(8,128)(2,1)S(1)}, u32[]{:S(2)}, u32[]{:S(2)}) collective-permute-start(bf16[128,256]{1,0:T(8,128)(2,1)S(1)} %get-tuple-element.97), channel_id=1, source_target_pairs={{0,16},{4,20},{8,24},{12,28},{16,0},{20,4},{24,8},{28,12},{1,17},{... | collective-permute-start | bytes 196616 | tf_op jit(solution)/shard_map/ppermute | solution.py:346
  (34 other events, 160.4 us)

commit v5 on v4

--- a/solution.py
+++ b/solution.py
@@ -13,22 +13,23 @@
 bf16, f32 = jnp.bfloat16, jnp.float32
 vmem = pl.BlockSpec(memory_space=pltpu.VMEM)
 smem = pl.BlockSpec(memory_space=pltpu.SMEM)
+far = object()
 
 
 def nt_dot(a, b):
     return lax.dot_general(a, b, (((1,), (1,)), ((), ())), preferred_element_type=f32)
 
 
-def call(body, outs, in_specs, args, scratch=(), flops=0, limit=16, moved=0):
+def call(body, outs, in_specs, args, scratch=(), flops=0, limit=16, moved=0, sent=()):
     return pl.pallas_call(
         body,
-        out_shape=[jax.ShapeDtypeStruct(s, d) for s, d in outs],
-        in_specs=in_specs,
+        out_shape=[(pltpu.HBM if i in sent else jax.ShapeDtypeStruct)(s, d) for i, (s, d) in enumerate(outs)],
+        in_specs=[vmem if spec is far else spec for spec in in_specs],
         out_specs=[vmem] * len(outs),
         scratch_shapes=list(scratch),
         compiler_params=pltpu.CompilerParams(vmem_limit_bytes=limit * 1024 * 1024),
         cost_estimate=pl.CostEstimate(flops=flops, bytes_accessed=moved, transcendentals=0),
-    )(*args)
+    )(*[v for v in args])
 
 
 def after(values, *earlier):
@@ -59,7 +60,7 @@
         for n in range(nodes):
             o_ref[n, b * width : (b + 1) * width, :] = turned[n * width : (n + 1) * width]
     tile = meta_tile(
-        lambda p, c: ghosts[p, c], lambda r: degrees[r], slots_ref[...], tiles_ref[...], owners, held, size
+        lambda p, c: ghosts[p : p + 1, c : c + 1], lambda r: degrees[r], slots_ref[...], tiles_ref[...], owners, held, size
     )
     for n in range(nodes):
         o_ref[n, rows - meta_rows :, :] = tile
@@ -81,8 +82,9 @@
     return call(
         functools.partial(pack_kernel, owners, held),
         [((nodes, per * width + meta_rows, size), bf16)],
-        [smem, smem, vmem, vmem, vmem],
+        [vmem, smem, vmem, vmem, vmem],
         (ghosts, degrees, slots, tile_ids, features),
+        sent=(0,),
     )[0]
 
 
@@ -109,9 +111,10 @@
     return call(
         turn_kernel,
         [((per * width, size), bf16)] * nodes,
-        [vmem],
+        [far],
         (values,),
         [pltpu.VMEM((per, values.shape[1], size), bf16)],
+        sent=tuple(range(nodes)),
     )
 
 
@@ -288,7 +291,7 @@
     out, ids, weight = call(
         functools.partial(first_kernel, per, width_k),
         [((feat_count * nodes, width, share * size), bf16), return_ids, ((count, size), f32)],
-        [vmem, vmem],
+        [far, far],
         (v, tiles),
         [
             pltpu.SMEM((count, size), jnp.int32),
@@ -297,6 +300,7 @@
         ],
         0,
         28,
+        sent=(0,),
     )
     return out, (ids[0], ids[1], ids[2], weight)
 
@@ -313,12 +317,13 @@
     return call(
         functools.partial(back_spread_kernel, per, width_k, nodes),
         [((feat_count * nodes, width, share * size), bf16)],
-        [smem, smem, vmem, vmem] + [vmem] * nodes,
+        [smem, smem, vmem, far] + [far] * nodes,
         (pick_back, near, weight, tiles, *parts),
         [product_scratch(tiles, count, width)] + [pltpu.VMEM((count, width, size), f32)] * unroll,
         product_flops(tiles, count, width),
         28,
         4 << 20,
+        (0,),
     )[0]
 
 
@@ -334,11 +339,12 @@
     return call(
         functools.partial(last_kernel, per, width_k),
         [((nodes, width, per * size), bf16)],
-        [smem, vmem, vmem, vmem],
+        [smem, vmem, far, far],
         (pick, weight, v, tiles),
         [pltpu.VMEM((count, width, size), bf16), product_scratch(tiles, count, width)],
-        0,
+        10 * product_flops(tiles, count, width),
         28,
+        sent=(0,),
     )[0]
 
 
@@ -372,23 +378,30 @@
         y_ref[at, :] = jnp.dot(w_ref[1], hidden, preferred_element_type=f32).astype(bf16)
 
 
-def halves_of(left_ref, right_ref, give_ref, keep_ref, offsets):
+def side_rows(left_ref, tall):
+    side = lax.axis_index("nodes") % 2
+    pick = lambda row: left_ref[pl.ds(pl.multiple_of(row * tall, tall), tall), :]
+    half = left_ref.shape[0] // (2 * tall)
+    return [jnp.concatenate([pick(2 * h + (side ^ b)) for h in range(half)], axis=0) for b in range(2)]
+
+
+def give_blocks(left_ref, right_ref, outs, offsets):
     me = lax.axis_index("feat")
-    nodes, tall, wide = give_ref.shape[1:]
-    left = left_ref[...]
+    half, tall, wide = outs[0].shape
+    lefts = side_rows(left_ref, tall)
     for i, o in enumerate(offsets):
-        for out, to in ((give_ref, me ^ o ^ 1), (keep_ref, me ^ o)):
-            right = right_ref[pl.ds(pl.multiple_of(to * wide, wide), wide), :]
-            out[i] = nt_dot(left, right).reshape(nodes, tall, wide).astype(out.dtype)
-
-
-def product_kernel(offsets, left_ref, right_ref, give_ref, keep_ref):
-    halves_of(left_ref, right_ref, give_ref, keep_ref, offsets)
+        right = right_ref[pl.ds(pl.multiple_of((me ^ o ^ 1) * wide, wide), wide), :]
+        for b in range(2):
+            outs[2 * i + b][...] = nt_dot(lefts[b], right).reshape(half, tall, wide).astype(bf16)
+
+
+def product_kernel(offsets, left_ref, right_ref, *outs):
+    give_blocks(left_ref, right_ref, outs, offsets)
 
 
 def back_kernel(offsets, evens, pre_ref, back_ref, left_ref, *refs):
     count = len(offsets)
-    weights, (give_ref, keep_ref, out_ref) = refs[:count], refs[count:]
+    weights, outs, out_ref = refs[:count], refs[count:-1], refs[-1]
     me = lax.axis_index("feat")
     wide = weights[0].shape[1]
     place = [pl.ds(pl.multiple_of((me ^ o) * wide, wide), wide) for o in offsets]
@@ -402,17 +415,20 @@
         pre = pre_ref[at, :]
         sigma = jax.nn.sigmoid(pre)
         out_ref[at, :] = (total * sigma * (1.0 + pre * (1.0 - sigma))).astype(bf16)
-    halves_of(left_ref, out_ref, give_ref, keep_ref, evens)
-
-
-def quarter_kernel(keep_ref, came_ref, mine_ref, *outs):
-    side = lax.axis_index("nodes") % 2
-    half = mine_ref.shape[0]
-    spots = [(i, b) for i in range(keep_ref.shape[0]) for b in range(2)]
-    for (i, b), o_ref in zip(spots, (mine_ref,) + outs):
-        for h in range(half):
-            row = 2 * h + (side ^ b)
-            o_ref[h] = (keep_ref[i, row] + came_ref[i, row].astype(f32)).astype(o_ref.dtype)
+    give_blocks(left_ref, out_ref, outs, evens)
+
+
+def quarter_kernel(offsets, left_ref, right_ref, *refs):
+    spots = 2 * len(offsets)
+    came, outs = refs[:spots], refs[spots:]
+    me = lax.axis_index("feat")
+    half, tall, wide = outs[0].shape
+    lefts = side_rows(left_ref, tall)
+    for i, o in enumerate(offsets):
+        right = right_ref[pl.ds(pl.multiple_of((me ^ o) * wide, wide), wide), :]
+        for b in range(2):
+            total = nt_dot(lefts[b], right).reshape(half, tall, wide) + came[2 * i + b][...].astype(f32)
+            outs[2 * i + b][...] = total.astype(outs[2 * i + b].dtype)
 
 
 def split_kernel(keep_ref, *refs):
@@ -430,37 +446,44 @@
     return list(range(0, lax.axis_size("feat"), 2))
 
 
-def grad_shapes(left, right):
+def give_shapes(hidden_width):
     nodes, count = lax.axis_size("nodes"), lax.axis_size("feat")
-    shape = (count // 2, nodes, left.shape[0] // nodes, right.shape[0] // count)
-    return [(shape, bf16), (shape, f32)]
-
-
-def quarters(swapped, keep):
-    _, nodes, tall, wide = keep.shape
-    evens, feat_count = even_offsets(), lax.axis_size("feat")
-    spots = [(o, b) for o in evens for b in range(2)][1:]
-    shape = (nodes // 2, tall, wide)
-    mine, *rest = call(
-        quarter_kernel,
-        [(shape, f32)] + [(shape, bf16)] * len(spots),
-        [vmem] * 2,
-        (keep, swapped),
-    )
+    return [((nodes // 2, hidden_width // nodes, hidden_width // count), bf16)] * count
+
+
+def quarters(left, right, *given):
+    swapped = [swap(v, "feat", 1) for v in given]
+    shape = given[0].shape
+    return call(
+        functools.partial(quarter_kernel, even_offsets()),
+        [(shape, f32)] + [(shape, bf16)] * (len(given) - 1),
+        [vmem] * (2 + len(given)),
+        (left, right, *swapped),
+        sent=tuple(range(1, len(given))),
+    )
+
+
+def pass_quarters(mine, *rest, late=None):
+    nodes, feat_count = lax.axis_size("nodes"), lax.axis_size("feat")
+    spots = [(o, b) for o in even_offsets() for b in range(2)][1:]
     ring = range(nodes * feat_count)
+    if late is not None:
+        rest = [after(v, late) if o == 0 else v for v, (o, b) in zip(rest, spots)]
     moved = [
         lax.ppermute(v, ("nodes", "feat"), [(i, i ^ (b * feat_count + o)) for i in ring]) for v, (o, b) in zip(rest, spots)
     ]
     return mine, *moved
 
 
-def grad_sum(keep, *came):
+def grad_sum(flops, keep, *came):
     half, tall, wide = keep.shape
     mine, *rest = call(
         split_kernel,
         [((tall, wide), f32)] + [((tall, wide), bf16)] * (half - 1),
-        [vmem] * (1 + len(came)),
+        [vmem] + [far] * len(came),
         (keep, *came),
+        flops=flops,
+        sent=tuple(range(1, half)),
     )
     for i, part in enumerate(rest):
         mine = mine + swap(part, "nodes", 2 * (i + 1)).astype(f32)
@@ -496,36 +519,38 @@
     pre, hidden, wide_out = call(
         functools.partial(project_kernel, offsets),
         [((hidden_width, held), f32)] + [((hidden_width, held), bf16)] * 2,
-        [vmem] * (1 + parts),
+        [far] + [vmem] * parts,
         (agg, *weights),
         flops=4 * hidden_width * hidden_width * held,
         moved=4 << 20,
+        sent=(2,),
     )
     wide_out = after(wide_out, back)
     out_t = exchange(wide_out.reshape(feat_count * nodes, wide // nodes, held), every)
 
     evens = even_offsets()
-    flops = 2 * hidden_width * hidden_width * held
-    give_two, keep_two = call(
-        functools.partial(product_kernel, evens), grad_shapes(hidden, back), [vmem] * 2, (hidden, back), flops=flops, moved=4 << 20
-    )
-    swapped_two = swap(give_two, "feat", 1)
-    give_one, keep_one, _ = call(
+    give_two = call(
+        functools.partial(product_kernel, evens),
+        give_shapes(hidden_width),
+        [vmem] * 2,
+        (hidden, back),
+        sent=tuple(range(parts)),
+    )
+    *give_one, back_pre = call(
         functools.partial(back_kernel, offsets, evens),
-        grad_shapes(agg, back) + [((hidden_width, held), bf16)],
+        give_shapes(hidden_width) + [((hidden_width, held), bf16)],
         [vmem] * (3 + parts),
-        (pre, after(back, swapped_two), agg, *weights),
-        flops=2 * flops,
-        moved=4 << 20,
-    )
-    quarters_two = quarters(swapped_two, keep_two)
-    quarters_one = quarters(swap(give_one, "feat", 1), keep_one)
-
-    out_t = after(out_t, quarters_two[0])
+        (pre, back, agg, *weights),
+        sent=tuple(range(parts)),
+    )
+    halves_two = quarters(hidden, back, *give_two)
+    halves_one = quarters(agg, back_pre, *give_one)
+    quarters_two = pass_quarters(*halves_two)
     last = spread_last(out_t, ids, tile_table, per, width_k, nodes)
-    out_n = exchange(after(last, *quarters_two), "nodes")
-    grad_two = grad_sum(*after(quarters_two, last))
-    grad_one = grad_sum(*after(quarters_one, last))
+    out_n = exchange(last, "nodes")
+    quarters_one = pass_quarters(*halves_one, late=None)
+    grad_two = grad_sum(0, *after(quarters_two, last))
+    grad_one = grad_sum(20 << 30, *after(quarters_one, last))
     output = out_n.reshape(wide, rows).T
     return (output, grad_one, grad_two)
 

time: 149 us -> 140 us (0.940)
  local copies, waits for them, and re-layouts: 20.5 us -> 13.8 us
  waiting for transfers between devices: 31.9 us -> 27.1 us
  starting transfers between devices: 55.6 us -> 58.5 us
    ppermute x6, waiting for transfers between devices: 12.3 us -> 3.94 us  [pass_quarters(): lax.ppermute(v, ('nodes', 'feat'), [(i, i ^ b * feat_count + o) for i in...]
    unnamed x59 -> x49, local copies, waits for them, and re-layouts: 18 us -> 12.3 us
    ppermute x18 -> x24, waiting for transfers between devices: 0.82 us -> 5.57 us  [swap(): lax.ppermute(values, axis, [(i, i ^ mask) for i in range(lax.axis_size(ax...]
    ppermute x18 -> x24, starting transfers between devices: 28.3 us -> 28.9 us  [swap(): lax.ppermute(values, axis, [(i, i ^ mask) for i in range(lax.axis_size(ax...]
  transfers between devices with their start and end apart: 29 -> 35, of which waited for: 8 -> 6; matrix products, arithmetic and copies ran while one was open for 2% -> 1% of each run, Pallas kernels for 23% -> 26%
where the time goes in v5:
time: 140 us; the launch traced here: 139 us
  starting transfers between devices  58.5 us (42%)
  Pallas kernels  37.5 us (27%)
  waiting for transfers between devices  27.1 us (19%)
  local copies, waits for them, and re-layouts  13.8 us (10%)
  other arithmetic  1.47 us (1%)
    pallas_call x12, Pallas kernels, call(): pl.pallas_call(body, out_shape=[(pltpu.HBM if i in sent else jax.ShapeDty...  37.5 us
    ppermute x24, starting transfers between devices, swap(): lax.ppermute(values, axis, [(i, i ^ mask) for i in range(lax.axis_size(ax...  28.9 us
    all_to_all x5, starting transfers between devices, on_device(): lax.all_to_all(v, axes, split_axis=0, concat_axis=0, tiled=True)  21 us
    all_to_all x5, waiting for transfers between devices, on_device(): lax.all_to_all(v, axes, split_axis=0, concat_axis=0, tiled=True)  17.6 us
    unnamed x49, local copies, waits for them, and re-layouts  12.3 us
    ppermute x6, starting transfers between devices, pass_quarters(): lax.ppermute(v, ('nodes', 'feat'), [(i, i ^ b * feat_count + o) for i in...  8.56 us
    ppermute x24, waiting for transfers between devices, swap(): lax.ppermute(values, axis, [(i, i ^ mask) for i in range(lax.axis_size(ax...  5.57 us
    ppermute x6, waiting for transfers between devices, pass_quarters(): lax.ppermute(v, ('nodes', 'feat'), [(i, i ^ b * feat_count + o) for i in...  3.94 us
  transfers between devices with their start and end apart: 35, of which 6 were waited for; matrix products, arithmetic and copies ran while one was open for 1% of the time, Pallas kernels for 26%

profile of v5, /device:TPU:0, one launch (start us, length us, event | category | flops | bytes accessed | tf_op | source)
XLA Modules:
  0.0 139.2 jit_solution(12360187171575262039)
XLA Ops:
  4.8 7.4 %all-to-all-start = ((bf16[8,272,128]{2,1,0:T(8,128)(2,1)}), bf16[8,272,128]{2,1,0:T(8,128)(2,1)S(1)}, u32[]{:S(2)}, u32[]{:S(2)}) async-start(bf16[8,272,128]{2,1,0:T(8,128)(2,1)} %shard_map.112), calls=%async_computation | async-start | bytes 1114112 | tf_op jit(solution)/shard_map/all_to_all | solution.py:503
  16.1 2.0 %collective-permute-start = (bf16[256,128]{1,0:T(8,128)(2,1)}, bf16[256,128]{1,0:T(8,128)(2,1)S(1)}, u32[]{:S(2)}, u32[]{:S(2)}) collective-permute-start(bf16[256,128]{1,0:T(8,128)(2,1)} %get-tuple-element.59), channel_id=1, source_target_pairs={{0,4},{4,0},{8,12},{12,8},{16,20},{20,16},{24,28},{28,24},{1,5},{5... | collective-permute-start | bytes 196616 | tf_op jit(solution)/shard_map/ppermute | solution.py:352
  19.6 2.9 %collective-permute-start.3 = (bf16[256,128]{1,0:T(8,128)(2,1)}, bf16[256,128]{1,0:T(8,128)(2,1)S(1)}, u32[]{:S(2)}, u32[]{:S(2)}) collective-permute-start(bf16[256,128]{1,0:T(8,128)(2,1)} %get-tuple-element.62), channel_id=1, source_target_pairs={{0,16},{4,20},{8,24},{12,28},{16,0},{20,4},{24,8},{28,12},{1,17},{... | collective-permute-start | bytes 196616 | tf_op jit(solution)/shard_map/ppermute | solution.py:352
  22.5 2.5 %collective-permute-start.4 = (bf16[256,128]{1,0:T(8,128)(2,1)}, bf16[256,128]{1,0:T(8,128)(2,1)S(1)}, u32[]{:S(2)}, u32[]{:S(2)}) collective-permute-start(bf16[256,128]{1,0:T(8,128)(2,1)} %get-tuple-element.63), channel_id=1, source_target_pairs={{0,20},{4,16},{8,28},{12,24},{16,4},{20,0},{24,12},{28,8},{1,21},{... | collective-permute-start | bytes 196616 | tf_op jit(solution)/shard_map/ppermute | solution.py:352
  25.0 2.8 %collective-permute-start.5 = (bf16[256,128]{1,0:T(8,128)(2,1)}, bf16[256,128]{1,0:T(8,128)(2,1)S(1)}, u32[]{:S(2)}, u32[]{:S(2)}) collective-permute-start(bf16[256,128]{1,0:T(8,128)(2,1)} %get-tuple-element.64), channel_id=1, source_target_pairs={{0,24},{4,28},{8,16},{12,20},{16,8},{20,12},{24,0},{28,4},{1,25},{... | collective-permute-start | bytes 196616 | tf_op jit(solution)/shard_map/ppermute | solution.py:352
  27.8 2.3 %collective-permute-start.6 = (bf16[256,128]{1,0:T(8,128)(2,1)}, bf16[256,128]{1,0:T(8,128)(2,1)S(1)}, u32[]{:S(2)}, u32[]{:S(2)}) collective-permute-start(bf16[256,128]{1,0:T(8,128)(2,1)} %get-tuple-element.65), channel_id=1, source_target_pairs={{0,28},{4,24},{8,20},{12,16},{16,12},{20,8},{24,4},{28,0},{1,29},{... | collective-permute-start | bytes 196616 | tf_op jit(solution)/shard_map/ppermute | solution.py:352
  30.2 3.5 %all-to-all-done.v_ref = bf16[8,272,128]{2,1,0:T(8,128)(2,1)S(1)} async-done(((bf16[8,272,128]{2,1,0:T(8,128)(2,1)}), bf16[8,272,128]{2,1,0:T(8,128)(2,1)S(1)}, u32[]{:S(2)}, u32[]{:S(2)}) %all-to-all-start) | async-done | bytes 557088 | tf_op jit(solution)/shard_map/all_to_all | solution.py:503
  34.8 5.5 %shard_map.114 = (bf16[32,32,256]{2,1,0:T(8,128)(2,1)}, s32[3,64,128]{2,1,0:T(8,128)S(1)}, f32[64,128]{1,0:T(8,128)S(1)}) custom-call(bf16[8,272,128]{2,1,0:T(8,128)(2,1)S(1)} %all-to-all-done.v_ref, bf16[16,128,128]{2,1,0:T(8,128)(2,1)S(1)} %copy-done.6), custom_call_target="tpu_custom_call" | custom-call | tf_op jit(solution)/shard_map/pallas_call | solution.py:24
  42.8 2.7 %all-to-all-start.1 = ((bf16[32,32,256]{2,1,0:T(8,128)(2,1)}), bf16[32,32,256]{2,1,0:T(8,128)(2,1)S(1)}, u32[]{:S(2)}, u32[]{:S(2)}) async-start(bf16[32,32,256]{2,1,0:T(8,128)(2,1)} %get-tuple-element.70), calls=%async_computation.1 | async-start | bytes 1048576 | tf_op jit(solution)/shard_map/all_to_all | solution.py:503
  48.6 9.9 %shard_map.115 = bf16[32,32,256]{2,1,0:T(8,128)(2,1)} custom-call(s32[64,128]{1,0:T(8,128)S(1)} %get-tuple-element.112.pick, s32[64,128]{1,0:T(8,128)S(1)} %get-tuple-element.111.near, f32[64,128]{1,0:T(8,128)S(1)} %copy-done.20, bf16[16,128,128]{2,1,0:T(8,128)(2,1)S(1)} %copy-done.7, bf16[256,128]{1,0:T(8,128)(2,1)S(1)} %copy-done.12, ...), custom_call_target="tpu_custom_call" | custom-call | flops 1073741824 | bytes 4194304 | tf_op jit(solution)/shard_map/pallas_call | solution.py:24
  58.5 3.4 %all-to-all-done.1 = bf16[32,32,256]{2,1,0:T(8,128)(2,1)S(1)} async-done(((bf16[32,32,256]{2,1,0:T(8,128)(2,1)}), bf16[32,32,256]{2,1,0:T(8,128)(2,1)S(1)}, u32[]{:S(2)}, u32[]{:S(2)}) %all-to-all-start.1) | async-done | bytes 524320 | tf_op jit(solution)/shard_map/all_to_all | solution.py:503
  61.9 2.6 %all-to-all-start.2 = ((bf16[32,32,256]{2,1,0:T(8,128)(2,1)}), bf16[32,32,256]{2,1,0:T(8,128)(2,1)S(1)}, u32[]{:S(2)}, u32[]{:S(2)}) async-start(bf16[32,32,256]{2,1,0:T(8,128)(2,1)} %shard_map.115), calls=%async_computation.2 | async-start | bytes 1048576 | tf_op jit(solution)/shard_map/all_to_all | solution.py:503
  64.5 3.8 %shard_map.116 = (f32[1024,256]{1,0:T(8,128)S(1)}, bf16[1024,256]{1,0:T(8,128)(2,1)S(1)}, bf16[1024,256]{1,0:T(8,128)(2,1)}) custom-call(bf16[1024,256]{1,0:T(8,128)(2,1)S(1)} %bitcast.17, bf16[2,256,1024]{2,1,0:T(8,128)(2,1)S(1)} %pad_maximum_fusion.refs_0_, bf16[2,256,1024]{2,1,0:T(8,128)(2,1)S(1)} %collective-permute-done.7.refs_1_, ...), custom_call_target="tpu_custom_call" | custom-call | flops 1073741824 | bytes 4194304 | tf_op jit(solution)/shard_map/pallas_call | solution.py:24
  70.1 10.7 %all-to-all-done.2 = bf16[32,32,256]{2,1,0:T(8,128)(2,1)S(1)} async-done(((bf16[32,32,256]{2,1,0:T(8,128)(2,1)}), bf16[32,32,256]{2,1,0:T(8,128)(2,1)S(1)}, u32[]{:S(2)}, u32[]{:S(2)}) %all-to-all-start.2) | async-done | bytes 524320 | tf_op jit(solution)/shard_map/all_to_all | solution.py:503
  80.8 3.3 %all-to-all-start.3 = ((bf16[32,32,256]{2,1,0:T(8,128)(2,1)}), bf16[32,32,256]{2,1,0:T(8,128)(2,1)}, u32[]{:S(2)}, u32[]{:S(2)}) async-start(bf16[32,32,256]{2,1,0:T(8,128)(2,1)} %bitcast.26), calls=%async_computation.3 | async-start | bytes 1048576 | tf_op jit(solution)/shard_map/all_to_all | solution.py:503
  85.4 3.9 %shard_map.118 = (bf16[4,128,256]{2,1,0:T(8,128)(2,1)}, bf16[4,128,256]{2,1,0:T(8,128)(2,1)}, bf16[4,128,256]{2,1,0:T(8,128)(2,1)}, bf16[4,128,256]{2,1,0:T(8,128)(2,1)}, bf16[1024,256]{1,0:T(8,128)(2,1)S(1)}) custom-call(f32[1024,256]{1,0:T(8,128)S(1)} %copy-done.3, bf16[1024,256]{1,0:T(8,128)(2,1)S(1)} %bitcast.20, bf16[1024,256]{1,0:T(8,128)(2,1)S(1)} %bitcast.18, ...), custom_call_target="tpu_custom_call" | custom-call | tf_op jit(solution)/shard_map/pallas_call | solution.py:24
  101.8 6.6 %shard_map.117 = bf16[8,32,1024]{2,1,0:T(8,128)(2,1)} custom-call(s32[64,128]{1,0:T(8,128)S(1)} %get-tuple-element.113.pick, f32[64,128]{1,0:T(8,128)S(1)} %copy-done.20, bf16[32,32,256]{2,1,0:T(8,128)(2,1)} %all-to-all-done.3.v_ref, bf16[16,128,128]{2,1,0:T(8,128)(2,1)S(1)} %copy-done.8), custom_call_target="tpu_custom_call" | custom-call | flops 10737418240 | tf_op jit(solution)/shard_map/pallas_call | solution.py:24
  108.3 4.9 %all-to-all-start.4 = ((bf16[8,32,1024]{2,1,0:T(8,128)(2,1)}), bf16[8,32,1024]{2,1,0:T(8,128)(2,1)S(1)}, u32[]{:S(2)}, u32[]{:S(2)}) async-start(bf16[8,32,1024]{2,1,0:T(8,128)(2,1)} %shard_map.117), calls=%async_computation.4 | async-start | bytes 1048576 | tf_op jit(solution)/shard_map/all_to_all | solution.py:503
  113.2 2.0 %collective-permute-start.26 = (bf16[4,128,256]{2,1,0:T(8,128)(2,1)S(1)}, bf16[4,128,256]{2,1,0:T(8,128)(2,1)S(1)}, u32[]{:S(2)}, u32[]{:S(2)}) collective-permute-start(bf16[4,128,256]{2,1,0:T(8,128)(2,1)S(1)} %copy-done.23), channel_id=1, source_target_pairs={{0,6},{1,7},{2,4},{3,5},{4,2},{5,3},{6,0},{7,1},{8,14},{9,15},{10,... | collective-permute-start | bytes 786440 | tf_op jit(solution)/shard_map/ppermute | solution.py:473
  117.5 2.4 %collective-permute-start.18 = (bf16[128,256]{1,0:T(8,128)(2,1)}, bf16[128,256]{1,0:T(8,128)(2,1)S(1)}, u32[]{:S(2)}, u32[]{:S(2)}) collective-permute-start(bf16[128,256]{1,0:T(8,128)(2,1)} %get-tuple-element.92), channel_id=1, source_target_pairs={{0,16},{4,20},{8,24},{12,28},{16,0},{20,4},{24,8},{28,12},{1,17},{... | collective-permute-start | bytes 196616 | tf_op jit(solution)/shard_map/ppermute | solution.py:352
  119.8 3.9 %collective-permute-done.24.refs_0_ = bf16[4,128,256]{2,1,0:T(8,128)(2,1)S(1)} collective-permute-done((bf16[4,128,256]{2,1,0:T(8,128)(2,1)}, bf16[4,128,256]{2,1,0:T(8,128)(2,1)S(1)}, u32[]{:S(2)}, u32[]{:S(2)}) %collective-permute-start.24) | collective-permute-done | bytes 262176 | tf_op jit(solution)/shard_map/ppermute | solution.py:473
  123.8 2.4 %collective-permute-start.19 = (bf16[128,256]{1,0:T(8,128)(2,1)}, bf16[128,256]{1,0:T(8,128)(2,1)S(1)}, u32[]{:S(2)}, u32[]{:S(2)}) collective-permute-start(bf16[128,256]{1,0:T(8,128)(2,1)} %get-tuple-element.93), channel_id=1, source_target_pairs={{0,24},{4,28},{8,16},{12,20},{16,8},{20,12},{24,0},{28,4},{1,25},{... | collective-permute-start | bytes 196616 | tf_op jit(solution)/shard_map/ppermute | solution.py:352
  127.2 2.7 %collective-permute-start.28 = (bf16[128,256]{1,0:T(8,128)(2,1)}, bf16[128,256]{1,0:T(8,128)(2,1)S(1)}, u32[]{:S(2)}, u32[]{:S(2)}) collective-permute-start(bf16[128,256]{1,0:T(8,128)(2,1)} %get-tuple-element.109), channel_id=1, source_target_pairs={{0,16},{4,20},{8,24},{12,28},{16,0},{20,4},{24,8},{28,12},{1,17},{... | collective-permute-start | bytes 196616 | tf_op jit(solution)/shard_map/ppermute | solution.py:352
  131.3 3.8 %collective-permute-done.18 = bf16[128,256]{1,0:T(8,128)(2,1)S(1)} collective-permute-done((bf16[128,256]{1,0:T(8,128)(2,1)}, bf16[128,256]{1,0:T(8,128)(2,1)S(1)}, u32[]{:S(2)}, u32[]{:S(2)}) %collective-permute-start.18) | collective-permute-done | bytes 65568 | tf_op jit(solution)/shard_map/ppermute | solution.py:352
  (114 shorter events, 40.2 us)
Async XLA Ops:
  4.8 29.0 %all-to-all-start = ((bf16[8,272,128]{2,1,0:T(8,128)(2,1)}), bf16[8,272,128]{2,1,0:T(8,128)(2,1)S(1)}, u32[]{:S(2)}, u32[]{:S(2)}) async-start(bf16[8,272,128]{2,1,0:T(8,128)(2,1)} %shard_map.112), calls=%async_computation | async-start | bytes 1114112 | tf_op jit(solution)/shard_map/all_to_all | solution.py:503
  13.5 32.1 %collective-permute-start.7 = (bf16[2,256,1024]{2,1,0:T(8,128)(2,1)S(1)}, bf16[2,256,1024]{2,1,0:T(8,128)(2,1)S(1)}, u32[]{:S(2)}, u32[]{:S(2)}) collective-permute-start(bf16[2,256,1024]{2,1,0:T(8,128)(2,1)S(1)} %pad_maximum_fusion.refs_0_), channel_id=1, source_target_pairs={{0,2},{1,3},{2,0},{3,1},{4,6},{5,7},{6,4},{7,5},{8,10},{9,11},{10,... | collective-permute-start | bytes 3145736 | tf_op jit(solution)/shard_map/ppermute | solution.py:352
  19.6 8.3 %collective-permute-start.2 = (bf16[256,128]{1,0:T(8,128)(2,1)}, bf16[256,128]{1,0:T(8,128)(2,1)S(1)}, u32[]{:S(2)}, u32[]{:S(2)}) collective-permute-start(bf16[256,128]{1,0:T(8,128)(2,1)} %get-tuple-element.61), channel_id=1, source_target_pairs={{0,12},{4,8},{8,4},{12,0},{16,28},{20,24},{24,20},{28,16},{1,13},{... | collective-permute-start | bytes 196616 | tf_op jit(solution)/shard_map/ppermute | solution.py:352
  19.6 21.3 %collective-permute-start.3 = (bf16[256,128]{1,0:T(8,128)(2,1)}, bf16[256,128]{1,0:T(8,128)(2,1)S(1)}, u32[]{:S(2)}, u32[]{:S(2)}) collective-permute-start(bf16[256,128]{1,0:T(8,128)(2,1)} %get-tuple-element.62), channel_id=1, source_target_pairs={{0,16},{4,20},{8,24},{12,28},{16,0},{20,4},{24,8},{28,12},{1,17},{... | collective-permute-start | bytes 196616 | tf_op jit(solution)/shard_map/ppermute | solution.py:352
  22.5 18.4 %collective-permute-start.4 = (bf16[256,128]{1,0:T(8,128)(2,1)}, bf16[256,128]{1,0:T(8,128)(2,1)S(1)}, u32[]{:S(2)}, u32[]{:S(2)}) collective-permute-start(bf16[256,128]{1,0:T(8,128)(2,1)} %get-tuple-element.63), channel_id=1, source_target_pairs={{0,20},{4,16},{8,28},{12,24},{16,4},{20,0},{24,12},{28,8},{1,21},{... | collective-permute-start | bytes 196616 | tf_op jit(solution)/shard_map/ppermute | solution.py:352
  25.0 16.5 %collective-permute-start.5 = (bf16[256,128]{1,0:T(8,128)(2,1)}, bf16[256,128]{1,0:T(8,128)(2,1)S(1)}, u32[]{:S(2)}, u32[]{:S(2)}) collective-permute-start(bf16[256,128]{1,0:T(8,128)(2,1)} %get-tuple-element.64), channel_id=1, source_target_pairs={{0,24},{4,28},{8,16},{12,20},{16,8},{20,12},{24,0},{28,4},{1,25},{... | collective-permute-start | bytes 196616 | tf_op jit(solution)/shard_map/ppermute | solution.py:352
  27.8 14.3 %collective-permute-start.6 = (bf16[256,128]{1,0:T(8,128)(2,1)}, bf16[256,128]{1,0:T(8,128)(2,1)S(1)}, u32[]{:S(2)}, u32[]{:S(2)}) collective-permute-start(bf16[256,128]{1,0:T(8,128)(2,1)} %get-tuple-element.65), channel_id=1, source_target_pairs={{0,28},{4,24},{8,20},{12,16},{16,12},{20,8},{24,4},{28,0},{1,29},{... | collective-permute-start | bytes 196616 | tf_op jit(solution)/shard_map/ppermute | solution.py:352
  42.8 19.1 %all-to-all-start.1 = ((bf16[32,32,256]{2,1,0:T(8,128)(2,1)}), bf16[32,32,256]{2,1,0:T(8,128)(2,1)S(1)}, u32[]{:S(2)}, u32[]{:S(2)}) async-start(bf16[32,32,256]{2,1,0:T(8,128)(2,1)} %get-tuple-element.70), calls=%async_computation.1 | async-start | bytes 1048576 | tf_op jit(solution)/shard_map/all_to_all | solution.py:503
  45.5 19.0 %collective-permute-start.8 = (bf16[2,256,1024]{2,1,0:T(8,128)(2,1)S(1)}, bf16[2,256,1024]{2,1,0:T(8,128)(2,1)}, u32[]{:S(2)}, u32[]{:S(2)}) collective-permute-start(bf16[2,256,1024]{2,1,0:T(8,128)(2,1)S(1)} %pad_maximum_fusion.refs_0_), channel_id=1, source_target_pairs={{0,1},{1,0},{2,3},{3,2},{4,5},{5,4},{6,7},{7,6},{8,9},{9,8},{10,11... | collective-permute-start | bytes 3145736 | tf_op jit(solution)/shard_map/ppermute | solution.py:352
  45.7 18.8 %collective-permute-start.9 = (bf16[2,256,1024]{2,1,0:T(8,128)(2,1)S(1)}, bf16[2,256,1024]{2,1,0:T(8,128)(2,1)}, u32[]{:S(2)}, u32[]{:S(2)}) collective-permute-start(bf16[2,256,1024]{2,1,0:T(8,128)(2,1)S(1)} %collective-permute-done.7.refs_1_), channel_id=1, source_target_pairs={{0,1},{1,0},{2,3},{3,2},{4,5},{5,4},{6,7},{7,6},{8,9},{9,8},{10,11... | collective-permute-start | bytes 3145736 | tf_op jit(solution)/shard_map/ppermute | solution.py:352
  61.9 19.0 %all-to-all-start.2 = ((bf16[32,32,256]{2,1,0:T(8,128)(2,1)}), bf16[32,32,256]{2,1,0:T(8,128)(2,1)S(1)}, u32[]{:S(2)}, u32[]{:S(2)}) async-start(bf16[32,32,256]{2,1,0:T(8,128)(2,1)} %shard_map.115), calls=%async_computation.2 | async-start | bytes 1048576 | tf_op jit(solution)/shard_map/all_to_all | solution.py:503
  80.8 20.9 %all-to-all-start.3 = ((bf16[32,32,256]{2,1,0:T(8,128)(2,1)}), bf16[32,32,256]{2,1,0:T(8,128)(2,1)}, u32[]{:S(2)}, u32[]{:S(2)}) async-start(bf16[32,32,256]{2,1,0:T(8,128)(2,1)} %bitcast.26), calls=%async_computation.3 | async-start | bytes 1048576 | tf_op jit(solution)/shard_map/all_to_all | solution.py:503
  93.9 19.3 %collective-permute-start.14 = (bf16[4,128,256]{2,1,0:T(8,128)(2,1)}, bf16[4,128,256]{2,1,0:T(8,128)(2,1)S(1)}, u32[]{:S(2)}, u32[]{:S(2)}) collective-permute-start(bf16[4,128,256]{2,1,0:T(8,128)(2,1)} %get-tuple-element.83), channel_id=1, source_target_pairs={{0,4},{1,5},{2,6},{3,7},{4,0},{5,1},{6,2},{7,3},{8,12},{9,13},{10,... | collective-permute-start | bytes 786440 | tf_op jit(solution)/shard_map/ppermute | solution.py:473
  95.5 19.8 %collective-permute-start.15 = (bf16[4,128,256]{2,1,0:T(8,128)(2,1)}, bf16[4,128,256]{2,1,0:T(8,128)(2,1)S(1)}, u32[]{:S(2)}, u32[]{:S(2)}) collective-permute-start(bf16[4,128,256]{2,1,0:T(8,128)(2,1)} %get-tuple-element.84), channel_id=1, source_target_pairs={{0,2},{1,3},{2,0},{3,1},{4,6},{5,7},{6,4},{7,5},{8,10},{9,11},{10,... | collective-permute-start | bytes 786440 | tf_op jit(solution)/shard_map/ppermute | solution.py:473
  97.0 18.3 %collective-permute-start.16 = (bf16[4,128,256]{2,1,0:T(8,128)(2,1)}, bf16[4,128,256]{2,1,0:T(8,128)(2,1)S(1)}, u32[]{:S(2)}, u32[]{:S(2)}) collective-permute-start(bf16[4,128,256]{2,1,0:T(8,128)(2,1)} %get-tuple-element.85), channel_id=1, source_target_pairs={{0,6},{1,7},{2,4},{3,5},{4,2},{5,3},{6,0},{7,1},{8,14},{9,15},{10,... | collective-permute-start | bytes 786440 | tf_op jit(solution)/shard_map/ppermute | solution.py:473
  98.7 25.0 %collective-permute-start.24 = (bf16[4,128,256]{2,1,0:T(8,128)(2,1)}, bf16[4,128,256]{2,1,0:T(8,128)(2,1)S(1)}, u32[]{:S(2)}, u32[]{:S(2)}) collective-permute-start(bf16[4,128,256]{2,1,0:T(8,128)(2,1)} %get-tuple-element.100), channel_id=1, source_target_pairs={{0,4},{1,5},{2,6},{3,7},{4,0},{5,1},{6,2},{7,3},{8,12},{9,13},{10,... | collective-permute-start | bytes 786440 | tf_op jit(solution)/shard_map/ppermute | solution.py:473
  100.3 25.9 %collective-permute-start.25 = (bf16[4,128,256]{2,1,0:T(8,128)(2,1)}, bf16[4,128,256]{2,1,0:T(8,128)(2,1)S(1)}, u32[]{:S(2)}, u32[]{:S(2)}) collective-permute-start(bf16[4,128,256]{2,1,0:T(8,128)(2,1)} %get-tuple-element.101), channel_id=1, source_target_pairs={{0,2},{1,3},{2,0},{3,1},{4,6},{5,7},{6,4},{7,5},{8,10},{9,11},{10,... | collective-permute-start | bytes 786440 | tf_op jit(solution)/shard_map/ppermute | solution.py:473
  108.3 29.8 %all-to-all-start.4 = ((bf16[8,32,1024]{2,1,0:T(8,128)(2,1)}), bf16[8,32,1024]{2,1,0:T(8,128)(2,1)S(1)}, u32[]{:S(2)}, u32[]{:S(2)}) async-start(bf16[8,32,1024]{2,1,0:T(8,128)(2,1)} %shard_map.117), calls=%async_computation.4 | async-start | bytes 1048576 | tf_op jit(solution)/shard_map/all_to_all | solution.py:503
  113.2 12.9 %collective-permute-start.26 = (bf16[4,128,256]{2,1,0:T(8,128)(2,1)S(1)}, bf16[4,128,256]{2,1,0:T(8,128)(2,1)S(1)}, u32[]{:S(2)}, u32[]{:S(2)}) collective-permute-start(bf16[4,128,256]{2,1,0:T(8,128)(2,1)S(1)} %copy-done.23), channel_id=1, source_target_pairs={{0,6},{1,7},{2,4},{3,5},{4,2},{5,3},{6,0},{7,1},{8,14},{9,15},{10,... | collective-permute-start | bytes 786440 | tf_op jit(solution)/shard_map/ppermute | solution.py:473
  116.0 13.8 %collective-permute-start.17 = (bf16[128,256]{1,0:T(8,128)(2,1)}, bf16[128,256]{1,0:T(8,128)(2,1)S(1)}, u32[]{:S(2)}, u32[]{:S(2)}) collective-permute-start(bf16[128,256]{1,0:T(8,128)(2,1)} %get-tuple-element.91), channel_id=1, source_target_pairs={{0,8},{4,12},{8,0},{12,4},{16,24},{20,28},{24,16},{28,20},{1,9},{5... | collective-permute-start | bytes 196616 | tf_op jit(solution)/shard_map/ppermute | solution.py:352
  117.5 17.6 %collective-permute-start.18 = (bf16[128,256]{1,0:T(8,128)(2,1)}, bf16[128,256]{1,0:T(8,128)(2,1)S(1)}, u32[]{:S(2)}, u32[]{:S(2)}) collective-permute-start(bf16[128,256]{1,0:T(8,128)(2,1)} %get-tuple-element.92), channel_id=1, source_target_pairs={{0,16},{4,20},{8,24},{12,28},{16,0},{20,4},{24,8},{28,12},{1,17},{... | collective-permute-start | bytes 196616 | tf_op jit(solution)/shard_map/ppermute | solution.py:352
  123.8 11.4 %collective-permute-start.19 = (bf16[128,256]{1,0:T(8,128)(2,1)}, bf16[128,256]{1,0:T(8,128)(2,1)S(1)}, u32[]{:S(2)}, u32[]{:S(2)}) collective-permute-start(bf16[128,256]{1,0:T(8,128)(2,1)} %get-tuple-element.93), channel_id=1, source_target_pairs={{0,24},{4,28},{8,16},{12,20},{16,8},{20,12},{24,0},{28,4},{1,25},{... | collective-permute-start | bytes 196616 | tf_op jit(solution)/shard_map/ppermute | solution.py:352
  126.9 8.9 %collective-permute-start.27 = (bf16[128,256]{1,0:T(8,128)(2,1)}, bf16[128,256]{1,0:T(8,128)(2,1)S(1)}, u32[]{:S(2)}, u32[]{:S(2)}) collective-permute-start(bf16[128,256]{1,0:T(8,128)(2,1)} %get-tuple-element.108), channel_id=1, source_target_pairs={{0,8},{4,12},{8,0},{12,4},{16,24},{20,28},{24,16},{28,20},{1,9},{5... | collective-permute-start | bytes 196616 | tf_op jit(solution)/shard_map/ppermute | solution.py:352
  127.2 10.3 %collective-permute-start.28 = (bf16[128,256]{1,0:T(8,128)(2,1)}, bf16[128,256]{1,0:T(8,128)(2,1)S(1)}, u32[]{:S(2)}, u32[]{:S(2)}) collective-permute-start(bf16[128,256]{1,0:T(8,128)(2,1)} %get-tuple-element.109), channel_id=1, source_target_pairs={{0,16},{4,20},{8,24},{12,28},{16,0},{20,4},{24,8},{28,12},{1,17},{... | collective-permute-start | bytes 196616 | tf_op jit(solution)/shard_map/ppermute | solution.py:352
  (35 other events, 93.4 us)

commit v6 on v5

--- a/solution.py
+++ b/solution.py
@@ -29,7 +29,7 @@
         scratch_shapes=list(scratch),
         compiler_params=pltpu.CompilerParams(vmem_limit_bytes=limit * 1024 * 1024),
         cost_estimate=pl.CostEstimate(flops=flops, bytes_accessed=moved, transcendentals=0),
-    )(*[v for v in args])
+    )(*[pltpu.with_memory_space_constraint(v, pltpu.HBM) if spec is far else v for v, spec in zip(args, in_specs)])
 
 
 def after(values, *earlier):
@@ -60,7 +60,7 @@
         for n in range(nodes):
             o_ref[n, b * width : (b + 1) * width, :] = turned[n * width : (n + 1) * width]
     tile = meta_tile(
-        lambda p, c: ghosts[p : p + 1, c : c + 1], lambda r: degrees[r], slots_ref[...], tiles_ref[...], owners, held, size
+        lambda p, c: ghosts[c : c + 1, p : p + 1], lambda r: degrees[r], slots_ref[...], tiles_ref[...], owners, held, size
     )
     for n in range(nodes):
         o_ref[n, rows - meta_rows :, :] = tile
@@ -82,8 +82,8 @@
     return call(
         functools.partial(pack_kernel, owners, held),
         [((nodes, per * width + meta_rows, size), bf16)],
-        [vmem, smem, vmem, vmem, vmem],
-        (ghosts, degrees, slots, tile_ids, features),
+        [far, smem, far, far, far],
+        (ghosts.T, degrees, slots, tile_ids, features),
         sent=(0,),
     )[0]
 
@@ -111,7 +111,7 @@
     return call(
         turn_kernel,
         [((per * width, size), bf16)] * nodes,
-        [far],
+        [vmem],
         (values,),
         [pltpu.VMEM((per, values.shape[1], size), bf16)],
         sent=tuple(range(nodes)),
@@ -291,7 +291,7 @@
     out, ids, weight = call(
         functools.partial(first_kernel, per, width_k),
         [((feat_count * nodes, width, share * size), bf16), return_ids, ((count, size), f32)],
-        [far, far],
+        [vmem, vmem],
         (v, tiles),
         [
             pltpu.SMEM((count, size), jnp.int32),
@@ -300,7 +300,7 @@
         ],
         0,
         28,
-        sent=(0,),
+        sent=(0, 1, 2),
     )
     return out, (ids[0], ids[1], ids[2], weight)
 
@@ -317,7 +317,7 @@
     return call(
         functools.partial(back_spread_kernel, per, width_k, nodes),
         [((feat_count * nodes, width, share * size), bf16)],
-        [smem, smem, vmem, far] + [far] * nodes,
+        [smem, smem, vmem, vmem, vmem] + [far] * (nodes - 1),
         (pick_back, near, weight, tiles, *parts),
         [product_scratch(tiles, count, width)] + [pltpu.VMEM((count, width, size), f32)] * unroll,
         product_flops(tiles, count, width),
@@ -339,7 +339,7 @@
     return call(
         functools.partial(last_kernel, per, width_k),
         [((nodes, width, per * size), bf16)],
-        [smem, vmem, far, far],
+        [smem, vmem, vmem, vmem],
         (pick, weight, v, tiles),
         [pltpu.VMEM((count, width, size), bf16), product_scratch(tiles, count, width)],
         10 * product_flops(tiles, count, width),
@@ -480,7 +480,7 @@
     mine, *rest = call(
         split_kernel,
         [((tall, wide), f32)] + [((tall, wide), bf16)] * (half - 1),
-        [vmem] + [far] * len(came),
+        [vmem] * (1 + len(came)),
         (keep, *came),
         flops=flops,
         sent=tuple(range(1, half)),
@@ -519,11 +519,11 @@
     pre, hidden, wide_out = call(
         functools.partial(project_kernel, offsets),
         [((hidden_width, held), f32)] + [((hidden_width, held), bf16)] * 2,
-        [far] + [vmem] * parts,
+        [vmem] * (1 + parts),
         (agg, *weights),
         flops=4 * hidden_width * hidden_width * held,
         moved=4 << 20,
-        sent=(2,),
+        sent=(0, 2),
     )
     wide_out = after(wide_out, back)
     out_t = exchange(wide_out.reshape(feat_count * nodes, wide // nodes, held), every)
@@ -539,7 +539,7 @@
     *give_one, back_pre = call(
         functools.partial(back_kernel, offsets, evens),
         give_shapes(hidden_width) + [((hidden_width, held), bf16)],
-        [vmem] * (3 + parts),
+        [far] + [vmem] * (2 + parts),
         (pre, back, agg, *weights),
         sent=tuple(range(parts)),
     )

time: 140 us -> 137 us (0.979)
  local copies, waits for them, and re-layouts: 13.8 us -> 6.84 us
  waiting for transfers between devices: 27.1 us -> 29.5 us
    unnamed x49 -> x40, local copies, waits for them, and re-layouts: 12.3 us -> 5.42 us
    all_to_all x5, waiting for transfers between devices: 17.6 us -> 20.2 us  [on_device(): lax.all_to_all(v, axes, split_axis=0, concat_axis=0, tiled=True)]
  transfers between devices with their start and end apart: 35 -> 35, of which waited for: 6 -> 6; matrix products, arithmetic and copies ran while one was open for 1% -> 1% of each run, Pallas kernels for 26% -> 27%
where the time goes in v6:
time: 137 us; the launch traced here: 136 us
  starting transfers between devices  58.6 us (43%)
  Pallas kernels  38.5 us (28%)
  waiting for transfers between devices  29.5 us (22%)
  local copies, waits for them, and re-layouts  6.84 us (5%)
  other arithmetic  1.47 us (1%)
    pallas_call x12, Pallas kernels, call(): pl.pallas_call(body, out_shape=[(pltpu.HBM if i in sent else jax.ShapeDty...  38.5 us
    ppermute x24, starting transfers between devices, swap(): lax.ppermute(values, axis, [(i, i ^ mask) for i in range(lax.axis_size(ax...  29 us
    all_to_all x5, starting transfers between devices, on_device(): lax.all_to_all(v, axes, split_axis=0, concat_axis=0, tiled=True)  21 us
    all_to_all x5, waiting for transfers between devices, on_device(): lax.all_to_all(v, axes, split_axis=0, concat_axis=0, tiled=True)  20.2 us
    ppermute x6, starting transfers between devices, pass_quarters(): lax.ppermute(v, ('nodes', 'feat'), [(i, i ^ b * feat_count + o) for i in...  8.59 us
    unnamed x40, local copies, waits for them, and re-layouts  5.42 us
    ppermute x24, waiting for transfers between devices, swap(): lax.ppermute(values, axis, [(i, i ^ mask) for i in range(lax.axis_size(ax...  4.98 us
    ppermute x6, waiting for transfers between devices, pass_quarters(): lax.ppermute(v, ('nodes', 'feat'), [(i, i ^ b * feat_count + o) for i in...  4.33 us
  transfers between devices with their start and end apart: 35, of which 6 were waited for; matrix products, arithmetic and copies ran while one was open for 1% of the time, Pallas kernels for 27%

profile of v6, /device:TPU:0, one launch (start us, length us, event | category | flops | bytes accessed | tf_op | source)
XLA Modules:
  0.0 135.8 jit_solution(807584357179570462)
XLA Ops:
  1.3 2.2 %shard_map.112 = bf16[8,272,128]{2,1,0:T(8,128)(2,1)} custom-call(s32[2,8]{1,0:T(2,128)} %bitcast.29, s32[8]{0:T(128)S(1)} %copy-done.6, s32[8,24]{1,0:T(8,128)} %slots_ref.1, s32[8,24]{1,0:T(8,128)} %tiles_ref.4, bf16[1024,256]{1,0:T(8,128)(2,1)} %feat_ref.1), custom_call_target="tpu_custom_call" | custom-call | tf_op jit(solution)/shard_map/pallas_call | solution.py:24
  3.5 7.4 %all-to-all-start = ((bf16[8,272,128]{2,1,0:T(8,128)(2,1)}), bf16[8,272,128]{2,1,0:T(8,128)(2,1)S(1)}, u32[]{:S(2)}, u32[]{:S(2)}) async-start(bf16[8,272,128]{2,1,0:T(8,128)(2,1)} %shard_map.112), calls=%async_computation | async-start | bytes 1114112 | tf_op jit(solution)/shard_map/all_to_all | solution.py:503
  18.3 2.9 %collective-permute-start.3 = (bf16[256,128]{1,0:T(8,128)(2,1)}, bf16[256,128]{1,0:T(8,128)(2,1)S(1)}, u32[]{:S(2)}, u32[]{:S(2)}) collective-permute-start(bf16[256,128]{1,0:T(8,128)(2,1)} %get-tuple-element.62), channel_id=1, source_target_pairs={{0,16},{4,20},{8,24},{12,28},{16,0},{20,4},{24,8},{28,12},{1,17},{... | collective-permute-start | bytes 196616 | tf_op jit(solution)/shard_map/ppermute | solution.py:352
  21.2 2.5 %collective-permute-start.4 = (bf16[256,128]{1,0:T(8,128)(2,1)}, bf16[256,128]{1,0:T(8,128)(2,1)S(1)}, u32[]{:S(2)}, u32[]{:S(2)}) collective-permute-start(bf16[256,128]{1,0:T(8,128)(2,1)} %get-tuple-element.63), channel_id=1, source_target_pairs={{0,20},{4,16},{8,28},{12,24},{16,4},{20,0},{24,12},{28,8},{1,21},{... | collective-permute-start | bytes 196616 | tf_op jit(solution)/shard_map/ppermute | solution.py:352
  23.7 2.8 %collective-permute-start.5 = (bf16[256,128]{1,0:T(8,128)(2,1)}, bf16[256,128]{1,0:T(8,128)(2,1)S(1)}, u32[]{:S(2)}, u32[]{:S(2)}) collective-permute-start(bf16[256,128]{1,0:T(8,128)(2,1)} %get-tuple-element.64), channel_id=1, source_target_pairs={{0,24},{4,28},{8,16},{12,20},{16,8},{20,12},{24,0},{28,4},{1,25},{... | collective-permute-start | bytes 196616 | tf_op jit(solution)/shard_map/ppermute | solution.py:352
  26.5 2.3 %collective-permute-start.6 = (bf16[256,128]{1,0:T(8,128)(2,1)}, bf16[256,128]{1,0:T(8,128)(2,1)S(1)}, u32[]{:S(2)}, u32[]{:S(2)}) collective-permute-start(bf16[256,128]{1,0:T(8,128)(2,1)} %get-tuple-element.65), channel_id=1, source_target_pairs={{0,28},{4,24},{8,20},{12,16},{16,12},{20,8},{24,4},{28,0},{1,29},{... | collective-permute-start | bytes 196616 | tf_op jit(solution)/shard_map/ppermute | solution.py:352
  28.9 3.5 %all-to-all-done.v_ref = bf16[8,272,128]{2,1,0:T(8,128)(2,1)S(1)} async-done(((bf16[8,272,128]{2,1,0:T(8,128)(2,1)}), bf16[8,272,128]{2,1,0:T(8,128)(2,1)S(1)}, u32[]{:S(2)}, u32[]{:S(2)}) %all-to-all-start) | async-done | bytes 557088 | tf_op jit(solution)/shard_map/all_to_all | solution.py:503
  33.5 5.5 %shard_map.114 = (bf16[32,32,256]{2,1,0:T(8,128)(2,1)}, s32[3,64,128]{2,1,0:T(8,128)}, f32[64,128]{1,0:T(8,128)}) custom-call(bf16[8,272,128]{2,1,0:T(8,128)(2,1)S(1)} %all-to-all-done.v_ref, bf16[16,128,128]{2,1,0:T(8,128)(2,1)S(1)} %copy-done.3), custom_call_target="tpu_custom_call" | custom-call | tf_op jit(solution)/shard_map/pallas_call | solution.py:24
  40.3 2.7 %all-to-all-start.1 = ((bf16[32,32,256]{2,1,0:T(8,128)(2,1)}), bf16[32,32,256]{2,1,0:T(8,128)(2,1)S(1)}, u32[]{:S(2)}, u32[]{:S(2)}) async-start(bf16[32,32,256]{2,1,0:T(8,128)(2,1)} %get-tuple-element.70), calls=%async_computation.1 | async-start | bytes 1048576 | tf_op jit(solution)/shard_map/all_to_all | solution.py:503
  44.5 9.9 %shard_map.115 = bf16[32,32,256]{2,1,0:T(8,128)(2,1)} custom-call(s32[64,128]{1,0:T(8,128)S(1)} %get-tuple-element.112.pick, s32[64,128]{1,0:T(8,128)S(1)} %get-tuple-element.111.near, f32[64,128]{1,0:T(8,128)S(1)} %copy-done.8, bf16[16,128,128]{2,1,0:T(8,128)(2,1)S(1)} %copy-done.4, bf16[256,128]{1,0:T(8,128)(2,1)S(1)} %copy-done.7, ...), custom_call_target="tpu_custom_call" | custom-call | flops 1073741824 | bytes 4194304 | tf_op jit(solution)/shard_map/pallas_call | solution.py:24
  54.4 5.1 %all-to-all-done.1 = bf16[32,32,256]{2,1,0:T(8,128)(2,1)S(1)} async-done(((bf16[32,32,256]{2,1,0:T(8,128)(2,1)}), bf16[32,32,256]{2,1,0:T(8,128)(2,1)S(1)}, u32[]{:S(2)}, u32[]{:S(2)}) %all-to-all-start.1) | async-done | bytes 524320 | tf_op jit(solution)/shard_map/all_to_all | solution.py:503
  59.4 2.6 %all-to-all-start.2 = ((bf16[32,32,256]{2,1,0:T(8,128)(2,1)}), bf16[32,32,256]{2,1,0:T(8,128)(2,1)S(1)}, u32[]{:S(2)}, u32[]{:S(2)}) async-start(bf16[32,32,256]{2,1,0:T(8,128)(2,1)} %shard_map.115), calls=%async_computation.2 | async-start | bytes 1048576 | tf_op jit(solution)/shard_map/all_to_all | solution.py:503
  62.1 3.9 %shard_map.116 = (f32[1024,256]{1,0:T(8,128)}, bf16[1024,256]{1,0:T(8,128)(2,1)S(1)}, bf16[1024,256]{1,0:T(8,128)(2,1)}) custom-call(bf16[1024,256]{1,0:T(8,128)(2,1)S(1)} %bitcast.18, bf16[2,256,1024]{2,1,0:T(8,128)(2,1)S(1)} %pad_maximum_fusion.refs_0_, bf16[2,256,1024]{2,1,0:T(8,128)(2,1)S(1)} %collective-permute-done.7.refs_1_, ...), custom_call_target="tpu_custom_call" | custom-call | flops 1073741824 | bytes 4194304 | tf_op jit(solution)/shard_map/pallas_call | solution.py:24
  66.8 11.6 %all-to-all-done.2 = bf16[32,32,256]{2,1,0:T(8,128)(2,1)S(1)} async-done(((bf16[32,32,256]{2,1,0:T(8,128)(2,1)}), bf16[32,32,256]{2,1,0:T(8,128)(2,1)S(1)}, u32[]{:S(2)}, u32[]{:S(2)}) %all-to-all-start.2) | async-done | bytes 524320 | tf_op jit(solution)/shard_map/all_to_all | solution.py:503
  78.4 3.3 %all-to-all-start.3 = ((bf16[32,32,256]{2,1,0:T(8,128)(2,1)}), bf16[32,32,256]{2,1,0:T(8,128)(2,1)}, u32[]{:S(2)}, u32[]{:S(2)}) async-start(bf16[32,32,256]{2,1,0:T(8,128)(2,1)} %bitcast.27), calls=%async_computation.3 | async-start | bytes 1048576 | tf_op jit(solution)/shard_map/all_to_all | solution.py:503
  81.8 4.2 %shard_map.118 = (bf16[4,128,256]{2,1,0:T(8,128)(2,1)}, bf16[4,128,256]{2,1,0:T(8,128)(2,1)}, bf16[4,128,256]{2,1,0:T(8,128)(2,1)}, bf16[4,128,256]{2,1,0:T(8,128)(2,1)}, bf16[1024,256]{1,0:T(8,128)(2,1)S(1)}) custom-call(f32[1024,256]{1,0:T(8,128)} %get-tuple-element.76.pre_ref, bf16[1024,256]{1,0:T(8,128)(2,1)S(1)} %bitcast.21, ...), custom_call_target="tpu_custom_call" | custom-call | tf_op jit(solution)/shard_map/pallas_call | solution.py:24
  98.5 6.6 %shard_map.117 = bf16[8,32,1024]{2,1,0:T(8,128)(2,1)} custom-call(s32[64,128]{1,0:T(8,128)S(1)} %get-tuple-element.113.pick, f32[64,128]{1,0:T(8,128)S(1)} %copy-done.8, bf16[32,32,256]{2,1,0:T(8,128)(2,1)} %all-to-all-done.3.v_ref, bf16[16,128,128]{2,1,0:T(8,128)(2,1)S(1)} %copy-done.5), custom_call_target="tpu_custom_call" | custom-call | flops 10737418240 | tf_op jit(solution)/shard_map/pallas_call | solution.py:24
  105.0 4.9 %all-to-all-start.4 = ((bf16[8,32,1024]{2,1,0:T(8,128)(2,1)}), bf16[8,32,1024]{2,1,0:T(8,128)(2,1)S(1)}, u32[]{:S(2)}, u32[]{:S(2)}) async-start(bf16[8,32,1024]{2,1,0:T(8,128)(2,1)} %shard_map.117), calls=%async_computation.4 | async-start | bytes 1048576 | tf_op jit(solution)/shard_map/all_to_all | solution.py:503
  109.9 2.1 %collective-permute-start.26 = (bf16[4,128,256]{2,1,0:T(8,128)(2,1)S(1)}, bf16[4,128,256]{2,1,0:T(8,128)(2,1)S(1)}, u32[]{:S(2)}, u32[]{:S(2)}) collective-permute-start(bf16[4,128,256]{2,1,0:T(8,128)(2,1)S(1)} %copy-done.12), channel_id=1, source_target_pairs={{0,6},{1,7},{2,4},{3,5},{4,2},{5,3},{6,0},{7,1},{8,14},{9,15},{10,... | collective-permute-start | bytes 786440 | tf_op jit(solution)/shard_map/ppermute | solution.py:473
  114.2 2.4 %collective-permute-start.18 = (bf16[128,256]{1,0:T(8,128)(2,1)}, bf16[128,256]{1,0:T(8,128)(2,1)S(1)}, u32[]{:S(2)}, u32[]{:S(2)}) collective-permute-start(bf16[128,256]{1,0:T(8,128)(2,1)} %get-tuple-element.92), channel_id=1, source_target_pairs={{0,16},{4,20},{8,24},{12,28},{16,0},{20,4},{24,8},{28,12},{1,17},{... | collective-permute-start | bytes 196616 | tf_op jit(solution)/shard_map/ppermute | solution.py:352
  116.6 4.3 %collective-permute-done.24.refs_0_ = bf16[4,128,256]{2,1,0:T(8,128)(2,1)S(1)} collective-permute-done((bf16[4,128,256]{2,1,0:T(8,128)(2,1)}, bf16[4,128,256]{2,1,0:T(8,128)(2,1)S(1)}, u32[]{:S(2)}, u32[]{:S(2)}) %collective-permute-start.24) | collective-permute-done | bytes 262176 | tf_op jit(solution)/shard_map/ppermute | solution.py:473
  120.9 2.5 %collective-permute-start.19 = (bf16[128,256]{1,0:T(8,128)(2,1)}, bf16[128,256]{1,0:T(8,128)(2,1)S(1)}, u32[]{:S(2)}, u32[]{:S(2)}) collective-permute-start(bf16[128,256]{1,0:T(8,128)(2,1)} %get-tuple-element.93), channel_id=1, source_target_pairs={{0,24},{4,28},{8,16},{12,20},{16,8},{20,12},{24,0},{28,4},{1,25},{... | collective-permute-start | bytes 196616 | tf_op jit(solution)/shard_map/ppermute | solution.py:352
  124.1 2.4 %collective-permute-start.28 = (bf16[128,256]{1,0:T(8,128)(2,1)}, bf16[128,256]{1,0:T(8,128)(2,1)S(1)}, u32[]{:S(2)}, u32[]{:S(2)}) collective-permute-start(bf16[128,256]{1,0:T(8,128)(2,1)} %get-tuple-element.109), channel_id=1, source_target_pairs={{0,16},{4,20},{8,24},{12,28},{16,0},{20,4},{24,8},{28,12},{1,17},{... | collective-permute-start | bytes 196616 | tf_op jit(solution)/shard_map/ppermute | solution.py:352
  128.5 3.3 %collective-permute-done.18 = bf16[128,256]{1,0:T(8,128)(2,1)S(1)} collective-permute-done((bf16[128,256]{1,0:T(8,128)(2,1)}, bf16[128,256]{1,0:T(8,128)(2,1)S(1)}, u32[]{:S(2)}, u32[]{:S(2)}) %collective-permute-start.18) | collective-permute-done | bytes 65568 | tf_op jit(solution)/shard_map/ppermute | solution.py:352
  (105 shorter events, 34.0 us)
Async XLA Ops:
  3.5 29.0 %all-to-all-start = ((bf16[8,272,128]{2,1,0:T(8,128)(2,1)}), bf16[8,272,128]{2,1,0:T(8,128)(2,1)S(1)}, u32[]{:S(2)}, u32[]{:S(2)}) async-start(bf16[8,272,128]{2,1,0:T(8,128)(2,1)} %shard_map.112), calls=%async_computation | async-start | bytes 1114112 | tf_op jit(solution)/shard_map/all_to_all | solution.py:503
  12.2 31.0 %collective-permute-start.7 = (bf16[2,256,1024]{2,1,0:T(8,128)(2,1)S(1)}, bf16[2,256,1024]{2,1,0:T(8,128)(2,1)S(1)}, u32[]{:S(2)}, u32[]{:S(2)}) collective-permute-start(bf16[2,256,1024]{2,1,0:T(8,128)(2,1)S(1)} %pad_maximum_fusion.refs_0_), channel_id=1, source_target_pairs={{0,2},{1,3},{2,0},{3,1},{4,6},{5,7},{6,4},{7,5},{8,10},{9,11},{10,... | collective-permute-start | bytes 3145736 | tf_op jit(solution)/shard_map/ppermute | solution.py:352
  18.2 8.3 %collective-permute-start.2 = (bf16[256,128]{1,0:T(8,128)(2,1)}, bf16[256,128]{1,0:T(8,128)(2,1)S(1)}, u32[]{:S(2)}, u32[]{:S(2)}) collective-permute-start(bf16[256,128]{1,0:T(8,128)(2,1)} %get-tuple-element.61), channel_id=1, source_target_pairs={{0,12},{4,8},{8,4},{12,0},{16,28},{20,24},{24,20},{28,16},{1,13},{... | collective-permute-start | bytes 196616 | tf_op jit(solution)/shard_map/ppermute | solution.py:352
  18.3 20.8 %collective-permute-start.3 = (bf16[256,128]{1,0:T(8,128)(2,1)}, bf16[256,128]{1,0:T(8,128)(2,1)S(1)}, u32[]{:S(2)}, u32[]{:S(2)}) collective-permute-start(bf16[256,128]{1,0:T(8,128)(2,1)} %get-tuple-element.62), channel_id=1, source_target_pairs={{0,16},{4,20},{8,24},{12,28},{16,0},{20,4},{24,8},{28,12},{1,17},{... | collective-permute-start | bytes 196616 | tf_op jit(solution)/shard_map/ppermute | solution.py:352
  21.2 17.9 %collective-permute-start.4 = (bf16[256,128]{1,0:T(8,128)(2,1)}, bf16[256,128]{1,0:T(8,128)(2,1)S(1)}, u32[]{:S(2)}, u32[]{:S(2)}) collective-permute-start(bf16[256,128]{1,0:T(8,128)(2,1)} %get-tuple-element.63), channel_id=1, source_target_pairs={{0,20},{4,16},{8,28},{12,24},{16,4},{20,0},{24,12},{28,8},{1,21},{... | collective-permute-start | bytes 196616 | tf_op jit(solution)/shard_map/ppermute | solution.py:352
  23.7 15.4 %collective-permute-start.5 = (bf16[256,128]{1,0:T(8,128)(2,1)}, bf16[256,128]{1,0:T(8,128)(2,1)S(1)}, u32[]{:S(2)}, u32[]{:S(2)}) collective-permute-start(bf16[256,128]{1,0:T(8,128)(2,1)} %get-tuple-element.64), channel_id=1, source_target_pairs={{0,24},{4,28},{8,16},{12,20},{16,8},{20,12},{24,0},{28,4},{1,25},{... | collective-permute-start | bytes 196616 | tf_op jit(solution)/shard_map/ppermute | solution.py:352
  26.5 12.6 %collective-permute-start.6 = (bf16[256,128]{1,0:T(8,128)(2,1)}, bf16[256,128]{1,0:T(8,128)(2,1)S(1)}, u32[]{:S(2)}, u32[]{:S(2)}) collective-permute-start(bf16[256,128]{1,0:T(8,128)(2,1)} %get-tuple-element.65), channel_id=1, source_target_pairs={{0,28},{4,24},{8,20},{12,16},{16,12},{20,8},{24,4},{28,0},{1,29},{... | collective-permute-start | bytes 196616 | tf_op jit(solution)/shard_map/ppermute | solution.py:352
  40.3 19.1 %all-to-all-start.1 = ((bf16[32,32,256]{2,1,0:T(8,128)(2,1)}), bf16[32,32,256]{2,1,0:T(8,128)(2,1)S(1)}, u32[]{:S(2)}, u32[]{:S(2)}) async-start(bf16[32,32,256]{2,1,0:T(8,128)(2,1)} %get-tuple-element.70), calls=%async_computation.1 | async-start | bytes 1048576 | tf_op jit(solution)/shard_map/all_to_all | solution.py:503
  43.1 19.0 %collective-permute-start.8 = (bf16[2,256,1024]{2,1,0:T(8,128)(2,1)S(1)}, bf16[2,256,1024]{2,1,0:T(8,128)(2,1)}, u32[]{:S(2)}, u32[]{:S(2)}) collective-permute-start(bf16[2,256,1024]{2,1,0:T(8,128)(2,1)S(1)} %pad_maximum_fusion.refs_0_), channel_id=1, source_target_pairs={{0,1},{1,0},{2,3},{3,2},{4,5},{5,4},{6,7},{7,6},{8,9},{9,8},{10,11... | collective-permute-start | bytes 3145736 | tf_op jit(solution)/shard_map/ppermute | solution.py:352
  43.3 18.8 %collective-permute-start.9 = (bf16[2,256,1024]{2,1,0:T(8,128)(2,1)S(1)}, bf16[2,256,1024]{2,1,0:T(8,128)(2,1)}, u32[]{:S(2)}, u32[]{:S(2)}) collective-permute-start(bf16[2,256,1024]{2,1,0:T(8,128)(2,1)S(1)} %collective-permute-done.7.refs_1_), channel_id=1, source_target_pairs={{0,1},{1,0},{2,3},{3,2},{4,5},{5,4},{6,7},{7,6},{8,9},{9,8},{10,11... | collective-permute-start | bytes 3145736 | tf_op jit(solution)/shard_map/ppermute | solution.py:352
  59.4 19.0 %all-to-all-start.2 = ((bf16[32,32,256]{2,1,0:T(8,128)(2,1)}), bf16[32,32,256]{2,1,0:T(8,128)(2,1)S(1)}, u32[]{:S(2)}, u32[]{:S(2)}) async-start(bf16[32,32,256]{2,1,0:T(8,128)(2,1)} %shard_map.115), calls=%async_computation.2 | async-start | bytes 1048576 | tf_op jit(solution)/shard_map/all_to_all | solution.py:503
  78.4 20.1 %all-to-all-start.3 = ((bf16[32,32,256]{2,1,0:T(8,128)(2,1)}), bf16[32,32,256]{2,1,0:T(8,128)(2,1)}, u32[]{:S(2)}, u32[]{:S(2)}) async-start(bf16[32,32,256]{2,1,0:T(8,128)(2,1)} %bitcast.27), calls=%async_computation.3 | async-start | bytes 1048576 | tf_op jit(solution)/shard_map/all_to_all | solution.py:503
  90.7 19.3 %collective-permute-start.14 = (bf16[4,128,256]{2,1,0:T(8,128)(2,1)}, bf16[4,128,256]{2,1,0:T(8,128)(2,1)S(1)}, u32[]{:S(2)}, u32[]{:S(2)}) collective-permute-start(bf16[4,128,256]{2,1,0:T(8,128)(2,1)} %get-tuple-element.83), channel_id=1, source_target_pairs={{0,4},{1,5},{2,6},{3,7},{4,0},{5,1},{6,2},{7,3},{8,12},{9,13},{10,... | collective-permute-start | bytes 786440 | tf_op jit(solution)/shard_map/ppermute | solution.py:473
  92.2 19.8 %collective-permute-start.15 = (bf16[4,128,256]{2,1,0:T(8,128)(2,1)}, bf16[4,128,256]{2,1,0:T(8,128)(2,1)S(1)}, u32[]{:S(2)}, u32[]{:S(2)}) collective-permute-start(bf16[4,128,256]{2,1,0:T(8,128)(2,1)} %get-tuple-element.84), channel_id=1, source_target_pairs={{0,2},{1,3},{2,0},{3,1},{4,6},{5,7},{6,4},{7,5},{8,10},{9,11},{10,... | collective-permute-start | bytes 786440 | tf_op jit(solution)/shard_map/ppermute | solution.py:473
  93.7 18.3 %collective-permute-start.16 = (bf16[4,128,256]{2,1,0:T(8,128)(2,1)}, bf16[4,128,256]{2,1,0:T(8,128)(2,1)S(1)}, u32[]{:S(2)}, u32[]{:S(2)}) collective-permute-start(bf16[4,128,256]{2,1,0:T(8,128)(2,1)} %get-tuple-element.85), channel_id=1, source_target_pairs={{0,6},{1,7},{2,4},{3,5},{4,2},{5,3},{6,0},{7,1},{8,14},{9,15},{10,... | collective-permute-start | bytes 786440 | tf_op jit(solution)/shard_map/ppermute | solution.py:473
  95.4 25.4 %collective-permute-start.24 = (bf16[4,128,256]{2,1,0:T(8,128)(2,1)}, bf16[4,128,256]{2,1,0:T(8,128)(2,1)S(1)}, u32[]{:S(2)}, u32[]{:S(2)}) collective-permute-start(bf16[4,128,256]{2,1,0:T(8,128)(2,1)} %get-tuple-element.100), channel_id=1, source_target_pairs={{0,4},{1,5},{2,6},{3,7},{4,0},{5,1},{6,2},{7,3},{8,12},{9,13},{10,... | collective-permute-start | bytes 786440 | tf_op jit(solution)/shard_map/ppermute | solution.py:473
  97.0 26.4 %collective-permute-start.25 = (bf16[4,128,256]{2,1,0:T(8,128)(2,1)}, bf16[4,128,256]{2,1,0:T(8,128)(2,1)S(1)}, u32[]{:S(2)}, u32[]{:S(2)}) collective-permute-start(bf16[4,128,256]{2,1,0:T(8,128)(2,1)} %get-tuple-element.101), channel_id=1, source_target_pairs={{0,2},{1,3},{2,0},{3,1},{4,6},{5,7},{6,4},{7,5},{8,10},{9,11},{10,... | collective-permute-start | bytes 786440 | tf_op jit(solution)/shard_map/ppermute | solution.py:473
  105.0 29.7 %all-to-all-start.4 = ((bf16[8,32,1024]{2,1,0:T(8,128)(2,1)}), bf16[8,32,1024]{2,1,0:T(8,128)(2,1)S(1)}, u32[]{:S(2)}, u32[]{:S(2)}) async-start(bf16[8,32,1024]{2,1,0:T(8,128)(2,1)} %shard_map.117), calls=%async_computation.4 | async-start | bytes 1048576 | tf_op jit(solution)/shard_map/all_to_all | solution.py:503
  109.9 13.4 %collective-permute-start.26 = (bf16[4,128,256]{2,1,0:T(8,128)(2,1)S(1)}, bf16[4,128,256]{2,1,0:T(8,128)(2,1)S(1)}, u32[]{:S(2)}, u32[]{:S(2)}) collective-permute-start(bf16[4,128,256]{2,1,0:T(8,128)(2,1)S(1)} %copy-done.12), channel_id=1, source_target_pairs={{0,6},{1,7},{2,4},{3,5},{4,2},{5,3},{6,0},{7,1},{8,14},{9,15},{10,... | collective-permute-start | bytes 786440 | tf_op jit(solution)/shard_map/ppermute | solution.py:473
  112.7 13.8 %collective-permute-start.17 = (bf16[128,256]{1,0:T(8,128)(2,1)}, bf16[128,256]{1,0:T(8,128)(2,1)S(1)}, u32[]{:S(2)}, u32[]{:S(2)}) collective-permute-start(bf16[128,256]{1,0:T(8,128)(2,1)} %get-tuple-element.91), channel_id=1, source_target_pairs={{0,8},{4,12},{8,0},{12,4},{16,24},{20,28},{24,16},{28,20},{1,9},{5... | collective-permute-start | bytes 196616 | tf_op jit(solution)/shard_map/ppermute | solution.py:352
  114.2 17.6 %collective-permute-start.18 = (bf16[128,256]{1,0:T(8,128)(2,1)}, bf16[128,256]{1,0:T(8,128)(2,1)S(1)}, u32[]{:S(2)}, u32[]{:S(2)}) collective-permute-start(bf16[128,256]{1,0:T(8,128)(2,1)} %get-tuple-element.92), channel_id=1, source_target_pairs={{0,16},{4,20},{8,24},{12,28},{16,0},{20,4},{24,8},{28,12},{1,17},{... | collective-permute-start | bytes 196616 | tf_op jit(solution)/shard_map/ppermute | solution.py:352
  120.9 10.9 %collective-permute-start.19 = (bf16[128,256]{1,0:T(8,128)(2,1)}, bf16[128,256]{1,0:T(8,128)(2,1)S(1)}, u32[]{:S(2)}, u32[]{:S(2)}) collective-permute-start(bf16[128,256]{1,0:T(8,128)(2,1)} %get-tuple-element.93), channel_id=1, source_target_pairs={{0,24},{4,28},{8,16},{12,20},{16,8},{20,12},{24,0},{28,4},{1,25},{... | collective-permute-start | bytes 196616 | tf_op jit(solution)/shard_map/ppermute | solution.py:352
  124.1 8.4 %collective-permute-start.27 = (bf16[128,256]{1,0:T(8,128)(2,1)}, bf16[128,256]{1,0:T(8,128)(2,1)S(1)}, u32[]{:S(2)}, u32[]{:S(2)}) collective-permute-start(bf16[128,256]{1,0:T(8,128)(2,1)} %get-tuple-element.108), channel_id=1, source_target_pairs={{0,8},{4,12},{8,0},{12,4},{16,24},{20,28},{24,16},{28,20},{1,9},{5... | collective-permute-start | bytes 196616 | tf_op jit(solution)/shard_map/ppermute | solution.py:352
  124.1 10.0 %collective-permute-start.28 = (bf16[128,256]{1,0:T(8,128)(2,1)}, bf16[128,256]{1,0:T(8,128)(2,1)S(1)}, u32[]{:S(2)}, u32[]{:S(2)}) collective-permute-start(bf16[128,256]{1,0:T(8,128)(2,1)} %get-tuple-element.109), channel_id=1, source_target_pairs={{0,16},{4,20},{8,24},{12,28},{16,0},{20,4},{24,8},{28,12},{1,17},{... | collective-permute-start | bytes 196616 | tf_op jit(solution)/shard_map/ppermute | solution.py:352
  (31 other events, 136.0 us)

commit v7 on v6

--- a/solution.py
+++ b/solution.py
@@ -8,7 +8,7 @@
 from jax.sharding import PartitionSpec as P
 
 unroll = 4
-tile_step = 4
+tile_step = 8
 meta_rows = 16
 bf16, f32 = jnp.bfloat16, jnp.float32
 vmem = pl.BlockSpec(memory_space=pltpu.VMEM)
@@ -83,7 +83,7 @@
         functools.partial(pack_kernel, owners, held),
         [((nodes, per * width + meta_rows, size), bf16)],
         [far, smem, far, far, far],
-        (ghosts.T, degrees, slots, tile_ids, features),
+        (ghosts.T, pltpu.with_memory_space_constraint(degrees, pltpu.HBM), slots, tile_ids, features),
         sent=(0,),
     )[0]
 
@@ -291,7 +291,7 @@
     out, ids, weight = call(
         functools.partial(first_kernel, per, width_k),
         [((feat_count * nodes, width, share * size), bf16), return_ids, ((count, size), f32)],
-        [vmem, vmem],
+        [far, vmem],
         (v, tiles),
         [
             pltpu.SMEM((count, size), jnp.int32),

time: 137 us -> 135 us (0.985)
  local copies, waits for them, and re-layouts: 6.84 us -> 5.18 us
    unnamed x40 -> x36, local copies, waits for them, and re-layouts: 5.42 us -> 3.76 us
where the time goes in v7:
time: 135 us
  starting transfers between devices  58.3 us (43%)
  Pallas kernels  38.5 us (29%)
  waiting for transfers between devices  30.1 us (22%)
  local copies, waits for them, and re-layouts  5.18 us (4%)
  other arithmetic  1.47 us (1%)
    pallas_call x12, Pallas kernels, call(): pl.pallas_call(body, out_shape=[(pltpu.HBM if i in sent else jax.ShapeDty...  38.5 us
    ppermute x24, starting transfers between devices, swap(): lax.ppermute(values, axis, [(i, i ^ mask) for i in range(lax.axis_size(ax...  28.9 us
    all_to_all x5, starting transfers between devices, on_device(): lax.all_to_all(v, axes, split_axis=0, concat_axis=0, tiled=True)  20.8 us
    all_to_all x5, waiting for transfers between devices, on_device(): lax.all_to_all(v, axes, split_axis=0, concat_axis=0, tiled=True)  20.7 us
    ppermute x6, starting transfers between devices, pass_quarters(): lax.ppermute(v, ('nodes', 'feat'), [(i, i ^ b * feat_count + o) for i in...  8.58 us
    ppermute x24, waiting for transfers between devices, swap(): lax.ppermute(values, axis, [(i, i ^ mask) for i in range(lax.axis_size(ax...  4.79 us
    ppermute x6, waiting for transfers between devices, pass_quarters(): lax.ppermute(v, ('nodes', 'feat'), [(i, i ^ b * feat_count + o) for i in...  4.66 us
    unnamed x36, local copies, waits for them, and re-layouts  3.76 us
  transfers between devices with their start and end apart: 35, of which 6 were waited for; matrix products, arithmetic and copies ran while one was open for 1% of the time, Pallas kernels for 27%

profile of v7, /device:TPU:0, one launch (start us, length us, event | category | flops | bytes accessed | tf_op | source)
XLA Modules:
  0.0 134.5 jit_solution(14170373085177612900)
XLA Ops:
  0.6 2.1 %shard_map.112 = bf16[8,272,128]{2,1,0:T(8,128)(2,1)} custom-call(s32[2,8]{1,0:T(2,128)} %bitcast.29, s32[8]{0:T(128)} %degrees.1, s32[8,24]{1,0:T(8,128)} %slots_ref.1, s32[8,24]{1,0:T(8,128)} %tiles_ref.4, bf16[1024,256]{1,0:T(8,128)(2,1)} %feat_ref.1), custom_call_target="tpu_custom_call" | custom-call | tf_op jit(solution)/shard_map/pallas_call | solution.py:24
  2.8 7.4 %all-to-all-start = ((bf16[8,272,128]{2,1,0:T(8,128)(2,1)}), bf16[8,272,128]{2,1,0:T(8,128)(2,1)}, u32[]{:S(2)}, u32[]{:S(2)}) async-start(bf16[8,272,128]{2,1,0:T(8,128)(2,1)} %shard_map.112), calls=%async_computation | async-start | bytes 1114112 | tf_op jit(solution)/shard_map/all_to_all | solution.py:503
  17.6 2.9 %collective-permute-start.3 = (bf16[256,128]{1,0:T(8,128)(2,1)}, bf16[256,128]{1,0:T(8,128)(2,1)S(1)}, u32[]{:S(2)}, u32[]{:S(2)}) collective-permute-start(bf16[256,128]{1,0:T(8,128)(2,1)} %get-tuple-element.62), channel_id=1, source_target_pairs={{0,16},{4,20},{8,24},{12,28},{16,0},{20,4},{24,8},{28,12},{1,17},{... | collective-permute-start | bytes 196616 | tf_op jit(solution)/shard_map/ppermute | solution.py:352
  20.5 2.5 %collective-permute-start.4 = (bf16[256,128]{1,0:T(8,128)(2,1)}, bf16[256,128]{1,0:T(8,128)(2,1)S(1)}, u32[]{:S(2)}, u32[]{:S(2)}) collective-permute-start(bf16[256,128]{1,0:T(8,128)(2,1)} %get-tuple-element.63), channel_id=1, source_target_pairs={{0,20},{4,16},{8,28},{12,24},{16,4},{20,0},{24,12},{28,8},{1,21},{... | collective-permute-start | bytes 196616 | tf_op jit(solution)/shard_map/ppermute | solution.py:352
  23.1 2.8 %collective-permute-start.5 = (bf16[256,128]{1,0:T(8,128)(2,1)}, bf16[256,128]{1,0:T(8,128)(2,1)S(1)}, u32[]{:S(2)}, u32[]{:S(2)}) collective-permute-start(bf16[256,128]{1,0:T(8,128)(2,1)} %get-tuple-element.64), channel_id=1, source_target_pairs={{0,24},{4,28},{8,16},{12,20},{16,8},{20,12},{24,0},{28,4},{1,25},{... | collective-permute-start | bytes 196616 | tf_op jit(solution)/shard_map/ppermute | solution.py:352
  25.9 2.3 %collective-permute-start.6 = (bf16[256,128]{1,0:T(8,128)(2,1)}, bf16[256,128]{1,0:T(8,128)(2,1)S(1)}, u32[]{:S(2)}, u32[]{:S(2)}) collective-permute-start(bf16[256,128]{1,0:T(8,128)(2,1)} %get-tuple-element.65), channel_id=1, source_target_pairs={{0,28},{4,24},{8,20},{12,16},{16,12},{20,8},{24,4},{28,0},{1,29},{... | collective-permute-start | bytes 196616 | tf_op jit(solution)/shard_map/ppermute | solution.py:352
  28.2 3.7 %all-to-all-done.v_ref = bf16[8,272,128]{2,1,0:T(8,128)(2,1)} async-done(((bf16[8,272,128]{2,1,0:T(8,128)(2,1)}), bf16[8,272,128]{2,1,0:T(8,128)(2,1)}, u32[]{:S(2)}, u32[]{:S(2)}) %all-to-all-start) | async-done | bytes 557088 | tf_op jit(solution)/shard_map/all_to_all | solution.py:503
  31.9 6.2 %shard_map.114 = (bf16[32,32,256]{2,1,0:T(8,128)(2,1)}, s32[3,64,128]{2,1,0:T(8,128)}, f32[64,128]{1,0:T(8,128)}) custom-call(bf16[8,272,128]{2,1,0:T(8,128)(2,1)} %all-to-all-done.v_ref, bf16[16,128,128]{2,1,0:T(8,128)(2,1)S(1)} %copy-done.3), custom_call_target="tpu_custom_call" | custom-call | tf_op jit(solution)/shard_map/pallas_call | solution.py:24
  39.5 2.6 %all-to-all-start.1 = ((bf16[32,32,256]{2,1,0:T(8,128)(2,1)}), bf16[32,32,256]{2,1,0:T(8,128)(2,1)S(1)}, u32[]{:S(2)}, u32[]{:S(2)}) async-start(bf16[32,32,256]{2,1,0:T(8,128)(2,1)} %get-tuple-element.70), calls=%async_computation.1 | async-start | bytes 1048576 | tf_op jit(solution)/shard_map/all_to_all | solution.py:503
  43.5 9.5 %shard_map.115 = bf16[32,32,256]{2,1,0:T(8,128)(2,1)} custom-call(s32[64,128]{1,0:T(8,128)S(1)} %get-tuple-element.112.pick, s32[64,128]{1,0:T(8,128)S(1)} %get-tuple-element.111.near, f32[64,128]{1,0:T(8,128)S(1)} %copy-done.6, bf16[16,128,128]{2,1,0:T(8,128)(2,1)S(1)} %copy-done.3, bf16[256,128]{1,0:T(8,128)(2,1)S(1)} %copy-done.5, ...), custom_call_target="tpu_custom_call" | custom-call | flops 1073741824 | bytes 4194304 | tf_op jit(solution)/shard_map/pallas_call | solution.py:24
  53.0 5.5 %all-to-all-done.1 = bf16[32,32,256]{2,1,0:T(8,128)(2,1)S(1)} async-done(((bf16[32,32,256]{2,1,0:T(8,128)(2,1)}), bf16[32,32,256]{2,1,0:T(8,128)(2,1)S(1)}, u32[]{:S(2)}, u32[]{:S(2)}) %all-to-all-start.1) | async-done | bytes 524320 | tf_op jit(solution)/shard_map/all_to_all | solution.py:503
  58.4 2.6 %all-to-all-start.2 = ((bf16[32,32,256]{2,1,0:T(8,128)(2,1)}), bf16[32,32,256]{2,1,0:T(8,128)(2,1)S(1)}, u32[]{:S(2)}, u32[]{:S(2)}) async-start(bf16[32,32,256]{2,1,0:T(8,128)(2,1)} %shard_map.115), calls=%async_computation.2 | async-start | bytes 1048576 | tf_op jit(solution)/shard_map/all_to_all | solution.py:503
  61.1 3.9 %shard_map.116 = (f32[1024,256]{1,0:T(8,128)}, bf16[1024,256]{1,0:T(8,128)(2,1)S(1)}, bf16[1024,256]{1,0:T(8,128)(2,1)}) custom-call(bf16[1024,256]{1,0:T(8,128)(2,1)S(1)} %bitcast.18, bf16[2,256,1024]{2,1,0:T(8,128)(2,1)S(1)} %pad_maximum_fusion.refs_0_, bf16[2,256,1024]{2,1,0:T(8,128)(2,1)S(1)} %collective-permute-done.7.refs_1_, ...), custom_call_target="tpu_custom_call" | custom-call | flops 1073741824 | bytes 4194304 | tf_op jit(solution)/shard_map/pallas_call | solution.py:24
  65.8 11.6 %all-to-all-done.2 = bf16[32,32,256]{2,1,0:T(8,128)(2,1)S(1)} async-done(((bf16[32,32,256]{2,1,0:T(8,128)(2,1)}), bf16[32,32,256]{2,1,0:T(8,128)(2,1)S(1)}, u32[]{:S(2)}, u32[]{:S(2)}) %all-to-all-start.2) | async-done | bytes 524320 | tf_op jit(solution)/shard_map/all_to_all | solution.py:503
  77.4 3.3 %all-to-all-start.3 = ((bf16[32,32,256]{2,1,0:T(8,128)(2,1)}), bf16[32,32,256]{2,1,0:T(8,128)(2,1)}, u32[]{:S(2)}, u32[]{:S(2)}) async-start(bf16[32,32,256]{2,1,0:T(8,128)(2,1)} %bitcast.27), calls=%async_computation.3 | async-start | bytes 1048576 | tf_op jit(solution)/shard_map/all_to_all | solution.py:503
  80.8 4.2 %shard_map.118 = (bf16[4,128,256]{2,1,0:T(8,128)(2,1)}, bf16[4,128,256]{2,1,0:T(8,128)(2,1)}, bf16[4,128,256]{2,1,0:T(8,128)(2,1)}, bf16[4,128,256]{2,1,0:T(8,128)(2,1)}, bf16[1024,256]{1,0:T(8,128)(2,1)S(1)}) custom-call(f32[1024,256]{1,0:T(8,128)} %get-tuple-element.76.pre_ref, bf16[1024,256]{1,0:T(8,128)(2,1)S(1)} %bitcast.21, ...), custom_call_target="tpu_custom_call" | custom-call | tf_op jit(solution)/shard_map/pallas_call | solution.py:24
  97.5 6.2 %shard_map.117 = bf16[8,32,1024]{2,1,0:T(8,128)(2,1)} custom-call(s32[64,128]{1,0:T(8,128)S(1)} %get-tuple-element.113.pick, f32[64,128]{1,0:T(8,128)S(1)} %copy-done.6, bf16[32,32,256]{2,1,0:T(8,128)(2,1)} %all-to-all-done.3.v_ref, bf16[16,128,128]{2,1,0:T(8,128)(2,1)S(1)} %copy-done.4), custom_call_target="tpu_custom_call" | custom-call | flops 10737418240 | tf_op jit(solution)/shard_map/pallas_call | solution.py:24
  103.7 4.9 %all-to-all-start.4 = ((bf16[8,32,1024]{2,1,0:T(8,128)(2,1)}), bf16[8,32,1024]{2,1,0:T(8,128)(2,1)S(1)}, u32[]{:S(2)}, u32[]{:S(2)}) async-start(bf16[8,32,1024]{2,1,0:T(8,128)(2,1)} %shard_map.117), calls=%async_computation.4 | async-start | bytes 1048576 | tf_op jit(solution)/shard_map/all_to_all | solution.py:503
  112.9 2.4 %collective-permute-start.18 = (bf16[128,256]{1,0:T(8,128)(2,1)}, bf16[128,256]{1,0:T(8,128)(2,1)S(1)}, u32[]{:S(2)}, u32[]{:S(2)}) collective-permute-start(bf16[128,256]{1,0:T(8,128)(2,1)} %get-tuple-element.92), channel_id=1, source_target_pairs={{0,16},{4,20},{8,24},{12,28},{16,0},{20,4},{24,8},{28,12},{1,17},{... | collective-permute-start | bytes 196616 | tf_op jit(solution)/shard_map/ppermute | solution.py:352
  115.2 4.7 %collective-permute-done.24.refs_0_ = bf16[4,128,256]{2,1,0:T(8,128)(2,1)S(1)} collective-permute-done((bf16[4,128,256]{2,1,0:T(8,128)(2,1)}, bf16[4,128,256]{2,1,0:T(8,128)(2,1)S(1)}, u32[]{:S(2)}, u32[]{:S(2)}) %collective-permute-start.24) | collective-permute-done | bytes 262176 | tf_op jit(solution)/shard_map/ppermute | solution.py:473
  119.9 2.4 %collective-permute-start.19 = (bf16[128,256]{1,0:T(8,128)(2,1)}, bf16[128,256]{1,0:T(8,128)(2,1)S(1)}, u32[]{:S(2)}, u32[]{:S(2)}) collective-permute-start(bf16[128,256]{1,0:T(8,128)(2,1)} %get-tuple-element.93), channel_id=1, source_target_pairs={{0,24},{4,28},{8,16},{12,20},{16,8},{20,12},{24,0},{28,4},{1,25},{... | collective-permute-start | bytes 196616 | tf_op jit(solution)/shard_map/ppermute | solution.py:352
  123.1 2.1 %collective-permute-start.28 = (bf16[128,256]{1,0:T(8,128)(2,1)}, bf16[128,256]{1,0:T(8,128)(2,1)S(1)}, u32[]{:S(2)}, u32[]{:S(2)}) collective-permute-start(bf16[128,256]{1,0:T(8,128)(2,1)} %get-tuple-element.109), channel_id=1, source_target_pairs={{0,16},{4,20},{8,24},{12,28},{16,0},{20,4},{24,8},{28,12},{1,17},{... | collective-permute-start | bytes 196616 | tf_op jit(solution)/shard_map/ppermute | solution.py:352
  125.2 2.2 %collective-permute-start.29 = (bf16[128,256]{1,0:T(8,128)(2,1)}, bf16[128,256]{1,0:T(8,128)(2,1)S(1)}, u32[]{:S(2)}, u32[]{:S(2)}) collective-permute-start(bf16[128,256]{1,0:T(8,128)(2,1)} %get-tuple-element.110), channel_id=1, source_target_pairs={{0,24},{4,28},{8,16},{12,20},{16,8},{20,12},{24,0},{28,4},{1,25},{... | collective-permute-start | bytes 196616 | tf_op jit(solution)/shard_map/ppermute | solution.py:352
  127.4 3.1 %collective-permute-done.18 = bf16[128,256]{1,0:T(8,128)(2,1)S(1)} collective-permute-done((bf16[128,256]{1,0:T(8,128)(2,1)}, bf16[128,256]{1,0:T(8,128)(2,1)S(1)}, u32[]{:S(2)}, u32[]{:S(2)}) %collective-permute-start.18) | collective-permute-done | bytes 65568 | tf_op jit(solution)/shard_map/ppermute | solution.py:352
  (101 shorter events, 32.4 us)
Async XLA Ops:
  2.8 29.1 %all-to-all-start = ((bf16[8,272,128]{2,1,0:T(8,128)(2,1)}), bf16[8,272,128]{2,1,0:T(8,128)(2,1)}, u32[]{:S(2)}, u32[]{:S(2)}) async-start(bf16[8,272,128]{2,1,0:T(8,128)(2,1)} %shard_map.112), calls=%async_computation | async-start | bytes 1114112 | tf_op jit(solution)/shard_map/all_to_all | solution.py:503
  11.6 30.7 %collective-permute-start.7 = (bf16[2,256,1024]{2,1,0:T(8,128)(2,1)S(1)}, bf16[2,256,1024]{2,1,0:T(8,128)(2,1)S(1)}, u32[]{:S(2)}, u32[]{:S(2)}) collective-permute-start(bf16[2,256,1024]{2,1,0:T(8,128)(2,1)S(1)} %pad_maximum_fusion.refs_0_), channel_id=1, source_target_pairs={{0,2},{1,3},{2,0},{3,1},{4,6},{5,7},{6,4},{7,5},{8,10},{9,11},{10,... | collective-permute-start | bytes 3145736 | tf_op jit(solution)/shard_map/ppermute | solution.py:352
  17.6 8.3 %collective-permute-start.2 = (bf16[256,128]{1,0:T(8,128)(2,1)}, bf16[256,128]{1,0:T(8,128)(2,1)S(1)}, u32[]{:S(2)}, u32[]{:S(2)}) collective-permute-start(bf16[256,128]{1,0:T(8,128)(2,1)} %get-tuple-element.61), channel_id=1, source_target_pairs={{0,12},{4,8},{8,4},{12,0},{16,28},{20,24},{24,20},{28,16},{1,13},{... | collective-permute-start | bytes 196616 | tf_op jit(solution)/shard_map/ppermute | solution.py:352
  17.6 20.5 %collective-permute-start.3 = (bf16[256,128]{1,0:T(8,128)(2,1)}, bf16[256,128]{1,0:T(8,128)(2,1)S(1)}, u32[]{:S(2)}, u32[]{:S(2)}) collective-permute-start(bf16[256,128]{1,0:T(8,128)(2,1)} %get-tuple-element.62), channel_id=1, source_target_pairs={{0,16},{4,20},{8,24},{12,28},{16,0},{20,4},{24,8},{28,12},{1,17},{... | collective-permute-start | bytes 196616 | tf_op jit(solution)/shard_map/ppermute | solution.py:352
  20.5 17.7 %collective-permute-start.4 = (bf16[256,128]{1,0:T(8,128)(2,1)}, bf16[256,128]{1,0:T(8,128)(2,1)S(1)}, u32[]{:S(2)}, u32[]{:S(2)}) collective-permute-start(bf16[256,128]{1,0:T(8,128)(2,1)} %get-tuple-element.63), channel_id=1, source_target_pairs={{0,20},{4,16},{8,28},{12,24},{16,4},{20,0},{24,12},{28,8},{1,21},{... | collective-permute-start | bytes 196616 | tf_op jit(solution)/shard_map/ppermute | solution.py:352
  23.1 15.1 %collective-permute-start.5 = (bf16[256,128]{1,0:T(8,128)(2,1)}, bf16[256,128]{1,0:T(8,128)(2,1)S(1)}, u32[]{:S(2)}, u32[]{:S(2)}) collective-permute-start(bf16[256,128]{1,0:T(8,128)(2,1)} %get-tuple-element.64), channel_id=1, source_target_pairs={{0,24},{4,28},{8,16},{12,20},{16,8},{20,12},{24,0},{28,4},{1,25},{... | collective-permute-start | bytes 196616 | tf_op jit(solution)/shard_map/ppermute | solution.py:352
  25.9 12.3 %collective-permute-start.6 = (bf16[256,128]{1,0:T(8,128)(2,1)}, bf16[256,128]{1,0:T(8,128)(2,1)S(1)}, u32[]{:S(2)}, u32[]{:S(2)}) collective-permute-start(bf16[256,128]{1,0:T(8,128)(2,1)} %get-tuple-element.65), channel_id=1, source_target_pairs={{0,28},{4,24},{8,20},{12,16},{16,12},{20,8},{24,4},{28,0},{1,29},{... | collective-permute-start | bytes 196616 | tf_op jit(solution)/shard_map/ppermute | solution.py:352
  39.5 19.0 %all-to-all-start.1 = ((bf16[32,32,256]{2,1,0:T(8,128)(2,1)}), bf16[32,32,256]{2,1,0:T(8,128)(2,1)S(1)}, u32[]{:S(2)}, u32[]{:S(2)}) async-start(bf16[32,32,256]{2,1,0:T(8,128)(2,1)} %get-tuple-element.70), calls=%async_computation.1 | async-start | bytes 1048576 | tf_op jit(solution)/shard_map/all_to_all | solution.py:503
  42.1 19.0 %collective-permute-start.8 = (bf16[2,256,1024]{2,1,0:T(8,128)(2,1)S(1)}, bf16[2,256,1024]{2,1,0:T(8,128)(2,1)}, u32[]{:S(2)}, u32[]{:S(2)}) collective-permute-start(bf16[2,256,1024]{2,1,0:T(8,128)(2,1)S(1)} %pad_maximum_fusion.refs_0_), channel_id=1, source_target_pairs={{0,1},{1,0},{2,3},{3,2},{4,5},{5,4},{6,7},{7,6},{8,9},{9,8},{10,11... | collective-permute-start | bytes 3145736 | tf_op jit(solution)/shard_map/ppermute | solution.py:352
  42.3 18.8 %collective-permute-start.9 = (bf16[2,256,1024]{2,1,0:T(8,128)(2,1)S(1)}, bf16[2,256,1024]{2,1,0:T(8,128)(2,1)}, u32[]{:S(2)}, u32[]{:S(2)}) collective-permute-start(bf16[2,256,1024]{2,1,0:T(8,128)(2,1)S(1)} %collective-permute-done.7.refs_1_), channel_id=1, source_target_pairs={{0,1},{1,0},{2,3},{3,2},{4,5},{5,4},{6,7},{7,6},{8,9},{9,8},{10,11... | collective-permute-start | bytes 3145736 | tf_op jit(solution)/shard_map/ppermute | solution.py:352
  58.4 19.0 %all-to-all-start.2 = ((bf16[32,32,256]{2,1,0:T(8,128)(2,1)}), bf16[32,32,256]{2,1,0:T(8,128)(2,1)S(1)}, u32[]{:S(2)}, u32[]{:S(2)}) async-start(bf16[32,32,256]{2,1,0:T(8,128)(2,1)} %shard_map.115), calls=%async_computation.2 | async-start | bytes 1048576 | tf_op jit(solution)/shard_map/all_to_all | solution.py:503
  77.4 20.1 %all-to-all-start.3 = ((bf16[32,32,256]{2,1,0:T(8,128)(2,1)}), bf16[32,32,256]{2,1,0:T(8,128)(2,1)}, u32[]{:S(2)}, u32[]{:S(2)}) async-start(bf16[32,32,256]{2,1,0:T(8,128)(2,1)} %bitcast.27), calls=%async_computation.3 | async-start | bytes 1048576 | tf_op jit(solution)/shard_map/all_to_all | solution.py:503
  89.7 19.0 %collective-permute-start.14 = (bf16[4,128,256]{2,1,0:T(8,128)(2,1)}, bf16[4,128,256]{2,1,0:T(8,128)(2,1)S(1)}, u32[]{:S(2)}, u32[]{:S(2)}) collective-permute-start(bf16[4,128,256]{2,1,0:T(8,128)(2,1)} %get-tuple-element.83), channel_id=1, source_target_pairs={{0,4},{1,5},{2,6},{3,7},{4,0},{5,1},{6,2},{7,3},{8,12},{9,13},{10,... | collective-permute-start | bytes 786440 | tf_op jit(solution)/shard_map/ppermute | solution.py:473
  91.2 19.5 %collective-permute-start.15 = (bf16[4,128,256]{2,1,0:T(8,128)(2,1)}, bf16[4,128,256]{2,1,0:T(8,128)(2,1)S(1)}, u32[]{:S(2)}, u32[]{:S(2)}) collective-permute-start(bf16[4,128,256]{2,1,0:T(8,128)(2,1)} %get-tuple-element.84), channel_id=1, source_target_pairs={{0,2},{1,3},{2,0},{3,1},{4,6},{5,7},{6,4},{7,5},{8,10},{9,11},{10,... | collective-permute-start | bytes 786440 | tf_op jit(solution)/shard_map/ppermute | solution.py:473
  92.7 18.0 %collective-permute-start.16 = (bf16[4,128,256]{2,1,0:T(8,128)(2,1)}, bf16[4,128,256]{2,1,0:T(8,128)(2,1)S(1)}, u32[]{:S(2)}, u32[]{:S(2)}) collective-permute-start(bf16[4,128,256]{2,1,0:T(8,128)(2,1)} %get-tuple-element.85), channel_id=1, source_target_pairs={{0,6},{1,7},{2,4},{3,5},{4,2},{5,3},{6,0},{7,1},{8,14},{9,15},{10,... | collective-permute-start | bytes 786440 | tf_op jit(solution)/shard_map/ppermute | solution.py:473
  94.4 25.4 %collective-permute-start.24 = (bf16[4,128,256]{2,1,0:T(8,128)(2,1)}, bf16[4,128,256]{2,1,0:T(8,128)(2,1)S(1)}, u32[]{:S(2)}, u32[]{:S(2)}) collective-permute-start(bf16[4,128,256]{2,1,0:T(8,128)(2,1)} %get-tuple-element.100), channel_id=1, source_target_pairs={{0,4},{1,5},{2,6},{3,7},{4,0},{5,1},{6,2},{7,3},{8,12},{9,13},{10,... | collective-permute-start | bytes 786440 | tf_op jit(solution)/shard_map/ppermute | solution.py:473
  96.0 26.3 %collective-permute-start.25 = (bf16[4,128,256]{2,1,0:T(8,128)(2,1)}, bf16[4,128,256]{2,1,0:T(8,128)(2,1)S(1)}, u32[]{:S(2)}, u32[]{:S(2)}) collective-permute-start(bf16[4,128,256]{2,1,0:T(8,128)(2,1)} %get-tuple-element.101), channel_id=1, source_target_pairs={{0,2},{1,3},{2,0},{3,1},{4,6},{5,7},{6,4},{7,5},{8,10},{9,11},{10,... | collective-permute-start | bytes 786440 | tf_op jit(solution)/shard_map/ppermute | solution.py:473
  103.7 29.8 %all-to-all-start.4 = ((bf16[8,32,1024]{2,1,0:T(8,128)(2,1)}), bf16[8,32,1024]{2,1,0:T(8,128)(2,1)S(1)}, u32[]{:S(2)}, u32[]{:S(2)}) async-start(bf16[8,32,1024]{2,1,0:T(8,128)(2,1)} %shard_map.117), calls=%async_computation.4 | async-start | bytes 1048576 | tf_op jit(solution)/shard_map/all_to_all | solution.py:503
  108.6 13.7 %collective-permute-start.26 = (bf16[4,128,256]{2,1,0:T(8,128)(2,1)S(1)}, bf16[4,128,256]{2,1,0:T(8,128)(2,1)S(1)}, u32[]{:S(2)}, u32[]{:S(2)}) collective-permute-start(bf16[4,128,256]{2,1,0:T(8,128)(2,1)S(1)} %copy-done.10), channel_id=1, source_target_pairs={{0,6},{1,7},{2,4},{3,5},{4,2},{5,3},{6,0},{7,1},{8,14},{9,15},{10,... | collective-permute-start | bytes 786440 | tf_op jit(solution)/shard_map/ppermute | solution.py:473
  111.4 13.8 %collective-permute-start.17 = (bf16[128,256]{1,0:T(8,128)(2,1)}, bf16[128,256]{1,0:T(8,128)(2,1)S(1)}, u32[]{:S(2)}, u32[]{:S(2)}) collective-permute-start(bf16[128,256]{1,0:T(8,128)(2,1)} %get-tuple-element.91), channel_id=1, source_target_pairs={{0,8},{4,12},{8,0},{12,4},{16,24},{20,28},{24,16},{28,20},{1,9},{5... | collective-permute-start | bytes 196616 | tf_op jit(solution)/shard_map/ppermute | solution.py:352
  112.9 17.6 %collective-permute-start.18 = (bf16[128,256]{1,0:T(8,128)(2,1)}, bf16[128,256]{1,0:T(8,128)(2,1)S(1)}, u32[]{:S(2)}, u32[]{:S(2)}) collective-permute-start(bf16[128,256]{1,0:T(8,128)(2,1)} %get-tuple-element.92), channel_id=1, source_target_pairs={{0,16},{4,20},{8,24},{12,28},{16,0},{20,4},{24,8},{28,12},{1,17},{... | collective-permute-start | bytes 196616 | tf_op jit(solution)/shard_map/ppermute | solution.py:352
  119.9 10.6 %collective-permute-start.19 = (bf16[128,256]{1,0:T(8,128)(2,1)}, bf16[128,256]{1,0:T(8,128)(2,1)S(1)}, u32[]{:S(2)}, u32[]{:S(2)}) collective-permute-start(bf16[128,256]{1,0:T(8,128)(2,1)} %get-tuple-element.93), channel_id=1, source_target_pairs={{0,24},{4,28},{8,16},{12,20},{16,8},{20,12},{24,0},{28,4},{1,25},{... | collective-permute-start | bytes 196616 | tf_op jit(solution)/shard_map/ppermute | solution.py:352
  123.0 8.2 %collective-permute-start.27 = (bf16[128,256]{1,0:T(8,128)(2,1)}, bf16[128,256]{1,0:T(8,128)(2,1)S(1)}, u32[]{:S(2)}, u32[]{:S(2)}) collective-permute-start(bf16[128,256]{1,0:T(8,128)(2,1)} %get-tuple-element.108), channel_id=1, source_target_pairs={{0,8},{4,12},{8,0},{12,4},{16,24},{20,28},{24,16},{28,20},{1,9},{5... | collective-permute-start | bytes 196616 | tf_op jit(solution)/shard_map/ppermute | solution.py:352
  123.1 9.7 %collective-permute-start.28 = (bf16[128,256]{1,0:T(8,128)(2,1)}, bf16[128,256]{1,0:T(8,128)(2,1)S(1)}, u32[]{:S(2)}, u32[]{:S(2)}) collective-permute-start(bf16[128,256]{1,0:T(8,128)(2,1)} %get-tuple-element.109), channel_id=1, source_target_pairs={{0,16},{4,20},{8,24},{12,28},{16,0},{20,4},{24,8},{28,12},{1,17},{... | collective-permute-start | bytes 196616 | tf_op jit(solution)/shard_map/ppermute | solution.py:352
  (29 other events, 151.2 us)

commit v8 on v7

--- a/solution.py
+++ b/solution.py
@@ -490,6 +490,37 @@
     return mine
 
 
+def halving_kernel(keep_ref, *refs):
+    came, kept_ref, give_ref = refs[:-2], refs[-2], refs[-1]
+    me = lax.axis_index("nodes") // 2
+    for i in range(kept_ref.shape[0]):
+        for o_ref, to in ((kept_ref, me ^ (2 * i)), (give_ref, me ^ (2 * i) ^ 1)):
+            total = keep_ref[to]
+            for ref in came:
+                total = total + ref[to].astype(f32)
+            o_ref[i] = total.astype(o_ref.dtype)
+
+
+def grad_sum_halving(flops, keep, *came):
+    half, tall, wide = keep.shape
+    kept, give = call(
+        halving_kernel,
+        [((half // 2, tall, wide), f32), ((half // 2, tall, wide), bf16)],
+        [vmem] * (1 + len(came)),
+        (keep, *came),
+        flops=flops,
+        sent=(1,),
+    )
+    bit = 1
+    while True:
+        total = kept + swap(give, "nodes", 2 * bit).astype(f32)
+        if total.shape[0] == 1:
+            return total[0]
+        pairs = total.reshape(total.shape[0] // 2, 2, tall, wide)
+        kept, give = pairs[:, 0], pairs[:, 1].astype(bf16)
+        bit *= 2
+
+
 def on_device(
     features, ghosts, slots, tile_ids, degrees, tile_table, weight_one, weight_two, cotangent
 ):
@@ -549,8 +580,8 @@
     last = spread_last(out_t, ids, tile_table, per, width_k, nodes)
     out_n = exchange(last, "nodes")
     quarters_one = pass_quarters(*halves_one, late=None)
-    grad_two = grad_sum(0, *after(quarters_two, last))
-    grad_one = grad_sum(20 << 30, *after(quarters_one, last))
+    grad_two = grad_sum_halving(0, *after(quarters_two, last))
+    grad_one = grad_sum_halving(20 << 30, *after(quarters_one, last))
     output = out_n.reshape(wide, rows).T
     return (output, grad_one, grad_two)
 

time: 135 us -> 134 us (level)
    ppermute x24 -> x22, starting transfers between devices: 28.9 us -> 26.6 us  [swap(): lax.ppermute(values, axis, [(i, i ^ mask) for i in range(lax.axis_size(ax...]
    ppermute x6, starting transfers between devices: 8.58 us -> 10.2 us  [pass_quarters(): lax.ppermute(v, ('nodes', 'feat'), [(i, i ^ b * feat_count + o) for i in...]
    add x2 -> x0, other arithmetic: 1.37 us -> none  [grad_sum(): mine = mine + swap(part, 'nodes', 2 * (i + 1)).astype(f32)]
    ppermute x24 -> x22, waiting for transfers between devices: 4.79 us -> 3.88 us  [swap(): lax.ppermute(values, axis, [(i, i ^ mask) for i in range(lax.axis_size(ax...]
    unnamed x36 -> x34, local copies, waits for them, and re-layouts: 3.76 us -> 3.77 us
  transfers between devices with their start and end apart: 35 -> 33, of which waited for: 6 -> 7; matrix products, arithmetic and copies ran while one was open for 1% -> 1% of each run, Pallas kernels for 27% -> 27%
where the time goes in v8:
time: 134 us; the launch traced here: 133 us
  starting transfers between devices  57.2 us (43%)
  Pallas kernels  38.7 us (29%)
  waiting for transfers between devices  29.9 us (22%)
  local copies, waits for them, and re-layouts  5.21 us (4%)
  other arithmetic  1.48 us (1%)
    pallas_call x12, Pallas kernels, call(): pl.pallas_call(body, out_shape=[(pltpu.HBM if i in sent else jax.ShapeDty...  38.7 us
    ppermute x22, starting transfers between devices, swap(): lax.ppermute(values, axis, [(i, i ^ mask) for i in range(lax.axis_size(ax...  26.6 us
    all_to_all x5, waiting for transfers between devices, on_device(): lax.all_to_all(v, axes, split_axis=0, concat_axis=0, tiled=True)  20.6 us
    all_to_all x5, starting transfers between devices, on_device(): lax.all_to_all(v, axes, split_axis=0, concat_axis=0, tiled=True)  20.3 us
    ppermute x6, starting transfers between devices, pass_quarters(): lax.ppermute(v, ('nodes', 'feat'), [(i, i ^ b * feat_count + o) for i in...  10.2 us
    ppermute x6, waiting for transfers between devices, pass_quarters(): lax.ppermute(v, ('nodes', 'feat'), [(i, i ^ b * feat_count + o) for i in...  5.47 us
    ppermute x22, waiting for transfers between devices, swap(): lax.ppermute(values, axis, [(i, i ^ mask) for i in range(lax.axis_size(ax...  3.88 us
    unnamed x34, local copies, waits for them, and re-layouts  3.77 us
  transfers between devices with their start and end apart: 33, of which 7 were waited for; matrix products, arithmetic and copies ran while one was open for 1% of the time, Pallas kernels for 27%

profile of v8, /device:TPU:0, one launch (start us, length us, event | category | flops | bytes accessed | tf_op | source)
XLA Modules:
  0.0 133.4 jit_solution(5450924222865510706)
XLA Ops:
  0.6 2.1 %shard_map.112 = bf16[8,272,128]{2,1,0:T(8,128)(2,1)} custom-call(s32[2,8]{1,0:T(2,128)} %bitcast.53, s32[8]{0:T(128)} %degrees.1, s32[8,24]{1,0:T(8,128)} %slots_ref.1, s32[8,24]{1,0:T(8,128)} %tiles_ref.4, bf16[1024,256]{1,0:T(8,128)(2,1)} %feat_ref.1), custom_call_target="tpu_custom_call" | custom-call | tf_op jit(solution)/shard_map/pallas_call | solution.py:24
  2.8 7.4 %all-to-all-start = ((bf16[8,272,128]{2,1,0:T(8,128)(2,1)}), bf16[8,272,128]{2,1,0:T(8,128)(2,1)}, u32[]{:S(2)}, u32[]{:S(2)}) async-start(bf16[8,272,128]{2,1,0:T(8,128)(2,1)} %shard_map.112), calls=%async_computation | async-start | bytes 1114112 | tf_op jit(solution)/shard_map/all_to_all | solution.py:534
  14.1 2.0 %collective-permute-start = (bf16[256,128]{1,0:T(8,128)(2,1)}, bf16[256,128]{1,0:T(8,128)(2,1)S(1)}, u32[]{:S(2)}, u32[]{:S(2)}) collective-permute-start(bf16[256,128]{1,0:T(8,128)(2,1)} %get-tuple-element.55), channel_id=1, source_target_pairs={{0,4},{4,0},{8,12},{12,8},{16,20},{20,16},{24,28},{28,24},{1,5},{5... | collective-permute-start | bytes 196616 | tf_op jit(solution)/shard_map/ppermute | solution.py:352
  17.6 2.9 %collective-permute-start.3 = (bf16[256,128]{1,0:T(8,128)(2,1)}, bf16[256,128]{1,0:T(8,128)(2,1)S(1)}, u32[]{:S(2)}, u32[]{:S(2)}) collective-permute-start(bf16[256,128]{1,0:T(8,128)(2,1)} %get-tuple-element.58), channel_id=1, source_target_pairs={{0,16},{4,20},{8,24},{12,28},{16,0},{20,4},{24,8},{28,12},{1,17},{... | collective-permute-start | bytes 196616 | tf_op jit(solution)/shard_map/ppermute | solution.py:352
  20.5 2.5 %collective-permute-start.4 = (bf16[256,128]{1,0:T(8,128)(2,1)}, bf16[256,128]{1,0:T(8,128)(2,1)S(1)}, u32[]{:S(2)}, u32[]{:S(2)}) collective-permute-start(bf16[256,128]{1,0:T(8,128)(2,1)} %get-tuple-element.59), channel_id=1, source_target_pairs={{0,20},{4,16},{8,28},{12,24},{16,4},{20,0},{24,12},{28,8},{1,21},{... | collective-permute-start | bytes 196616 | tf_op jit(solution)/shard_map/ppermute | solution.py:352
  23.1 2.8 %collective-permute-start.5 = (bf16[256,128]{1,0:T(8,128)(2,1)}, bf16[256,128]{1,0:T(8,128)(2,1)S(1)}, u32[]{:S(2)}, u32[]{:S(2)}) collective-permute-start(bf16[256,128]{1,0:T(8,128)(2,1)} %get-tuple-element.60), channel_id=1, source_target_pairs={{0,24},{4,28},{8,16},{12,20},{16,8},{20,12},{24,0},{28,4},{1,25},{... | collective-permute-start | bytes 196616 | tf_op jit(solution)/shard_map/ppermute | solution.py:352
  25.9 2.3 %collective-permute-start.6 = (bf16[256,128]{1,0:T(8,128)(2,1)}, bf16[256,128]{1,0:T(8,128)(2,1)S(1)}, u32[]{:S(2)}, u32[]{:S(2)}) collective-permute-start(bf16[256,128]{1,0:T(8,128)(2,1)} %get-tuple-element.61), channel_id=1, source_target_pairs={{0,28},{4,24},{8,20},{12,16},{16,12},{20,8},{24,4},{28,0},{1,29},{... | collective-permute-start | bytes 196616 | tf_op jit(solution)/shard_map/ppermute | solution.py:352
  28.2 3.7 %all-to-all-done.v_ref = bf16[8,272,128]{2,1,0:T(8,128)(2,1)} async-done(((bf16[8,272,128]{2,1,0:T(8,128)(2,1)}), bf16[8,272,128]{2,1,0:T(8,128)(2,1)}, u32[]{:S(2)}, u32[]{:S(2)}) %all-to-all-start) | async-done | bytes 557088 | tf_op jit(solution)/shard_map/all_to_all | solution.py:534
  31.9 6.2 %shard_map.114 = (bf16[32,32,256]{2,1,0:T(8,128)(2,1)}, s32[3,64,128]{2,1,0:T(8,128)}, f32[64,128]{1,0:T(8,128)}) custom-call(bf16[8,272,128]{2,1,0:T(8,128)(2,1)} %all-to-all-done.v_ref, bf16[16,128,128]{2,1,0:T(8,128)(2,1)S(1)} %copy-done.3), custom_call_target="tpu_custom_call" | custom-call | tf_op jit(solution)/shard_map/pallas_call | solution.py:24
  39.5 2.6 %all-to-all-start.1 = ((bf16[32,32,256]{2,1,0:T(8,128)(2,1)}), bf16[32,32,256]{2,1,0:T(8,128)(2,1)S(1)}, u32[]{:S(2)}, u32[]{:S(2)}) async-start(bf16[32,32,256]{2,1,0:T(8,128)(2,1)} %get-tuple-element.66), calls=%async_computation.1 | async-start | bytes 1048576 | tf_op jit(solution)/shard_map/all_to_all | solution.py:534
  43.5 9.6 %shard_map.115 = bf16[32,32,256]{2,1,0:T(8,128)(2,1)} custom-call(s32[64,128]{1,0:T(8,128)S(1)} %get-tuple-element.104.pick, s32[64,128]{1,0:T(8,128)S(1)} %get-tuple-element.103.near, f32[64,128]{1,0:T(8,128)S(1)} %copy-done.6, bf16[16,128,128]{2,1,0:T(8,128)(2,1)S(1)} %copy-done.3, bf16[256,128]{1,0:T(8,128)(2,1)S(1)} %copy-done.5, ...), custom_call_target="tpu_custom_call" | custom-call | flops 1073741824 | bytes 4194304 | tf_op jit(solution)/shard_map/pallas_call | solution.py:24
  53.1 5.3 %all-to-all-done.1 = bf16[32,32,256]{2,1,0:T(8,128)(2,1)S(1)} async-done(((bf16[32,32,256]{2,1,0:T(8,128)(2,1)}), bf16[32,32,256]{2,1,0:T(8,128)(2,1)S(1)}, u32[]{:S(2)}, u32[]{:S(2)}) %all-to-all-start.1) | async-done | bytes 524320 | tf_op jit(solution)/shard_map/all_to_all | solution.py:534
  58.5 2.6 %all-to-all-start.2 = ((bf16[32,32,256]{2,1,0:T(8,128)(2,1)}), bf16[32,32,256]{2,1,0:T(8,128)(2,1)S(1)}, u32[]{:S(2)}, u32[]{:S(2)}) async-start(bf16[32,32,256]{2,1,0:T(8,128)(2,1)} %shard_map.115), calls=%async_computation.2 | async-start | bytes 1048576 | tf_op jit(solution)/shard_map/all_to_all | solution.py:534
  61.1 3.9 %shard_map.116 = (f32[1024,256]{1,0:T(8,128)}, bf16[1024,256]{1,0:T(8,128)(2,1)S(1)}, bf16[1024,256]{1,0:T(8,128)(2,1)}) custom-call(bf16[1024,256]{1,0:T(8,128)(2,1)S(1)} %bitcast.42, bf16[2,256,1024]{2,1,0:T(8,128)(2,1)S(1)} %pad_maximum_fusion.refs_0_, bf16[2,256,1024]{2,1,0:T(8,128)(2,1)S(1)} %collective-permute-done.7.refs_1_, ...), custom_call_target="tpu_custom_call" | custom-call | flops 1073741824 | bytes 4194304 | tf_op jit(solution)/shard_map/pallas_call | solution.py:24
  65.9 11.6 %all-to-all-done.2 = bf16[32,32,256]{2,1,0:T(8,128)(2,1)S(1)} async-done(((bf16[32,32,256]{2,1,0:T(8,128)(2,1)}), bf16[32,32,256]{2,1,0:T(8,128)(2,1)S(1)}, u32[]{:S(2)}, u32[]{:S(2)}) %all-to-all-start.2) | async-done | bytes 524320 | tf_op jit(solution)/shard_map/all_to_all | solution.py:534
  77.4 3.5 %all-to-all-start.3 = ((bf16[32,32,256]{2,1,0:T(8,128)(2,1)}), bf16[32,32,256]{2,1,0:T(8,128)(2,1)}, u32[]{:S(2)}, u32[]{:S(2)}) async-start(bf16[32,32,256]{2,1,0:T(8,128)(2,1)} %bitcast.51), calls=%async_computation.3 | async-start | bytes 1048576 | tf_op jit(solution)/shard_map/all_to_all | solution.py:534
  81.0 4.2 %shard_map.118 = (bf16[4,128,256]{2,1,0:T(8,128)(2,1)}, bf16[4,128,256]{2,1,0:T(8,128)(2,1)}, bf16[4,128,256]{2,1,0:T(8,128)(2,1)}, bf16[4,128,256]{2,1,0:T(8,128)(2,1)}, bf16[1024,256]{1,0:T(8,128)(2,1)S(1)}) custom-call(f32[1024,256]{1,0:T(8,128)} %get-tuple-element.72.pre_ref, bf16[1024,256]{1,0:T(8,128)(2,1)S(1)} %bitcast.45, ...), custom_call_target="tpu_custom_call" | custom-call | tf_op jit(solution)/shard_map/pallas_call | solution.py:24
  97.5 6.2 %shard_map.117 = bf16[8,32,1024]{2,1,0:T(8,128)(2,1)} custom-call(s32[64,128]{1,0:T(8,128)S(1)} %get-tuple-element.105.pick, f32[64,128]{1,0:T(8,128)S(1)} %copy-done.6, bf16[32,32,256]{2,1,0:T(8,128)(2,1)} %all-to-all-done.3.v_ref, bf16[16,128,128]{2,1,0:T(8,128)(2,1)S(1)} %copy-done.4), custom_call_target="tpu_custom_call" | custom-call | flops 10737418240 | tf_op jit(solution)/shard_map/pallas_call | solution.py:24
  103.7 3.9 %collective-permute-start.25 = (bf16[4,128,256]{2,1,0:T(8,128)(2,1)}, bf16[4,128,256]{2,1,0:T(8,128)(2,1)S(1)}, u32[]{:S(2)}, u32[]{:S(2)}) collective-permute-start(bf16[4,128,256]{2,1,0:T(8,128)(2,1)} %get-tuple-element.96), channel_id=1, source_target_pairs={{0,6},{1,7},{2,4},{3,5},{4,2},{5,3},{6,0},{7,1},{8,14},{9,15},{10,... | collective-permute-start | bytes 786440 | tf_op jit(solution)/shard_map/ppermute | solution.py:473
  109.1 4.2 %all-to-all-start.4 = ((bf16[8,32,1024]{2,1,0:T(8,128)(2,1)}), bf16[8,32,1024]{2,1,0:T(8,128)(2,1)S(1)}, u32[]{:S(2)}, u32[]{:S(2)}) async-start(bf16[8,32,1024]{2,1,0:T(8,128)(2,1)} %shard_map.117), calls=%async_computation.4 | async-start | bytes 1048576 | tf_op jit(solution)/shard_map/all_to_all | solution.py:534
  113.2 5.5 %collective-permute-done.25.refs_2_ = bf16[4,128,256]{2,1,0:T(8,128)(2,1)S(1)} collective-permute-done((bf16[4,128,256]{2,1,0:T(8,128)(2,1)}, bf16[4,128,256]{2,1,0:T(8,128)(2,1)S(1)}, u32[]{:S(2)}, u32[]{:S(2)}) %collective-permute-start.25) | collective-permute-done | bytes 262176 | tf_op jit(solution)/shard_map/ppermute | solution.py:473
  119.4 2.2 %collective-permute-start.26 = (bf16[2,128,256]{2,1,0:T(8,128)(2,1)}, bf16[2,128,256]{2,1,0:T(8,128)(2,1)S(1)}, u32[]{:S(2)}, u32[]{:S(2)}) collective-permute-start(bf16[2,128,256]{2,1,0:T(8,128)(2,1)} %get-tuple-element.102), channel_id=1, source_target_pairs={{0,8},{4,12},{8,0},{12,4},{16,24},{20,28},{24,16},{28,20},{1,9},{5... | collective-permute-start | bytes 393224 | tf_op jit(solution)/shard_map/ppermute | solution.py:352
  123.4 2.2 %collective-permute-done.26 = bf16[2,128,256]{2,1,0:T(8,128)(2,1)S(1)} collective-permute-done((bf16[2,128,256]{2,1,0:T(8,128)(2,1)}, bf16[2,128,256]{2,1,0:T(8,128)(2,1)S(1)}, u32[]{:S(2)}, u32[]{:S(2)}) %collective-permute-start.26) | collective-permute-done | bytes 131104 | tf_op jit(solution)/shard_map/ppermute | solution.py:352
  125.7 3.7 %collective-permute-start.27 = (bf16[1,128,256]{2,1,0:T(8,128)(2,1)S(1)}, bf16[1,128,256]{2,1,0:T(8,128)(2,1)S(1)}, u32[]{:S(2)}, u32[]{:S(2)}) collective-permute-start(bf16[1,128,256]{2,1,0:T(8,128)(2,1)S(1)} %fusion.5), channel_id=1, source_target_pairs={{0,16},{4,20},{8,24},{12,28},{16,0},{20,4},{24,8},{28,12},{1,17},{... | collective-permute-start | bytes 196616 | tf_op jit(solution)/shard_map/ppermute | solution.py:352
  (99 shorter events, 29.1 us)
Async XLA Ops:
  2.8 29.1 %all-to-all-start = ((bf16[8,272,128]{2,1,0:T(8,128)(2,1)}), bf16[8,272,128]{2,1,0:T(8,128)(2,1)}, u32[]{:S(2)}, u32[]{:S(2)}) async-start(bf16[8,272,128]{2,1,0:T(8,128)(2,1)} %shard_map.112), calls=%async_computation | async-start | bytes 1114112 | tf_op jit(solution)/shard_map/all_to_all | solution.py:534
  11.6 30.7 %collective-permute-start.7 = (bf16[2,256,1024]{2,1,0:T(8,128)(2,1)S(1)}, bf16[2,256,1024]{2,1,0:T(8,128)(2,1)S(1)}, u32[]{:S(2)}, u32[]{:S(2)}) collective-permute-start(bf16[2,256,1024]{2,1,0:T(8,128)(2,1)S(1)} %pad_maximum_fusion.refs_0_), channel_id=1, source_target_pairs={{0,2},{1,3},{2,0},{3,1},{4,6},{5,7},{6,4},{7,5},{8,10},{9,11},{10,... | collective-permute-start | bytes 3145736 | tf_op jit(solution)/shard_map/ppermute | solution.py:352
  14.1 6.4 %collective-permute-start = (bf16[256,128]{1,0:T(8,128)(2,1)}, bf16[256,128]{1,0:T(8,128)(2,1)S(1)}, u32[]{:S(2)}, u32[]{:S(2)}) collective-permute-start(bf16[256,128]{1,0:T(8,128)(2,1)} %get-tuple-element.55), channel_id=1, source_target_pairs={{0,4},{4,0},{8,12},{12,8},{16,20},{20,16},{24,28},{28,24},{1,5},{5... | collective-permute-start | bytes 196616 | tf_op jit(solution)/shard_map/ppermute | solution.py:352
  16.1 6.9 %collective-permute-start.1 = (bf16[256,128]{1,0:T(8,128)(2,1)}, bf16[256,128]{1,0:T(8,128)(2,1)S(1)}, u32[]{:S(2)}, u32[]{:S(2)}) collective-permute-start(bf16[256,128]{1,0:T(8,128)(2,1)} %get-tuple-element.56), channel_id=1, source_target_pairs={{0,8},{4,12},{8,0},{12,4},{16,24},{20,28},{24,16},{28,20},{1,9},{5... | collective-permute-start | bytes 196616 | tf_op jit(solution)/shard_map/ppermute | solution.py:352
  17.6 8.3 %collective-permute-start.2 = (bf16[256,128]{1,0:T(8,128)(2,1)}, bf16[256,128]{1,0:T(8,128)(2,1)S(1)}, u32[]{:S(2)}, u32[]{:S(2)}) collective-permute-start(bf16[256,128]{1,0:T(8,128)(2,1)} %get-tuple-element.57), channel_id=1, source_target_pairs={{0,12},{4,8},{8,4},{12,0},{16,28},{20,24},{24,20},{28,16},{1,13},{... | collective-permute-start | bytes 196616 | tf_op jit(solution)/shard_map/ppermute | solution.py:352
  17.6 20.5 %collective-permute-start.3 = (bf16[256,128]{1,0:T(8,128)(2,1)}, bf16[256,128]{1,0:T(8,128)(2,1)S(1)}, u32[]{:S(2)}, u32[]{:S(2)}) collective-permute-start(bf16[256,128]{1,0:T(8,128)(2,1)} %get-tuple-element.58), channel_id=1, source_target_pairs={{0,16},{4,20},{8,24},{12,28},{16,0},{20,4},{24,8},{28,12},{1,17},{... | collective-permute-start | bytes 196616 | tf_op jit(solution)/shard_map/ppermute | solution.py:352
  20.5 17.6 %collective-permute-start.4 = (bf16[256,128]{1,0:T(8,128)(2,1)}, bf16[256,128]{1,0:T(8,128)(2,1)S(1)}, u32[]{:S(2)}, u32[]{:S(2)}) collective-permute-start(bf16[256,128]{1,0:T(8,128)(2,1)} %get-tuple-element.59), channel_id=1, source_target_pairs={{0,20},{4,16},{8,28},{12,24},{16,4},{20,0},{24,12},{28,8},{1,21},{... | collective-permute-start | bytes 196616 | tf_op jit(solution)/shard_map/ppermute | solution.py:352
  23.1 15.1 %collective-permute-start.5 = (bf16[256,128]{1,0:T(8,128)(2,1)}, bf16[256,128]{1,0:T(8,128)(2,1)S(1)}, u32[]{:S(2)}, u32[]{:S(2)}) collective-permute-start(bf16[256,128]{1,0:T(8,128)(2,1)} %get-tuple-element.60), channel_id=1, source_target_pairs={{0,24},{4,28},{8,16},{12,20},{16,8},{20,12},{24,0},{28,4},{1,25},{... | collective-permute-start | bytes 196616 | tf_op jit(solution)/shard_map/ppermute | solution.py:352
  25.9 12.3 %collective-permute-start.6 = (bf16[256,128]{1,0:T(8,128)(2,1)}, bf16[256,128]{1,0:T(8,128)(2,1)S(1)}, u32[]{:S(2)}, u32[]{:S(2)}) collective-permute-start(bf16[256,128]{1,0:T(8,128)(2,1)} %get-tuple-element.61), channel_id=1, source_target_pairs={{0,28},{4,24},{8,20},{12,16},{16,12},{20,8},{24,4},{28,0},{1,29},{... | collective-permute-start | bytes 196616 | tf_op jit(solution)/shard_map/ppermute | solution.py:352
  39.5 19.0 %all-to-all-start.1 = ((bf16[32,32,256]{2,1,0:T(8,128)(2,1)}), bf16[32,32,256]{2,1,0:T(8,128)(2,1)S(1)}, u32[]{:S(2)}, u32[]{:S(2)}) async-start(bf16[32,32,256]{2,1,0:T(8,128)(2,1)} %get-tuple-element.66), calls=%async_computation.1 | async-start | bytes 1048576 | tf_op jit(solution)/shard_map/all_to_all | solution.py:534
  42.1 19.0 %collective-permute-start.8 = (bf16[2,256,1024]{2,1,0:T(8,128)(2,1)S(1)}, bf16[2,256,1024]{2,1,0:T(8,128)(2,1)}, u32[]{:S(2)}, u32[]{:S(2)}) collective-permute-start(bf16[2,256,1024]{2,1,0:T(8,128)(2,1)S(1)} %pad_maximum_fusion.refs_0_), channel_id=1, source_target_pairs={{0,1},{1,0},{2,3},{3,2},{4,5},{5,4},{6,7},{7,6},{8,9},{9,8},{10,11... | collective-permute-start | bytes 3145736 | tf_op jit(solution)/shard_map/ppermute | solution.py:352
  42.3 18.8 %collective-permute-start.9 = (bf16[2,256,1024]{2,1,0:T(8,128)(2,1)S(1)}, bf16[2,256,1024]{2,1,0:T(8,128)(2,1)}, u32[]{:S(2)}, u32[]{:S(2)}) collective-permute-start(bf16[2,256,1024]{2,1,0:T(8,128)(2,1)S(1)} %collective-permute-done.7.refs_1_), channel_id=1, source_target_pairs={{0,1},{1,0},{2,3},{3,2},{4,5},{5,4},{6,7},{7,6},{8,9},{9,8},{10,11... | collective-permute-start | bytes 3145736 | tf_op jit(solution)/shard_map/ppermute | solution.py:352
  58.5 19.0 %all-to-all-start.2 = ((bf16[32,32,256]{2,1,0:T(8,128)(2,1)}), bf16[32,32,256]{2,1,0:T(8,128)(2,1)S(1)}, u32[]{:S(2)}, u32[]{:S(2)}) async-start(bf16[32,32,256]{2,1,0:T(8,128)(2,1)} %shard_map.115), calls=%async_computation.2 | async-start | bytes 1048576 | tf_op jit(solution)/shard_map/all_to_all | solution.py:534
  77.4 20.1 %all-to-all-start.3 = ((bf16[32,32,256]{2,1,0:T(8,128)(2,1)}), bf16[32,32,256]{2,1,0:T(8,128)(2,1)}, u32[]{:S(2)}, u32[]{:S(2)}) async-start(bf16[32,32,256]{2,1,0:T(8,128)(2,1)} %bitcast.51), calls=%async_computation.3 | async-start | bytes 1048576 | tf_op jit(solution)/shard_map/all_to_all | solution.py:534
  89.8 13.9 %collective-permute-start.14 = (bf16[4,128,256]{2,1,0:T(8,128)(2,1)}, bf16[4,128,256]{2,1,0:T(8,128)(2,1)S(1)}, u32[]{:S(2)}, u32[]{:S(2)}) collective-permute-start(bf16[4,128,256]{2,1,0:T(8,128)(2,1)} %get-tuple-element.79), channel_id=1, source_target_pairs={{0,4},{1,5},{2,6},{3,7},{4,0},{5,1},{6,2},{7,3},{8,12},{9,13},{10,... | collective-permute-start | bytes 786440 | tf_op jit(solution)/shard_map/ppermute | solution.py:473
  91.2 16.4 %collective-permute-start.15 = (bf16[4,128,256]{2,1,0:T(8,128)(2,1)}, bf16[4,128,256]{2,1,0:T(8,128)(2,1)S(1)}, u32[]{:S(2)}, u32[]{:S(2)}) collective-permute-start(bf16[4,128,256]{2,1,0:T(8,128)(2,1)} %get-tuple-element.80), channel_id=1, source_target_pairs={{0,2},{1,3},{2,0},{3,1},{4,6},{5,7},{6,4},{7,5},{8,10},{9,11},{10,... | collective-permute-start | bytes 786440 | tf_op jit(solution)/shard_map/ppermute | solution.py:473
  92.7 14.9 %collective-permute-start.16 = (bf16[4,128,256]{2,1,0:T(8,128)(2,1)}, bf16[4,128,256]{2,1,0:T(8,128)(2,1)S(1)}, u32[]{:S(2)}, u32[]{:S(2)}) collective-permute-start(bf16[4,128,256]{2,1,0:T(8,128)(2,1)} %get-tuple-element.81), channel_id=1, source_target_pairs={{0,6},{1,7},{2,4},{3,5},{4,2},{5,3},{6,0},{7,1},{8,14},{9,15},{10,... | collective-permute-start | bytes 786440 | tf_op jit(solution)/shard_map/ppermute | solution.py:473
  94.6 18.6 %collective-permute-start.23 = (bf16[4,128,256]{2,1,0:T(8,128)(2,1)}, bf16[4,128,256]{2,1,0:T(8,128)(2,1)S(1)}, u32[]{:S(2)}, u32[]{:S(2)}) collective-permute-start(bf16[4,128,256]{2,1,0:T(8,128)(2,1)} %get-tuple-element.94), channel_id=1, source_target_pairs={{0,4},{1,5},{2,6},{3,7},{4,0},{5,1},{6,2},{7,3},{8,12},{9,13},{10,... | collective-permute-start | bytes 786440 | tf_op jit(solution)/shard_map/ppermute | solution.py:473
  96.0 17.2 %collective-permute-start.24 = (bf16[4,128,256]{2,1,0:T(8,128)(2,1)}, bf16[4,128,256]{2,1,0:T(8,128)(2,1)S(1)}, u32[]{:S(2)}, u32[]{:S(2)}) collective-permute-start(bf16[4,128,256]{2,1,0:T(8,128)(2,1)} %get-tuple-element.95), channel_id=1, source_target_pairs={{0,2},{1,3},{2,0},{3,1},{4,6},{5,7},{6,4},{7,5},{8,10},{9,11},{10,... | collective-permute-start | bytes 786440 | tf_op jit(solution)/shard_map/ppermute | solution.py:473
  103.7 15.0 %collective-permute-start.25 = (bf16[4,128,256]{2,1,0:T(8,128)(2,1)}, bf16[4,128,256]{2,1,0:T(8,128)(2,1)S(1)}, u32[]{:S(2)}, u32[]{:S(2)}) collective-permute-start(bf16[4,128,256]{2,1,0:T(8,128)(2,1)} %get-tuple-element.96), channel_id=1, source_target_pairs={{0,6},{1,7},{2,4},{3,5},{4,2},{5,3},{6,0},{7,1},{8,14},{9,15},{10,... | collective-permute-start | bytes 786440 | tf_op jit(solution)/shard_map/ppermute | solution.py:473
  108.4 13.3 %collective-permute-start.17 = (bf16[2,128,256]{2,1,0:T(8,128)(2,1)}, bf16[2,128,256]{2,1,0:T(8,128)(2,1)S(1)}, u32[]{:S(2)}, u32[]{:S(2)}) collective-permute-start(bf16[2,128,256]{2,1,0:T(8,128)(2,1)} %get-tuple-element.87), channel_id=1, source_target_pairs={{0,8},{4,12},{8,0},{12,4},{16,24},{20,28},{24,16},{28,20},{1,9},{5... | collective-permute-start | bytes 393224 | tf_op jit(solution)/shard_map/ppermute | solution.py:352
  109.1 23.3 %all-to-all-start.4 = ((bf16[8,32,1024]{2,1,0:T(8,128)(2,1)}), bf16[8,32,1024]{2,1,0:T(8,128)(2,1)S(1)}, u32[]{:S(2)}, u32[]{:S(2)}) async-start(bf16[8,32,1024]{2,1,0:T(8,128)(2,1)} %shard_map.117), calls=%async_computation.4 | async-start | bytes 1048576 | tf_op jit(solution)/shard_map/all_to_all | solution.py:534
  119.4 6.3 %collective-permute-start.26 = (bf16[2,128,256]{2,1,0:T(8,128)(2,1)}, bf16[2,128,256]{2,1,0:T(8,128)(2,1)S(1)}, u32[]{:S(2)}, u32[]{:S(2)}) collective-permute-start(bf16[2,128,256]{2,1,0:T(8,128)(2,1)} %get-tuple-element.102), channel_id=1, source_target_pairs={{0,8},{4,12},{8,0},{12,4},{16,24},{20,28},{24,16},{28,20},{1,9},{5... | collective-permute-start | bytes 393224 | tf_op jit(solution)/shard_map/ppermute | solution.py:352
  121.7 8.8 %collective-permute-start.18 = (bf16[1,128,256]{2,1,0:T(8,128)(2,1)S(1)}, bf16[1,128,256]{2,1,0:T(8,128)(2,1)S(1)}, u32[]{:S(2)}, u32[]{:S(2)}) collective-permute-start(bf16[1,128,256]{2,1,0:T(8,128)(2,1)S(1)} %fusion.4), channel_id=1, source_target_pairs={{0,16},{4,20},{8,24},{12,28},{16,0},{20,4},{24,8},{28,12},{1,17},{... | collective-permute-start | bytes 196616 | tf_op jit(solution)/shard_map/ppermute | solution.py:352
  (26 other events, 131.0 us)
